TPU v7x, 32 devices: a whole 2x2x4 slice. The times are simulated.
32 devices in a mesh: row: 4 (over y, core), col: 8 (over z, x).
Axes of the slice: x: 2, y: 2, z: 4, core: 2. Of those that a mesh axis runs over, the one named last changes fastest.
Arguments:
- pan_left: bfloat16 [16, 2048, 512], P('row', 'col'), may hold values from -6 to 6
- pan_right: bfloat16 [16, 2048, 512], P('row', 'col'), may hold values from -0.125 to 0.125
- inverse: bfloat16 [2048, 2048], P('col'), may hold values from -0.25 to 1.25, as said below
- rank_list: int32 [16], replicated, may hold values from 32 to 512, as said below
Outputs:
- update_right: bfloat16 [16, 16, 2048, 512], P('row', 'col')
- update_gram: bfloat16 [16, 16, 512, 512], P('row', 'col')
Inputs may be any that keep to these rules, and one draw needn't show every extreme that they name: `inverse`: lower triangular; diagonal entries lie from 0.75 to 1.25. `rank_list`: columns of a tile's factors at or beyond its rank do not count.
All inputs are finite; a program needn't handle non-finite values.
Results may differ from a plain program's by a relative error of at most 0.0065.
Values may be sent and summed in bfloat16 or wider, within the bound.
No kernel may reach another device: no remote copies, remote signals or barrier semaphores. Data moves between devices by JAX's collectives and lax.ppermute only.
A program may use at most 128 MiB of HBM per device.

v0:
```python
import jax
import jax.numpy as jnp
from jax import lax
from jax.sharding import PartitionSpec as P


def from_root(array, axis, root):
    mine = lax.axis_index(axis) == root
    return lax.psum(jnp.where(mine, array, jnp.zeros_like(array)), axis)


def local(pan_left, pan_right, inverse, rank_list):
    tile_count = pan_right.shape[0]
    rank_width = pan_right.shape[2]
    row_count = inverse.shape[1]
    tile_total = tile_count * lax.axis_size("row")
    per_column = tile_total // lax.axis_size("col")
    my_row = lax.axis_index("row")
    my_col = lax.axis_index("col")
    full_right = lax.all_gather(pan_right, "col", axis=1, tiled=True)
    solved_slab = jnp.einsum(
        "rn,tnk->trk", inverse, full_right, preferred_element_type=jnp.float32
    ).astype(jnp.bfloat16)
    full_solved, full_left = (
        lax.all_gather(solved_slab, "col", axis=1, tiled=True),
        lax.all_gather(pan_left, "col", axis=1, tiled=True),
    )
    first_tile = my_col * per_column
    root_row = first_tile // tile_count
    local_start = first_tile % tile_count
    pick_solved = lax.dynamic_slice_in_dim(full_solved, local_start, per_column, 0)
    pick_left = lax.dynamic_slice_in_dim(full_left, local_start, per_column, 0)
    col_solved, col_left = (
        from_root(pick_solved, "row", root_row),
        from_root(pick_left, "row", root_row),
    )
    positions = jnp.arange(rank_width, dtype=jnp.int32)
    mine_ranks = lax.dynamic_slice_in_dim(rank_list, my_row * tile_count, tile_count, 0)
    their_ranks = lax.dynamic_slice_in_dim(rank_list, first_tile, per_column, 0)
    mine_live = (positions[None, :] < mine_ranks[:, None]).astype(jnp.float32)
    their_live = (positions[None, :] < their_ranks[:, None]).astype(jnp.float32)
    core = jnp.einsum("tnk,unl->tukl", full_solved, col_solved, preferred_element_type=jnp.float32)
    core = (core * mine_live[:, None, :, None] * their_live[None, :, None, :]).astype(jnp.bfloat16)
    update = jnp.einsum(
        "unl,tukl->tunk", col_left, core, preferred_element_type=jnp.float32
    ).astype(jnp.bfloat16)
    gram = (
        jnp.einsum("tunk,tunl->tukl", update, update, preferred_element_type=jnp.float32)
        / row_count
    ).astype(jnp.bfloat16)
    return (update, gram)


def solution(mesh):
    in_specs = (P("row", "col", None), P("row", "col", None), P("col", None), P())
    out_specs = (P("row", "col", None, None), P("row", "col", None, None))
    return jax.shard_map(local, mesh=mesh, in_specs=in_specs, out_specs=out_specs, check_vma=False)
```

profile of v0, /device:TPU:0, one launch (start us, length us, event | category | flops | bytes accessed | tf_op | source)
XLA Modules:
  0.0 619.2 jit_solution(16899952813526477768)
XLA Ops:
  7.2 0.0 copy-start
  7.2 0.0 all-gather.4.cloned.1.call-start
  7.2 2.3 copy.6
  9.6 0.0 all-gather.4.cloned.1.call-update
  9.6 0.0 all-gather.8.cloned.1.call-start
  9.6 2.3 copy.7
  12.0 0.0 all-gather.8.cloned.1.call-update
  12.0 0.0 all-gather.6.cloned.1.call-start
  12.0 126.7 %all-gather.4.cloned.1.call-done = bf16[4,2048,512]{1,2,0:T(8,128)(2,1)} async-done(((bf16[4,256,512]{1,2,0:T(8,128)(2,1)}), bf16[4,2048,512]{1,2,0:T(8,128)(2,1)}) %all-gather.4.cloned.1.call-update) | async-done | bytes 8388624 | tf_op jit(solution)/shard_map/all_gather | solution.py:20
  138.8 0.0 copy-done
  138.8 6.7 %fusion.13 = bf16[4,256,512]{1,2,0:T(8,128)(2,1)} fusion(bf16[4,2048,512]{1,2,0:T(8,128)(2,1)} %all-gather.4.cloned.1.call-done, bf16[256,2048]{1,0:T(8,128)(2,1)S(1)} %copy-done), kind=kOutput, calls=%fused_computation.13 | convolution fusion | flops 2148007936 | bytes 10485760 | tf_op jit(solution)/shard_map/rn,tnk->trk/dot_general | solution.py:21
  145.5 0.0 all-gather.6.cloned.1.call-update
  145.5 0.0 all-reduce.3.cloned.1.call-start
  145.6 118.8 %all-gather.8.cloned.1.call-done = bf16[4,2048,512]{1,2,0:T(8,128)(2,1)} async-done(((bf16[4,256,512]{1,2,0:T(8,128)(2,1)}), bf16[4,2048,512]{1,2,0:T(8,128)(2,1)}) %all-gather.8.cloned.1.call-update) | async-done | bytes 8388624 | tf_op jit(solution)/shard_map/all_gather | solution.py:26
  264.4 4.5 dynamic-slice_select_fusion
  268.9 0.0 copy-start.2
  268.9 121.8 %all-gather.6.cloned.1.call-done = bf16[4,2048,512]{1,2,0:T(8,128)(2,1)} async-done(((bf16[4,256,512]{1,2,0:T(8,128)(2,1)}), bf16[4,2048,512]{1,2,0:T(8,128)(2,1)}) %all-gather.6.cloned.1.call-update) | async-done | bytes 8388624 | tf_op jit(solution)/shard_map/all_gather | solution.py:25
  390.6 4.5 dynamic-slice_select_fusion.1
  395.1 0.0 all-reduce.3.cloned.1.call-update
  395.1 0.0 copy-done.2
  395.2 0.1 dynamic_slice.14
  395.2 0.1 dynamic_slice.13
  395.3 0.1 compare_convert_fusion
  395.4 0.1 fusion.15
  395.4 151.3 %all-reduce.3.cloned.1.call-done = (bf16[2,2048,512]{1,2,0:T(8,128)(2,1)}, bf16[2,2048,512]{1,2,0:T(8,128)(2,1)}) async-done(((bf16[2,2048,512]{1,2,0:T(8,128)(2,1)}, bf16[2,2048,512]{1,2,0:T(8,128)(2,1)}), (bf16[2,2048,512]{1,2,0:T(8,128)(2,1)}, bf16[2,2048,512]{1,2,0:T(8,128)(2,1)})) %all-reduce.3.cloned.1.call-update) | async-done | bytes 8388624 | tf_op jit(solution)/shard_map/psum | solution.py:9
  546.7 25.6 %convert_bitcast_fusion = bf16[4,2,2048,512]{2,3,0,1:T(8,128)(2,1)} fusion(bf16[4,2048,512]{1,2,0:T(8,128)(2,1)} %all-gather.6.cloned.1.call-done, bf16[2,2048,512]{1,2,0:T(8,128)(2,1)} %get-tuple-element.4, bf16[2,2048,512]{1,2,0:T(8,128)(2,1)} %get-tuple-element.5, f32[2,512]{1,0:T(2,128)S(1)} %compare_convert_fusion, f32[4,512]{1,0:T(4,128)S(1)} %fusion.15), kind=kOutput, calls=%fused_computation | convolution fusion | flops 17194549248 | bytes 33566720 | tf_op jit(solution)/shard_map/unl,tukl->tunk/dot_general | solution.py:44
  572.4 21.6 %copy.11 = bf16[4,2,2048,512]{3,2,1,0:T(8,128)(2,1)} copy(bf16[4,2,2048,512]{2,3,0,1:T(8,128)(2,1)} %convert_bitcast_fusion) | data formatting | bytes 33554432 | tf_op jit(solution)/shard_map/convert_element_type | solution.py:46
  593.9 0.0 copy-start.1
  593.9 18.7 %multiply_convert_fusion = bf16[4,2,512,512]{3,2,1,0:T(8,128)(2,1)} fusion(bf16[4,2,2048,512]{3,2,1,0:T(8,128)(2,1)} %copy.11), kind=kOutput, calls=%fused_computation.3 | convolution fusion | flops 8594128896 | bytes 20971520 | tf_op jit(solution)/shard_map/tunk,tunl->tukl/dot_general | solution.py:48
  612.6 0.0 copy-done.1
Async XLA Ops:
  7.2 131.6 %copy-start = (bf16[256,2048]{1,0:T(8,128)(2,1)S(1)}, bf16[256,2048]{1,0:T(8,128)(2,1)}, u32[]{:S(2)}) copy-start(bf16[256,2048]{1,0:T(8,128)(2,1)} %param.6) | copy-start | bytes 3145732
  7.2 131.6 %all-gather.4.cloned.1.call-start = ((), (), s32[]{:S(2)}) async-start(), calls=%async_computation | async-start | bytes 9437184 | tf_op jit(solution)/shard_map/all_gather | solution.py:20
  9.6 254.8 %all-gather.8.cloned.1.call-start = ((), (), s32[]{:S(2)}) async-start(), calls=%async_computation.2 | async-start | bytes 9437184 | tf_op jit(solution)/shard_map/all_gather | solution.py:26
  12.0 378.7 %all-gather.6.cloned.1.call-start = ((), (), s32[]{:S(2)}) async-start(), calls=%async_computation.1 | async-start | bytes 9437184 | tf_op jit(solution)/shard_map/all_gather | solution.py:25
  145.5 401.2 %all-reduce.3.cloned.1.call-start = ((), (), s32[]{:S(2)}) async-start(), calls=%async_computation.3 | async-start | bytes 16777216 | tf_op jit(solution)/shard_map/psum | solution.py:9
  268.9 126.3 %copy-start.2 = (s32[16]{0:T(128)S(1)}, s32[16]{0:T(128)}, u32[]{:S(2)}) copy-start(s32[16]{0:T(128)} %param.7) | copy-start | bytes 196
  593.9 18.7 %copy-start.1 = (bf16[256,2048]{1,0:T(8,128)(2,1)S(1)}, bf16[256,2048]{1,0:T(8,128)(2,1)}, u32[]{:S(2)}) copy-start(bf16[256,2048]{1,0:T(8,128)(2,1)} %param.6) | copy-start | bytes 3145732
Sparse Core Ops, SparseCore 0:
  10.6 128.0 all-gather.3
  140.8 123.5 all-gather.7
  267.0 123.5 all-gather.5
  395.3 151.4 all-reduce.2
where the time goes:
time: 620 us; the launch traced here: 619 us
  waiting for transfers between devices  519 us (84%)
  matrix products  51.1 us (8%)
  local copies, waits for them, and re-layouts  26.4 us (4%)
  between operations  13.8 us (2%)
  other arithmetic  9.09 us (1%)
    psum x1, waiting for transfers between devices, from_root(): return lax.psum(jnp.where(mine, array, jnp.zeros_like(array)), axis)  151 us
    all_gather x1, waiting for transfers between devices, local(): full_right = lax.all_gather(pan_right, 'col', axis=1, tiled=True)  127 us
    all_gather x1, waiting for transfers between devices, local(): lax.all_gather(solved_slab, 'col', axis=1, tiled=True)  122 us
    all_gather x1, waiting for transfers between devices, local(): lax.all_gather(pan_left, 'col', axis=1, tiled=True)  119 us
    dot_general x1, matrix products, local(): jnp.einsum('unl,tukl->tunk', col_left, core, preferred_element_type=jnp.f...  25.6 us
    convert_element_type x1, local copies, waits for them, and re-layouts, local(): update = jnp.einsum('unl,tukl->tunk', col_left, core, preferred_element_t...  21.6 us
    dot_general x1, matrix products, local(): jnp.einsum('tunk,tunl->tukl', update, update, preferred_element_type=jnp....  18.7 us
  transfers between devices with their start and end apart: 4, of which 4 were waited for; matrix products, arithmetic and copies ran while one was open for 2% of the time, Pallas kernels for 0%

commit v1 on v0

v1 whole, which is shorter than its diff:
```python
import functools

import jax
import jax.numpy as jnp
from jax import lax
from jax.experimental import pallas as pl
from jax.experimental.pallas import tpu as pltpu
from jax.sharding import PartitionSpec as P

NT = (((1,), (1,)), ((), ()))
NN = (((1,), (0,)), ((), ()))
BLOCK = 256
MIB = 1 << 20


def dot(a, b, dims):
    return lax.dot_general(a, b, dims, preferred_element_type=jnp.float32)


def ring_of(count):
    return list(range(0, count, 2)) + list(range(count - 1, 0, -2))


def ring_place(col, count):
    return jnp.where(col % 2 == 0, col // 2, count // 2 + (count - 1 - col) // 2)


def ring_col(place, count):
    place = place % count
    return jnp.where(place < count // 2, 2 * place, count - 1 - 2 * (place - count // 2))


def gather_row(piece, rows):
    held = [piece]
    for step in range(1, rows // 2):
        held.append(lax.ppermute(piece, "row", [(i, (i + 2 * step) % rows) for i in range(rows)]))
    swapped = [lax.ppermute(h, "row", [(i, i ^ 1) for i in range(rows)]) for h in held]
    return held + swapped


def row_ids(my_row, rows):
    other = jnp.bitwise_xor(my_row, 1)
    half = rows // 2
    return [(my_row - 2 * k) % rows for k in range(half)] + [(other - 2 * k) % rows for k in range(half)]


def solve_kernel(cols, rows, meta, *refs):
    it = iter(refs)
    cw = [next(it) for _ in range(cols)]
    ccw = [next(it) for _ in range(cols)]
    sent = [[next(it) for _ in range(cols)] for _ in range(3)]
    inv = [next(it) for _ in range(rows)]
    out, right, whole, solved, rsem, isem = it
    kind, core = meta[0], meta[1]
    width = right.shape[1] // cols
    pulls = []
    for s in range(cols):
        spot = pl.multiple_of(meta[2 + s] * width, width)
        target = right.at[:, pl.ds(spot, width)]
        for case in range(5):
            ref = (cw[s].at[core], ccw[s].at[core], sent[0][s], sent[1][s], sent[2][s])[case]

            @pl.when(kind == case)
            def _(ref=ref, target=target, s=s):
                pltpu.make_async_copy(ref, target, rsem.at[s]).start()

        pulls.append(pltpu.make_async_copy(sent[0][s], target, rsem.at[s]))
    for k in range(rows):
        copy = pltpu.make_async_copy(inv[k], whole.at[:, meta[2 + cols + k]], isem.at[k])
        copy.start()
        pulls.append(copy)
    for copy in pulls:
        copy.wait()
    size = right.shape[1]
    flat = whole.reshape(size, size)
    for b in range(size // BLOCK):
        end = (b + 1) * BLOCK
        solved[:, b * BLOCK : end] = dot(right[:, :end], flat[b * BLOCK : end, :end], NT).astype(jnp.bfloat16)
    for b in range(size // BLOCK):
        start = b * BLOCK
        out[:, start : start + BLOCK] = dot(
            solved[:, start:], flat[start:, start : start + BLOCK], NN
        ).astype(jnp.bfloat16)


def main_kernel(cols, rows, tiles, per, meta, *refs):
    it = iter(refs)
    cw = [next(it) for _ in range(cols)]
    ccw = [next(it) for _ in range(cols)]
    mine, other = next(it), next(it)
    left = [next(it) for _ in range(rows)]
    high, low = next(it), next(it)
    update, gram = next(it), next(it)
    right, turned, whole, upd, grm, sem, osem = it
    half = tiles // 2
    size, width = right.shape[2], right.shape[2] // cols
    core = meta[1]
    pulls = []

    def pull(src, dst):
        copy = pltpu.make_async_copy(src, dst, sem.at[len(pulls)])
        copy.start()
        pulls.append(copy)

    pull(mine, turned.at[core])
    pull(other, turned.at[1 - core])
    for s in range(cols):
        for part, msgs, base in ((0, cw, 2), (1, ccw, 2 + cols)):
            spot = pl.multiple_of(meta[base + s] * width, width)
            pull(msgs[s], right.at[pl.ds(part * half, half), :, pl.ds(spot, width)])
    for k in range(rows):
        pull(left[k], whole.at[:, :, meta[2 + 2 * cols + k]])
    for copy in pulls:
        copy.wait()
    base = 2 + 2 * cols + rows
    rank = right.shape[1]
    flat = whole.reshape(per, size, rank)
    chunk = min(512, size)
    row_at = lax.broadcasted_iota(jnp.int32, (rank, rank), 0)
    col_at = lax.broadcasted_iota(jnp.int32, (rank, rank), 1)

    def outs(i, j, slot):
        return (
            pltpu.make_async_copy(upd.at[slot], update.at[i, j], osem.at[0, slot]),
            pltpu.make_async_copy(grm.at[slot], gram.at[i, j], osem.at[1, slot]),
        )

    def pair(at, carry):
        i, j, slot = at // per, at % per, at % 2
        value = dot(right[i], turned[j], NT)
        live = (row_at < meta[base + i]) & (col_at < meta[base + tiles + j])
        value = jnp.where(live, value, 0.0).astype(jnp.bfloat16)

        @pl.when(at >= 2)
        def _():
            for copy in outs(i, j, slot):
                copy.wait()

        def rows_of(n, carry):
            spot = pl.multiple_of(n * chunk, chunk)
            upd[slot, pl.ds(spot, chunk), :] = dot(flat[j, pl.ds(spot, chunk), :], value, NT).astype(jnp.bfloat16)
            return carry

        lax.fori_loop(0, size // chunk, rows_of, 0)
        part = (dot(value, high[j], NN) + dot(value, low[j], NN)).astype(jnp.bfloat16)
        grm[slot] = (dot(part, value, NT) / size).astype(jnp.bfloat16)
        for copy in outs(i, j, slot):
            copy.start()
        return carry

    total = tiles * per
    lax.fori_loop(0, total, pair, 0)
    for at in range(max(0, total - 2), total):
        for copy in outs(at // per, at % per, at % 2):
            copy.wait()


def local(pan_left, pan_right, inverse, rank_list):
    tiles, slab, rank = pan_right.shape
    size = inverse.shape[1]
    rows, cols = lax.axis_size("row"), lax.axis_size("col")
    per = tiles * rows // cols
    my_row, my_col = lax.axis_index("row"), lax.axis_index("col")
    piece = slab // rows
    half = tiles // 2
    cut = pan_left.reshape(tiles, rows, piece, rank)
    cut = lax.all_to_all(cut, "row", 1, 0, tiled=False).reshape(cols, per, piece, rank)
    cut = lax.all_to_all(cut, "col", 0, 0, tiled=True)
    cut = jnp.swapaxes(cut, 0, 1)
    left = gather_row(cut, rows)
    quarter = lax.dynamic_slice_in_dim(inverse, my_row * piece, piece, 0)
    quarter = lax.all_gather(quarter, "col", axis=0, tiled=False)
    inv = gather_row(quarter, rows)
    turned = jnp.swapaxes(pan_right, 1, 2)
    ring = ring_of(cols)
    ahead = [(ring[i], ring[(i + 1) % cols]) for i in range(cols)]
    back = [(b, a) for a, b in ahead]
    cw, ccw = [turned[:half]], [turned[half:]]
    for _ in range(cols - 1):
        cw.append(lax.ppermute(cw[-1], "col", ahead))
        ccw.append(lax.ppermute(ccw[-1], "col", back))
    first_half = (my_col * per) % tiles == 0
    root = (my_col * per) // tiles
    sources = [(c * per) // tiles for c in range(cols)]
    to_partner = [(src * cols + c, (src ^ 1) * cols + c) for c, src in enumerate(sources)]

    def to_core(array, core):
        moved = None
        for step in range(1, rows // 2):
            pairs = [(src * cols + c, ((src - src % 2 + 2 * step) % rows + core) * cols + c) for c, src in enumerate(sources)]
            got = lax.ppermute(array, ("row", "col"), pairs)
            moved = got if moved is None else moved + got
        return moved

    sent = [[], [], []]
    for s in range(cols):
        give = jnp.where(first_half, cw[s], ccw[s])
        keep = lax.dynamic_index_in_dim(give, 1 - root % 2, 0, keepdims=False)
        sent[0].append(lax.ppermute(keep, ("row", "col"), to_partner))
        for core in range(2):
            sent[1 + core].append(to_core(give[core], core))
    place = ring_place(my_col, cols)
    cw_from = [ring_col(place - s + cols, cols) for s in range(cols)]
    ccw_from = [ring_col(place + s, cols) for s in range(cols)]
    ids = row_ids(my_row, rows)
    core = my_row % 2
    kind = jnp.where(
        my_row == root,
        jnp.where(first_half, 0, 1),
        jnp.where(my_row // 2 == root // 2, 2, 3 + core),
    )
    came = [jnp.where(first_half, a, b) for a, b in zip(cw_from, ccw_from)]
    meta = jnp.stack([kind, core] + came + ids).astype(jnp.int32)
    anywhere = pl.BlockSpec(memory_space=pl.ANY)
    vmem = pl.BlockSpec(memory_space=pltpu.VMEM)
    smem = pl.BlockSpec(memory_space=pltpu.SMEM)
    operands = cw + ccw + sent[0] + sent[1] + sent[2] + inv
    mine = pl.pallas_call(
        functools.partial(solve_kernel, cols, rows),
        out_shape=jax.ShapeDtypeStruct((rank, size), jnp.bfloat16),
        in_specs=[smem] + [anywhere] * len(operands),
        out_specs=vmem,
        scratch_shapes=[
            pltpu.VMEM((rank, size), jnp.bfloat16),
            pltpu.VMEM((cols, rows, piece, size), jnp.bfloat16),
            pltpu.VMEM((rank, size), jnp.bfloat16),
            pltpu.SemaphoreType.DMA((cols,)),
            pltpu.SemaphoreType.DMA((rows,)),
        ],
        compiler_params=pltpu.CompilerParams(vmem_limit_bytes=32 * MIB),
        cost_estimate=pl.CostEstimate(flops=2 * rank * size * size, bytes_accessed=2 * size * (size + 2 * rank), transcendentals=0),
        name="solve",
    )(meta, *operands)
    other = lax.ppermute(mine, "row", [(i, i ^ 1) for i in range(rows)])
    exact = sum(jnp.einsum("jcnk,jcnl->jkl", p, p, preferred_element_type=jnp.float32) for p in left)
    high = exact.astype(jnp.bfloat16)
    low = (exact - high.astype(jnp.float32)).astype(jnp.bfloat16)
    my_ranks = lax.dynamic_slice_in_dim(rank_list, my_row * tiles, tiles, 0)
    their_ranks = lax.dynamic_slice_in_dim(rank_list, my_col * per, per, 0)
    meta = jnp.concatenate([jnp.stack([kind, core] + cw_from + ccw_from + ids).astype(jnp.int32), my_ranks, their_ranks])
    operands = cw + ccw + [mine, other] + left
    pulls = 2 * cols + 2 + rows
    update, gram = pl.pallas_call(
        functools.partial(main_kernel, cols, rows, tiles, per),
        out_shape=(
            jax.ShapeDtypeStruct((tiles, per, size, rank), jnp.bfloat16),
            jax.ShapeDtypeStruct((tiles, per, rank, rank), jnp.bfloat16),
        ),
        in_specs=[smem] + [anywhere] * len(operands) + [vmem, vmem],
        out_specs=(anywhere, anywhere),
        scratch_shapes=[
            pltpu.VMEM((tiles, rank, size), jnp.bfloat16),
            pltpu.VMEM((per, rank, size), jnp.bfloat16),
            pltpu.VMEM((per, cols, rows, piece, rank), jnp.bfloat16),
            pltpu.VMEM((2, size, rank), jnp.bfloat16),
            pltpu.VMEM((2, rank, rank), jnp.bfloat16),
            pltpu.SemaphoreType.DMA((pulls,)),
            pltpu.SemaphoreType.DMA((2, 2)),
        ],
        compiler_params=pltpu.CompilerParams(vmem_limit_bytes=44 * MIB),
        cost_estimate=pl.CostEstimate(
            flops=tiles * per * (4 * rank * rank * size + 6 * rank**3),
            bytes_accessed=2 * tiles * per * size * rank + 2 * size * rank * (tiles + 2 * per),
            transcendentals=0,
        ),
        name="main",
    )(meta, *operands, high, low)
    return update, gram


def solution(mesh):
    in_specs = (P("row", "col", None), P("row", "col", None), P("col", None), P())
    out_specs = (P("row", "col", None, None), P("row", "col", None, None))
    return jax.shard_map(local, mesh=mesh, in_specs=in_specs, out_specs=out_specs, check_vma=False)
```

time: 620 us -> 323 us (0.52)
  the two profiles are of different devices: /device:TPU:0 before, /device:TPU:19 now
where the time goes in v1:
time: 323 us; the launch traced here: 321 us
  waiting for transfers between devices  122 us (38%)
  starting transfers between devices  73.8 us (23%)
  Pallas kernels  51.9 us (16%)
  local copies, waits for them, and re-layouts  42.2 us (13%)
  between operations  14.7 us (5%)
  matrix products  10.8 us (3%)
  other arithmetic  5.24 us (2%)
    ppermute x16, waiting for transfers between devices, to_core(): got = lax.ppermute(array, ('row', 'col'), pairs)  62.1 us
    pallas_call x1, Pallas kernels, local(): pl.pallas_call(functools.partial(main_kernel, cols, rows, tiles, per), ou...  40.8 us
    ppermute x7, waiting for transfers between devices, local(): ccw.append(lax.ppermute(ccw[-1], 'col', back))  39.8 us
    unnamed x101, local copies, waits for them, and re-layouts  31.1 us
    ppermute x7, starting transfers between devices, local(): cw.append(lax.ppermute(cw[-1], 'col', ahead))  24.8 us
    all_gather x1, waiting for transfers between devices, local(): quarter = lax.all_gather(quarter, 'col', axis=0, tiled=False)  20.2 us
    ppermute x16, starting transfers between devices, to_core(): got = lax.ppermute(array, ('row', 'col'), pairs)  17.7 us
    pallas_call x1, Pallas kernels, local(): pl.pallas_call(functools.partial(solve_kernel, cols, rows), out_shape=jax...  11.1 us
  transfers between devices with their start and end apart: 48, of which 12 were waited for; matrix products, arithmetic and copies ran while one was open for 9% of the time, Pallas kernels for 3%

profile of v1, /device:TPU:19, one launch (start us, length us, event | category | flops | bytes accessed | tf_op | source)
XLA Modules:
  0.0 321.1 jit_solution(5487380001821539724)
XLA Ops:
  7.2 1.2 copy-done
  9.2 1.5 copy.12
  11.6 1.3 collective-permute-start.7
  13.0 15.2 %collective-permute-done.7.refs_9_ = bf16[2,512,256]{2,1,0:T(8,128)(2,1)S(1)} collective-permute-done((bf16[2,512,256]{2,1,0:T(8,128)(2,1)S(1)}, bf16[2,512,256]{2,1,0:T(8,128)(2,1)S(1)}, u32[]{:S(2)}, u32[]{:S(2)}) %collective-permute-start.7) | collective-permute-done | bytes 524320 | tf_op jit(solution)/shard_map/ppermute | solution.py:181
  28.2 2.5 collective-permute-start.8
  30.7 2.0 slice_bitcast_fusion.7
  32.7 1.3 collective-permute-start.30
  34.0 1.4 collective-permute-start.22
  35.4 1.4 collective-permute-start.14
  37.6 5.3 %collective-permute-done.30.refs_32_ = bf16[512,256]{1,0:T(8,128)(2,1)S(1)} collective-permute-done((bf16[512,256]{1,0:T(8,128)(2,1)S(1)}, bf16[512,256]{1,0:T(8,128)(2,1)S(1)}, u32[]{:S(2)}, u32[]{:S(2)}) %collective-permute-start.30) | collective-permute-done | bytes 262176 | tf_op jit(solution)/shard_map/ppermute | solution.py:191
  42.9 20.2 %all-gather.3.cloned.1.call-done = bf16[512,2048]{1,0:T(8,128)(2,1)} async-done(((bf16[64,2048]{1,0:T(8,128)(2,1)}), bf16[512,2048]{1,0:T(8,128)(2,1)}) %all-gather.3.cloned.1.call-update) | async-done | bytes 2097168 | tf_op jit(solution)/shard_map/all_gather | solution.py:172
  63.1 1.2 collective-permute-start.38
  64.3 1.9 slice_bitcast_fusion.6
  66.2 1.3 collective-permute-start.31
  68.6 2.8 collective-permute-start.2
  72.3 41.1 %collective-permute-done.31.refs_33_ = bf16[512,256]{1,0:T(8,128)(2,1)S(1)} collective-permute-done((bf16[512,256]{1,0:T(8,128)(2,1)S(1)}, bf16[512,256]{1,0:T(8,128)(2,1)S(1)}, u32[]{:S(2)}, u32[]{:S(2)}) %collective-permute-start.31) | collective-permute-done | bytes 262176 | tf_op jit(solution)/shard_map/ppermute | solution.py:191
  114.2 1.4 collective-permute-start.15
  116.2 1.3 collective-permute-start.32
  118.1 2.6 collective-permute-start.3
  121.7 4.6 %all-to-all-start = ((bf16[1,4,4,64,512]{4,3,1,0,2:T(8,128)(2,1)}), bf16[1,4,4,64,512]{4,3,1,0,2:T(8,128)(2,1)}, u32[]{:S(2)}, u32[]{:S(2)}) async-start(bf16[1,4,4,64,512]{4,3,1,0,2:T(8,128)(2,1)} %copy.13), calls=%async_computation | async-start | bytes 2097152 | tf_op jit(solution)/shard_map/all_to_all | solution.py:167
  128.6 1.3 collective-permute-start.33
  131.3 1.6 collective-permute-done.10.refs_12_
  132.9 16.6 %collective-permute-start.4 = (bf16[2,512,256]{2,1,0:T(8,128)(2,1)}, bf16[2,512,256]{2,1,0:T(8,128)(2,1)}, u32[]{:S(2)}, u32[]{:S(2)}) collective-permute-start(bf16[2,512,256]{2,1,0:T(8,128)(2,1)} %collective-permute-done.3.refs_4_), channel_id=1, source_target_pairs={{0,2},{2,4},{4,6},{6,7},{7,5},{5,3},{3,1},{1,0},{8,10},{10,12},{12... | collective-permute-start | bytes 1572872 | tf_op jit(solution)/shard_map/ppermute | solution.py:180
  149.6 1.1 broadcast_select_fusion.3
  153.6 1.3 collective-permute-start.34
  155.6 1.4 collective-permute-start.26
  157.0 4.8 %collective-permute-done.11.refs_13_ = bf16[2,512,256]{2,1,0:T(8,128)(2,1)} collective-permute-done((bf16[2,512,256]{2,1,0:T(8,128)(2,1)}, bf16[2,512,256]{2,1,0:T(8,128)(2,1)}, u32[]{:S(2)}, u32[]{:S(2)}) %collective-permute-start.11) | collective-permute-done | bytes 524320 | tf_op jit(solution)/shard_map/ppermute | solution.py:181
  161.8 1.7 collective-permute-start.5
  165.2 5.1 %all-to-all-start.1 = ((bf16[8,2,64,512]{3,2,1,0:T(8,128)(2,1)}), bf16[8,2,64,512]{3,2,1,0:T(8,128)(2,1)}, u32[]{:S(2)}, u32[]{:S(2)}) async-start(bf16[8,2,64,512]{3,2,1,0:T(8,128)(2,1)} %bitcast.51), calls=%async_computation.1 | async-start | bytes 2097152 | tf_op jit(solution)/shard_map/all_to_all | solution.py:168
  170.9 1.1 broadcast_select_fusion.2
  172.1 3.0 collective-permute-done.12.refs_14_
  176.9 1.3 collective-permute-start.35
  178.2 1.1 broadcast_select_fusion.1
  179.4 13.4 %collective-permute-done.35.refs_37_ = bf16[512,256]{1,0:T(8,128)(2,1)S(1)} collective-permute-done((bf16[512,256]{1,0:T(8,128)(2,1)S(1)}, bf16[512,256]{1,0:T(8,128)(2,1)S(1)}, u32[]{:S(2)}, u32[]{:S(2)}) %collective-permute-start.35) | collective-permute-done | bytes 262176 | tf_op jit(solution)/shard_map/ppermute | solution.py:191
  193.5 15.2 %collective-permute-done.13.refs_15_ = bf16[2,512,256]{2,1,0:T(8,128)(2,1)S(1)} collective-permute-done((bf16[2,512,256]{2,1,0:T(8,128)(2,1)}, bf16[2,512,256]{2,1,0:T(8,128)(2,1)S(1)}, u32[]{:S(2)}, u32[]{:S(2)}) %collective-permute-start.13) | collective-permute-done | bytes 524320 | tf_op jit(solution)/shard_map/ppermute | solution.py:181
  209.3 1.3 collective-permute-start.36
  215.3 1.8 collective-permute-done.36.refs_38_
  217.8 1.3 collective-permute-start.37
  219.8 1.4 collective-permute-start.29
  221.8 1.4 collective-permute-start.21
  223.2 2.3 copy.21
  244.5 11.1 %solve.1.refs_16_ = bf16[512,2048]{1,0:T(8,128)(2,1)} custom-call(s32[14]{0:T(128)S(1)} %stack.105.meta, bf16[2,512,256]{2,1,0:T(8,128)(2,1)S(1)} %copy-done.16, bf16[2,512,256]{2,1,0:T(8,128)(2,1)S(1)} %collective-permute-done.refs_1_, bf16[2,512,256]{2,1,0:T(8,128)(2,1)S(1)} %collective-permute-done.1.refs_2_, ...), custom_call_target="tpu_custom_call" | custom-call | flops 4294967296 | bytes 12582912 | tf_op jit(solution)/shard_map/solve/pallas_call | solution.py:218
  255.7 5.8 %collective-permute-start.41 = (bf16[512,2048]{1,0:T(8,128)(2,1)}, bf16[512,2048]{1,0:T(8,128)(2,1)}, u32[]{:S(2)}, u32[]{:S(2)}) collective-permute-start(bf16[512,2048]{1,0:T(8,128)(2,1)} %solve.1.refs_16_), channel_id=1, source_target_pairs={{0,8},{8,0},{16,24},{24,16},{1,9},{9,1},{17,25},{25,17},{2,10},{10... | collective-permute-start | bytes 6291464 | tf_op jit(solution)/shard_map/ppermute | solution.py:234
  262.2 2.3 fusion
  264.5 2.3 fusion.1
  267.1 2.3 fusion.2
  269.5 3.9 %subtract_convert_fusion = (bf16[2,512,512]{2,1,0:T(8,128)(2,1)}, bf16[2,512,512]{2,1,0:T(8,128)(2,1)}) fusion(bf16[2,8,64,512]{3,2,1,0:T(8,128)(2,1)} %collective-permute-done.44.refs_21_, f32[2,512,512,1]{2,1,3,0:T(8,128)S(1)} %fusion.2, f32[2,512,512,1]{2,1,3,0:T(8,128)S(1)} %fusion.1, f32[2,512,512,1]{2,1,3,0:T(8,128)S(1)} %fusion), kind=kOutput, calls=%fused_computation.3 | convolution fusion | flops 540540928 | bytes 9437184 | tf_op jit(solution)/shard_map/jcnk,jcnl->jkl/dot_general | solution.py:235
  273.4 40.8 %main.1 = (bf16[4,2,2048,512]{3,2,1,0:T(8,128)(2,1)}, bf16[4,2,512,512]{3,2,1,0:T(8,128)(2,1)}) custom-call(s32[28]{0:T(128)S(1)} %concatenate.3.meta, bf16[2,512,256]{2,1,0:T(8,128)(2,1)S(1)} %copy-done.17, bf16[2,512,256]{2,1,0:T(8,128)(2,1)S(1)} %collective-permute-done.refs_1_, bf16[2,512,256]{2,1,0:T(8,128)(2,1)S(1)} %collective-permute-done.1.refs_2_, ...), custom_call_target="tpu_custom_call" | custom-call | flops 23622320128 | bytes 33554432 | tf_op jit(solution)/shard_map/main/pallas_call | solution.py:243
  (179 shorter events, 47.0 us)
Async XLA Ops:
  7.2 55.9 %all-gather.3.cloned.1.call-start = ((), (), s32[]{:S(2)}) async-start(), calls=%async_computation.2 | async-start | bytes 2359296 | tf_op jit(solution)/shard_map/all_gather | solution.py:172
  11.6 16.6 %collective-permute-start.7 = (bf16[2,512,256]{2,1,0:T(8,128)(2,1)S(1)}, bf16[2,512,256]{2,1,0:T(8,128)(2,1)S(1)}, u32[]{:S(2)}, u32[]{:S(2)}) collective-permute-start(bf16[2,512,256]{2,1,0:T(8,128)(2,1)S(1)} %get-tuple-element.5.refs_8_), channel_id=1, source_target_pairs={{2,0},{4,2},{6,4},{7,6},{5,7},{3,5},{1,3},{0,1},{10,8},{12,10},{14... | collective-permute-start | bytes 1572872 | tf_op jit(solution)/shard_map/ppermute | solution.py:181
  12.9 17.9 %collective-permute-start = (bf16[2,512,256]{2,1,0:T(8,128)(2,1)S(1)}, bf16[2,512,256]{2,1,0:T(8,128)(2,1)S(1)}, u32[]{:S(2)}, u32[]{:S(2)}) collective-permute-start(bf16[2,512,256]{2,1,0:T(8,128)(2,1)S(1)} %get-tuple-element.6.refs_0_), channel_id=1, source_target_pairs={{0,2},{2,4},{4,6},{6,7},{7,5},{5,3},{3,1},{1,0},{8,10},{10,12},{12... | collective-permute-start | bytes 1572872 | tf_op jit(solution)/shard_map/ppermute | solution.py:180
  28.2 40.0 %collective-permute-start.8 = (bf16[2,512,256]{2,1,0:T(8,128)(2,1)S(1)}, bf16[2,512,256]{2,1,0:T(8,128)(2,1)S(1)}, u32[]{:S(2)}, u32[]{:S(2)}) collective-permute-start(bf16[2,512,256]{2,1,0:T(8,128)(2,1)S(1)} %collective-permute-done.7.refs_9_), channel_id=1, source_target_pairs={{2,0},{4,2},{6,4},{7,6},{5,7},{3,5},{1,3},{0,1},{10,8},{12,10},{14... | collective-permute-start | bytes 1572872 | tf_op jit(solution)/shard_map/ppermute | solution.py:181
  30.7 37.8 %collective-permute-start.1 = (bf16[2,512,256]{2,1,0:T(8,128)(2,1)S(1)}, bf16[2,512,256]{2,1,0:T(8,128)(2,1)S(1)}, u32[]{:S(2)}, u32[]{:S(2)}) collective-permute-start(bf16[2,512,256]{2,1,0:T(8,128)(2,1)S(1)} %collective-permute-done.refs_1_), channel_id=1, source_target_pairs={{0,2},{2,4},{4,6},{6,7},{7,5},{5,3},{3,1},{1,0},{8,10},{10,12},{12... | collective-permute-start | bytes 1572872 | tf_op jit(solution)/shard_map/ppermute | solution.py:180
  32.7 10.2 %collective-permute-start.30 = (bf16[512,256]{1,0:T(8,128)(2,1)S(1)}, bf16[512,256]{1,0:T(8,128)(2,1)S(1)}, u32[]{:S(2)}, u32[]{:S(2)}) collective-permute-start(bf16[512,256]{1,0:T(8,128)(2,1)S(1)} %get-tuple-element.28), channel_id=1, source_target_pairs={{0,24},{1,25},{10,26},{11,27},{20,12},{21,13},{30,14},{31,15}} | collective-permute-start | bytes 786440 | tf_op jit(solution)/shard_map/ppermute | solution.py:191
  34.0 32.2 %collective-permute-start.22 = (bf16[512,256]{1,0:T(8,128)(2,1)}, bf16[512,256]{1,0:T(8,128)(2,1)}, u32[]{:S(2)}, u32[]{:S(2)}) collective-permute-start(bf16[512,256]{1,0:T(8,128)(2,1)} %get-tuple-element.29), channel_id=1, source_target_pairs={{0,16},{1,17},{10,18},{11,19},{20,4},{21,5},{30,6},{31,7}} | collective-permute-start | bytes 786440 | tf_op jit(solution)/shard_map/ppermute | solution.py:191
  35.4 32.1 %collective-permute-start.14 = (bf16[512,256]{1,0:T(8,128)(2,1)}, bf16[512,256]{1,0:T(8,128)(2,1)}, u32[]{:S(2)}, u32[]{:S(2)}) collective-permute-start(bf16[512,256]{1,0:T(8,128)(2,1)} %get-tuple-element.30), channel_id=1, source_target_pairs={{0,8},{1,9},{10,2},{11,3},{20,28},{21,29},{30,22},{31,23}} | collective-permute-start | bytes 786440 | tf_op jit(solution)/shard_map/ppermute | solution.py:199
  63.1 102.1 %collective-permute-start.38 = (bf16[8,64,2048]{2,1,0:T(8,128)(2,1)}, bf16[8,64,2048]{2,1,0:T(8,128)(2,1)}, u32[]{:S(2)}, u32[]{:S(2)}) collective-permute-start(bf16[8,64,2048]{2,1,0:T(8,128)(2,1)} %bitcast.47.refs_40_), channel_id=1, source_target_pairs={{0,16},{8,24},{16,0},{24,8},{1,17},{9,25},{17,1},{25,9},{2,18},{10... | collective-permute-start | bytes 6291464 | tf_op jit(solution)/shard_map/ppermute | solution.py:36
  66.2 47.3 %collective-permute-start.31 = (bf16[512,256]{1,0:T(8,128)(2,1)S(1)}, bf16[512,256]{1,0:T(8,128)(2,1)S(1)}, u32[]{:S(2)}, u32[]{:S(2)}) collective-permute-start(bf16[512,256]{1,0:T(8,128)(2,1)S(1)} %get-tuple-element.25), channel_id=1, source_target_pairs={{0,24},{1,25},{10,26},{11,27},{20,12},{21,13},{30,14},{31,15}} | collective-permute-start | bytes 786440 | tf_op jit(solution)/shard_map/ppermute | solution.py:191
  67.5 48.0 %collective-permute-start.23 = (bf16[512,256]{1,0:T(8,128)(2,1)S(1)}, bf16[512,256]{1,0:T(8,128)(2,1)S(1)}, u32[]{:S(2)}, u32[]{:S(2)}) collective-permute-start(bf16[512,256]{1,0:T(8,128)(2,1)S(1)} %get-tuple-element.26), channel_id=1, source_target_pairs={{0,16},{1,17},{10,18},{11,19},{20,4},{21,5},{30,6},{31,7}} | collective-permute-start | bytes 786440 | tf_op jit(solution)/shard_map/ppermute | solution.py:191
  68.2 49.3 %collective-permute-start.9 = (bf16[2,512,256]{2,1,0:T(8,128)(2,1)S(1)}, bf16[2,512,256]{2,1,0:T(8,128)(2,1)S(1)}, u32[]{:S(2)}, u32[]{:S(2)}) collective-permute-start(bf16[2,512,256]{2,1,0:T(8,128)(2,1)S(1)} %collective-permute-done.8.refs_10_), channel_id=1, source_target_pairs={{2,0},{4,2},{6,4},{7,6},{5,7},{3,5},{1,3},{0,1},{10,8},{12,10},{14... | collective-permute-start | bytes 1572872 | tf_op jit(solution)/shard_map/ppermute | solution.py:181
  68.6 49.5 %collective-permute-start.2 = (bf16[2,512,256]{2,1,0:T(8,128)(2,1)S(1)}, bf16[2,512,256]{2,1,0:T(8,128)(2,1)S(1)}, u32[]{:S(2)}, u32[]{:S(2)}) collective-permute-start(bf16[2,512,256]{2,1,0:T(8,128)(2,1)S(1)} %collective-permute-done.1.refs_2_), channel_id=1, source_target_pairs={{0,2},{2,4},{4,6},{6,7},{7,5},{5,3},{3,1},{1,0},{8,10},{10,12},{12... | collective-permute-start | bytes 1572872 | tf_op jit(solution)/shard_map/ppermute | solution.py:180
  114.2 12.2 %collective-permute-start.15 = (bf16[512,256]{1,0:T(8,128)(2,1)}, bf16[512,256]{1,0:T(8,128)(2,1)}, u32[]{:S(2)}, u32[]{:S(2)}) collective-permute-start(bf16[512,256]{1,0:T(8,128)(2,1)} %get-tuple-element.27), channel_id=1, source_target_pairs={{0,8},{1,9},{10,2},{11,3},{20,28},{21,29},{30,22},{31,23}} | collective-permute-start | bytes 786440 | tf_op jit(solution)/shard_map/ppermute | solution.py:199
  116.2 10.8 %collective-permute-start.32 = (bf16[512,256]{1,0:T(8,128)(2,1)}, bf16[512,256]{1,0:T(8,128)(2,1)}, u32[]{:S(2)}, u32[]{:S(2)}) collective-permute-start(bf16[512,256]{1,0:T(8,128)(2,1)} %get-tuple-element.22), channel_id=1, source_target_pairs={{0,24},{1,25},{10,26},{11,27},{20,12},{21,13},{30,14},{31,15}} | collective-permute-start | bytes 786440 | tf_op jit(solution)/shard_map/ppermute | solution.py:191
  117.5 15.4 %collective-permute-start.10 = (bf16[2,512,256]{2,1,0:T(8,128)(2,1)S(1)}, bf16[2,512,256]{2,1,0:T(8,128)(2,1)}, u32[]{:S(2)}, u32[]{:S(2)}) collective-permute-start(bf16[2,512,256]{2,1,0:T(8,128)(2,1)S(1)} %collective-permute-done.9.refs_11_), channel_id=1, source_target_pairs={{2,0},{4,2},{6,4},{7,6},{5,7},{3,5},{1,3},{0,1},{10,8},{12,10},{14... | collective-permute-start | bytes 1572872 | tf_op jit(solution)/shard_map/ppermute | solution.py:181
  118.1 14.8 %collective-permute-start.3 = (bf16[2,512,256]{2,1,0:T(8,128)(2,1)S(1)}, bf16[2,512,256]{2,1,0:T(8,128)(2,1)}, u32[]{:S(2)}, u32[]{:S(2)}) collective-permute-start(bf16[2,512,256]{2,1,0:T(8,128)(2,1)S(1)} %collective-permute-done.2.refs_3_), channel_id=1, source_target_pairs={{0,2},{2,4},{4,6},{6,7},{7,5},{5,3},{3,1},{1,0},{8,10},{10,12},{12... | collective-permute-start | bytes 1572872 | tf_op jit(solution)/shard_map/ppermute | solution.py:180
  121.7 43.4 %all-to-all-start = ((bf16[1,4,4,64,512]{4,3,1,0,2:T(8,128)(2,1)}), bf16[1,4,4,64,512]{4,3,1,0,2:T(8,128)(2,1)}, u32[]{:S(2)}, u32[]{:S(2)}) async-start(bf16[1,4,4,64,512]{4,3,1,0,2:T(8,128)(2,1)} %copy.13), calls=%async_computation | async-start | bytes 2097152 | tf_op jit(solution)/shard_map/all_to_all | solution.py:167
  126.4 1.5 collective-permute-start.24
  127.1 2.8 collective-permute-start.16
  128.6 22.1 %collective-permute-start.33 = (bf16[512,256]{1,0:T(8,128)(2,1)S(1)}, bf16[512,256]{1,0:T(8,128)(2,1)S(1)}, u32[]{:S(2)}, u32[]{:S(2)}) collective-permute-start(bf16[512,256]{1,0:T(8,128)(2,1)S(1)} %get-tuple-element.19), channel_id=1, source_target_pairs={{0,24},{1,25},{10,26},{11,27},{20,12},{21,13},{30,14},{31,15}} | collective-permute-start | bytes 786440 | tf_op jit(solution)/shard_map/ppermute | solution.py:191
  130.6 22.3 %collective-permute-start.25 = (bf16[512,256]{1,0:T(8,128)(2,1)S(1)}, bf16[512,256]{1,0:T(8,128)(2,1)S(1)}, u32[]{:S(2)}, u32[]{:S(2)}) collective-permute-start(bf16[512,256]{1,0:T(8,128)(2,1)S(1)} %get-tuple-element.20), channel_id=1, source_target_pairs={{0,16},{1,17},{10,18},{11,19},{20,4},{21,5},{30,6},{31,7}} | collective-permute-start | bytes 786440 | tf_op jit(solution)/shard_map/ppermute | solution.py:191
  132.9 28.9 %collective-permute-start.11 = (bf16[2,512,256]{2,1,0:T(8,128)(2,1)}, bf16[2,512,256]{2,1,0:T(8,128)(2,1)}, u32[]{:S(2)}, u32[]{:S(2)}) collective-permute-start(bf16[2,512,256]{2,1,0:T(8,128)(2,1)} %collective-permute-done.10.refs_12_), channel_id=1, source_target_pairs={{2,0},{4,2},{6,4},{7,6},{5,7},{3,5},{1,3},{0,1},{10,8},{12,10},{14... | collective-permute-start | bytes 1572872 | tf_op jit(solution)/shard_map/ppermute | solution.py:181
  132.9 28.9 %collective-permute-start.4 = (bf16[2,512,256]{2,1,0:T(8,128)(2,1)}, bf16[2,512,256]{2,1,0:T(8,128)(2,1)}, u32[]{:S(2)}, u32[]{:S(2)}) collective-permute-start(bf16[2,512,256]{2,1,0:T(8,128)(2,1)} %collective-permute-done.3.refs_4_), channel_id=1, source_target_pairs={{0,2},{2,4},{4,6},{6,7},{7,5},{5,3},{3,1},{1,0},{8,10},{10,12},{12... | collective-permute-start | bytes 1572872 | tf_op jit(solution)/shard_map/ppermute | solution.py:180
  151.4 3.6 %collective-permute-start.17 = (bf16[512,256]{1,0:T(8,128)(2,1)S(1)}, bf16[512,256]{1,0:T(8,128)(2,1)S(1)}, u32[]{:S(2)}, u32[]{:S(2)}) collective-permute-start(bf16[512,256]{1,0:T(8,128)(2,1)S(1)} %get-tuple-element.21), channel_id=1, source_target_pairs={{0,8},{1,9},{10,2},{11,3},{20,28},{21,29},{30,22},{31,23}} | collective-permute-start | bytes 786440 | tf_op jit(solution)/shard_map/ppermute | solution.py:199
  153.6 10.0 %collective-permute-start.34 = (bf16[512,256]{1,0:T(8,128)(2,1)S(1)}, bf16[512,256]{1,0:T(8,128)(2,1)S(1)}, u32[]{:S(2)}, u32[]{:S(2)}) collective-permute-start(bf16[512,256]{1,0:T(8,128)(2,1)S(1)} %get-tuple-element.16), channel_id=1, source_target_pairs={{0,24},{1,25},{10,26},{11,27},{20,12},{21,13},{30,14},{31,15}} | collective-permute-start | bytes 786440 | tf_op jit(solution)/shard_map/ppermute | solution.py:191
  155.6 14.6 %collective-permute-start.26 = (bf16[512,256]{1,0:T(8,128)(2,1)}, bf16[512,256]{1,0:T(8,128)(2,1)}, u32[]{:S(2)}, u32[]{:S(2)}) collective-permute-start(bf16[512,256]{1,0:T(8,128)(2,1)} %get-tuple-element.17), channel_id=1, source_target_pairs={{0,16},{1,17},{10,18},{11,19},{20,4},{21,5},{30,6},{31,7}} | collective-permute-start | bytes 786440 | tf_op jit(solution)/shard_map/ppermute | solution.py:191
  161.8 13.2 %collective-permute-start.12 = (bf16[2,512,256]{2,1,0:T(8,128)(2,1)}, bf16[2,512,256]{2,1,0:T(8,128)(2,1)}, u32[]{:S(2)}, u32[]{:S(2)}) collective-permute-start(bf16[2,512,256]{2,1,0:T(8,128)(2,1)} %collective-permute-done.11.refs_13_), channel_id=1, source_target_pairs={{2,0},{4,2},{6,4},{7,6},{5,7},{3,5},{1,3},{0,1},{10,8},{12,10},{14... | collective-permute-start | bytes 1572872 | tf_op jit(solution)/shard_map/ppermute | solution.py:181
  161.8 14.1 %collective-permute-start.5 = (bf16[2,512,256]{2,1,0:T(8,128)(2,1)}, bf16[2,512,256]{2,1,0:T(8,128)(2,1)}, u32[]{:S(2)}, u32[]{:S(2)}) collective-permute-start(bf16[2,512,256]{2,1,0:T(8,128)(2,1)} %collective-permute-done.4.refs_5_), channel_id=1, source_target_pairs={{0,2},{2,4},{4,6},{6,7},{7,5},{5,3},{3,1},{1,0},{8,10},{10,12},{12... | collective-permute-start | bytes 1572872 | tf_op jit(solution)/shard_map/ppermute | solution.py:180
  164.3 61.8 %collective-permute-start.39 = (bf16[8,64,2048]{2,1,0:T(8,128)(2,1)}, bf16[8,64,2048]{2,1,0:T(8,128)(2,1)}, u32[]{:S(2)}, u32[]{:S(2)}) collective-permute-start(bf16[8,64,2048]{2,1,0:T(8,128)(2,1)} %bitcast.47.refs_40_), channel_id=1, source_target_pairs={{0,8},{8,0},{16,24},{24,16},{1,9},{9,1},{17,25},{25,17},{2,10},{10... | collective-permute-start | bytes 6291464 | tf_op jit(solution)/shard_map/ppermute | solution.py:37
  165.1 60.9 %collective-permute-start.40 = (bf16[8,64,2048]{2,1,0:T(8,128)(2,1)}, bf16[8,64,2048]{2,1,0:T(8,128)(2,1)}, u32[]{:S(2)}, u32[]{:S(2)}) collective-permute-start(bf16[8,64,2048]{2,1,0:T(8,128)(2,1)} %collective-permute-done.38.refs_41_), channel_id=1, source_target_pairs={{0,8},{8,0},{16,24},{24,16},{1,9},{9,1},{17,25},{25,17},{2,10},{10... | collective-permute-start | bytes 6291464 | tf_op jit(solution)/shard_map/ppermute | solution.py:37
  165.2 58.1 %all-to-all-start.1 = ((bf16[8,2,64,512]{3,2,1,0:T(8,128)(2,1)}), bf16[8,2,64,512]{3,2,1,0:T(8,128)(2,1)}, u32[]{:S(2)}, u32[]{:S(2)}) async-start(bf16[8,2,64,512]{3,2,1,0:T(8,128)(2,1)} %bitcast.51), calls=%async_computation.1 | async-start | bytes 2097152 | tf_op jit(solution)/shard_map/all_to_all | solution.py:168
  170.3 6.6 %collective-permute-start.18 = (bf16[512,256]{1,0:T(8,128)(2,1)}, bf16[512,256]{1,0:T(8,128)(2,1)S(1)}, u32[]{:S(2)}, u32[]{:S(2)}) collective-permute-start(bf16[512,256]{1,0:T(8,128)(2,1)} %get-tuple-element.18), channel_id=1, source_target_pairs={{0,8},{1,9},{10,2},{11,3},{20,28},{21,29},{30,22},{31,23}} | collective-permute-start | bytes 786440 | tf_op jit(solution)/shard_map/ppermute | solution.py:199
  175.1 33.6 %collective-permute-start.13 = (bf16[2,512,256]{2,1,0:T(8,128)(2,1)}, bf16[2,512,256]{2,1,0:T(8,128)(2,1)S(1)}, u32[]{:S(2)}, u32[]{:S(2)}) collective-permute-start(bf16[2,512,256]{2,1,0:T(8,128)(2,1)} %collective-permute-done.12.refs_14_), channel_id=1, source_target_pairs={{2,0},{4,2},{6,4},{7,6},{5,7},{3,5},{1,3},{0,1},{10,8},{12,10},{14... | collective-permute-start | bytes 1572872 | tf_op jit(solution)/shard_map/ppermute | solution.py:181
  175.9 33.4 %collective-permute-start.6 = (bf16[2,512,256]{2,1,0:T(8,128)(2,1)}, bf16[2,512,256]{2,1,0:T(8,128)(2,1)S(1)}, u32[]{:S(2)}, u32[]{:S(2)}) collective-permute-start(bf16[2,512,256]{2,1,0:T(8,128)(2,1)} %collective-permute-done.5.refs_6_), channel_id=1, source_target_pairs={{0,2},{2,4},{4,6},{6,7},{7,5},{5,3},{3,1},{1,0},{8,10},{10,12},{12... | collective-permute-start | bytes 1572872 | tf_op jit(solution)/shard_map/ppermute | solution.py:180
  176.9 15.9 %collective-permute-start.35 = (bf16[512,256]{1,0:T(8,128)(2,1)S(1)}, bf16[512,256]{1,0:T(8,128)(2,1)S(1)}, u32[]{:S(2)}, u32[]{:S(2)}) collective-permute-start(bf16[512,256]{1,0:T(8,128)(2,1)S(1)} %get-tuple-element.13), channel_id=1, source_target_pairs={{0,24},{1,25},{10,26},{11,27},{20,12},{21,13},{30,14},{31,15}} | collective-permute-start | bytes 786440 | tf_op jit(solution)/shard_map/ppermute | solution.py:191
  192.8 18.8 %collective-permute-start.27 = (bf16[512,256]{1,0:T(8,128)(2,1)S(1)}, bf16[512,256]{1,0:T(8,128)(2,1)S(1)}, u32[]{:S(2)}, u32[]{:S(2)}) collective-permute-start(bf16[512,256]{1,0:T(8,128)(2,1)S(1)} %get-tuple-element.14), channel_id=1, source_target_pairs={{0,16},{1,17},{10,18},{11,19},{20,4},{21,5},{30,6},{31,7}} | collective-permute-start | bytes 786440 | tf_op jit(solution)/shard_map/ppermute | solution.py:191
  208.7 4.3 %collective-permute-start.19 = (bf16[512,256]{1,0:T(8,128)(2,1)S(1)}, bf16[512,256]{1,0:T(8,128)(2,1)S(1)}, u32[]{:S(2)}, u32[]{:S(2)}) collective-permute-start(bf16[512,256]{1,0:T(8,128)(2,1)S(1)} %get-tuple-element.15), channel_id=1, source_target_pairs={{0,8},{1,9},{10,2},{11,3},{20,28},{21,29},{30,22},{31,23}} | collective-permute-start | bytes 786440 | tf_op jit(solution)/shard_map/ppermute | solution.py:199
  209.3 7.7 %collective-permute-start.36 = (bf16[512,256]{1,0:T(8,128)(2,1)S(1)}, bf16[512,256]{1,0:T(8,128)(2,1)S(1)}, u32[]{:S(2)}, u32[]{:S(2)}) collective-permute-start(bf16[512,256]{1,0:T(8,128)(2,1)S(1)} %get-tuple-element.10), channel_id=1, source_target_pairs={{0,24},{1,25},{10,26},{11,27},{20,12},{21,13},{30,14},{31,15}} | collective-permute-start | bytes 786440 | tf_op jit(solution)/shard_map/ppermute | solution.py:191
  212.3 6.8 %collective-permute-start.28 = (bf16[512,256]{1,0:T(8,128)(2,1)S(1)}, bf16[512,256]{1,0:T(8,128)(2,1)S(1)}, u32[]{:S(2)}, u32[]{:S(2)}) collective-permute-start(bf16[512,256]{1,0:T(8,128)(2,1)S(1)} %get-tuple-element.11), channel_id=1, source_target_pairs={{0,16},{1,17},{10,18},{11,19},{20,4},{21,5},{30,6},{31,7}} | collective-permute-start | bytes 786440 | tf_op jit(solution)/shard_map/ppermute | solution.py:191
  213.7 7.5 %collective-permute-start.20 = (bf16[512,256]{1,0:T(8,128)(2,1)S(1)}, bf16[512,256]{1,0:T(8,128)(2,1)S(1)}, u32[]{:S(2)}, u32[]{:S(2)}) collective-permute-start(bf16[512,256]{1,0:T(8,128)(2,1)S(1)} %get-tuple-element.12), channel_id=1, source_target_pairs={{0,8},{1,9},{10,2},{11,3},{20,28},{21,29},{30,22},{31,23}} | collective-permute-start | bytes 786440 | tf_op jit(solution)/shard_map/ppermute | solution.py:199
  217.8 8.2 %collective-permute-start.37 = (bf16[512,256]{1,0:T(8,128)(2,1)}, bf16[512,256]{1,0:T(8,128)(2,1)}, u32[]{:S(2)}, u32[]{:S(2)}) collective-permute-start(bf16[512,256]{1,0:T(8,128)(2,1)} %get-tuple-element.7), channel_id=1, source_target_pairs={{0,24},{1,25},{10,26},{11,27},{20,12},{21,13},{30,14},{31,15}} | collective-permute-start | bytes 786440 | tf_op jit(solution)/shard_map/ppermute | solution.py:191
  219.8 6.3 %collective-permute-start.29 = (bf16[512,256]{1,0:T(8,128)(2,1)}, bf16[512,256]{1,0:T(8,128)(2,1)}, u32[]{:S(2)}, u32[]{:S(2)}) collective-permute-start(bf16[512,256]{1,0:T(8,128)(2,1)} %get-tuple-element.8), channel_id=1, source_target_pairs={{0,16},{1,17},{10,18},{11,19},{20,4},{21,5},{30,6},{31,7}} | collective-permute-start | bytes 786440 | tf_op jit(solution)/shard_map/ppermute | solution.py:191
  221.8 4.2 %collective-permute-start.21 = (bf16[512,256]{1,0:T(8,128)(2,1)}, bf16[512,256]{1,0:T(8,128)(2,1)}, u32[]{:S(2)}, u32[]{:S(2)}) collective-permute-start(bf16[512,256]{1,0:T(8,128)(2,1)} %get-tuple-element.9), channel_id=1, source_target_pairs={{0,8},{1,9},{10,2},{11,3},{20,28},{21,29},{30,22},{31,23}} | collective-permute-start | bytes 786440 | tf_op jit(solution)/shard_map/ppermute | solution.py:199
  225.9 35.6 %collective-permute-start.42 = (bf16[2,8,64,512]{3,2,1,0:T(8,128)(2,1)}, bf16[2,8,64,512]{3,2,1,0:T(8,128)(2,1)}, u32[]{:S(2)}, u32[]{:S(2)}) collective-permute-start(bf16[2,8,64,512]{3,2,1,0:T(8,128)(2,1)} %bitcast.103.refs_18_), channel_id=1, source_target_pairs={{0,16},{8,24},{16,0},{24,8},{1,17},{9,25},{17,1},{25,9},{2,18},{10... | collective-permute-start | bytes 3145736 | tf_op jit(solution)/shard_map/ppermute | solution.py:36
  255.7 17.7 %collective-permute-start.41 = (bf16[512,2048]{1,0:T(8,128)(2,1)}, bf16[512,2048]{1,0:T(8,128)(2,1)}, u32[]{:S(2)}, u32[]{:S(2)}) collective-permute-start(bf16[512,2048]{1,0:T(8,128)(2,1)} %solve.1.refs_16_), channel_id=1, source_target_pairs={{0,8},{8,0},{16,24},{24,16},{1,9},{9,1},{17,25},{25,17},{2,10},{10... | collective-permute-start | bytes 6291464 | tf_op jit(solution)/shard_map/ppermute | solution.py:234
  261.5 5.6 %collective-permute-start.43 = (bf16[2,8,64,512]{3,2,1,0:T(8,128)(2,1)}, bf16[2,8,64,512]{3,2,1,0:T(8,128)(2,1)}, u32[]{:S(2)}, u32[]{:S(2)}) collective-permute-start(bf16[2,8,64,512]{3,2,1,0:T(8,128)(2,1)} %bitcast.103.refs_18_), channel_id=1, source_target_pairs={{0,8},{8,0},{16,24},{24,16},{1,9},{9,1},{17,25},{25,17},{2,10},{10... | collective-permute-start | bytes 3145736 | tf_op jit(solution)/shard_map/ppermute | solution.py:37
  261.5 8.0 %collective-permute-start.44 = (bf16[2,8,64,512]{3,2,1,0:T(8,128)(2,1)}, bf16[2,8,64,512]{3,2,1,0:T(8,128)(2,1)}, u32[]{:S(2)}, u32[]{:S(2)}) collective-permute-start(bf16[2,8,64,512]{3,2,1,0:T(8,128)(2,1)} %collective-permute-done.42.refs_19_), channel_id=1, source_target_pairs={{0,8},{8,0},{16,24},{24,16},{1,9},{9,1},{17,25},{25,17},{2,10},{10... | collective-permute-start | bytes 3145736 | tf_op jit(solution)/shard_map/ppermute | solution.py:37
  (50 other events, 567.5 us)
Sparse Core Ops, SparseCore 0:
  10.1 52.8 all-gather.2

commit v2 on v1

v2 whole, which is shorter than its diff:
```python
import functools

import jax
import jax.numpy as jnp
from jax import lax
from jax.experimental import pallas as pl
from jax.experimental.pallas import tpu as pltpu
from jax.sharding import PartitionSpec as P

NT = (((1,), (1,)), ((), ()))
NN = (((1,), (0,)), ((), ()))
TN = (((0,), (0,)), ((), ()))
BLOCK = 256
MIB = 1 << 20


def dot(a, b, dims):
    return lax.dot_general(a, b, dims, preferred_element_type=jnp.float32)


def ring_of(count):
    return list(range(0, count, 2)) + list(range(count - 1, 0, -2))


def ring_place(col, count):
    return jnp.where(col % 2 == 0, col // 2, count // 2 + (count - 1 - col) // 2)


def ring_col(place, count):
    place = place % count
    return jnp.where(place < count // 2, 2 * place, count - 1 - 2 * (place - count // 2))


def tie(array, *after):
    return lax.optimization_barrier((array, *after))[0]


def gather_y(piece, rows):
    return [piece] + [
        lax.ppermute(piece, "row", [(i, (i + 2 * step) % rows) for i in range(rows)]) for step in range(1, rows // 2)
    ]


def swap_cores(held, rows):
    return [lax.ppermute(h, "row", [(i, i ^ 1) for i in range(rows)]) for h in held]


def gather_row(piece, rows):
    held = gather_y(piece, rows)
    return held + swap_cores(held, rows)


def row_ids(my_row, rows):
    other = jnp.bitwise_xor(my_row, 1)
    half = rows // 2
    return [(my_row - 2 * k) % rows for k in range(half)] + [(other - 2 * k) % rows for k in range(half)]


def solve_kernel(cols, meta, cut, *refs):
    it = iter(refs)
    inv = [next(it) for _ in range(4)]
    out, right, whole, solved, rsem, isem = it
    per, share, width = cut.shape[1:]
    core = meta[0]
    pulls = []
    for s in range(cols):
        for j in range(per):
            target = right.at[pl.ds(j * share, share), pl.ds(s * width, width)]
            pulls.append(pltpu.make_async_copy(cut.at[s, j], target, rsem.at[s, j]))
        for k in range(2):
            source = meta[1 + k * cols + s]
            pulls.append(pltpu.make_async_copy(inv[k].at[s], whole.at[source, core, k], isem.at[s, k, 0]))
            pulls.append(pltpu.make_async_copy(inv[2 + k].at[s], whole.at[source, 1 - core, k], isem.at[s, k, 1]))
    for copy in pulls:
        copy.start()
    for copy in pulls:
        copy.wait()
    size = right.shape[1]
    flat = whole.reshape(size, size)
    for b in range(size // BLOCK):
        end = (b + 1) * BLOCK
        solved[:, b * BLOCK : end] = dot(right[:, :end], flat[b * BLOCK : end, :end], NT).astype(jnp.bfloat16)
    for b in range(size // BLOCK):
        start = b * BLOCK
        out[:, start : start + BLOCK] = dot(
            solved[:, start:], flat[start:, start : start + BLOCK], NN
        ).astype(jnp.bfloat16)


def main_kernel(cols, rows, tiles, per, meta, *refs):
    it = iter(refs)
    cw = [next(it) for _ in range(cols)]
    ccw = [next(it) for _ in range(cols)]
    ours = [next(it) for _ in range(rows)]
    left = [next(it) for _ in range(rows)]
    update, gram = next(it), next(it)
    right, turned, whole, upd, grm, rsem, tsem, lsem, osem = it
    half = tiles // 2
    size, width, rank = right.shape[2], right.shape[2] // cols, right.shape[1]
    share = ours[0].shape[1]
    base = rows + 2 * cols

    def turned_copies():
        spots = [pl.multiple_of(meta[k] * share, share) for k in range(rows)]
        return [
            pltpu.make_async_copy(ours[k], turned.at[:, pl.ds(spots[k], share), :], tsem.at[k]) for k in range(rows)
        ]

    def left_copies():
        return [
            pltpu.make_async_copy(left[k].at[:, j], whole.at[j, :, meta[k]], lsem.at[k, j])
            for j in range(per)
            for k in range(rows)
        ]

    def right_copies(tile):
        msgs, start = (cw, rows) if tile < half else (ccw, rows + cols)
        spots = [pl.multiple_of(meta[start + s] * width, width) for s in range(cols)]
        return [
            pltpu.make_async_copy(
                msgs[s].at[tile % half], right.at[tile, :, pl.ds(spots[s], width)], rsem.at[tile, s]
            )
            for s in range(cols)
        ]

    for copy in turned_copies() + right_copies(0) + left_copies():
        copy.start()
    for tile in range(1, tiles):
        for copy in right_copies(tile):
            copy.start()
    for copy in turned_copies():
        copy.wait()
    flat = whole.reshape(per, size, rank)
    row_at = lax.broadcasted_iota(jnp.int32, (rank, rank), 0)
    col_at = lax.broadcasted_iota(jnp.int32, (rank, rank), 1)
    cut = rank // 2

    def outs(i, j, slot):
        return (
            pltpu.make_async_copy(upd.at[slot], update.at[i, j], osem.at[0, slot]),
            pltpu.make_async_copy(grm.at[slot], gram.at[i, j], osem.at[1, slot]),
        )

    def pair(at, carry):
        i, j, slot = at // per, at % per, at % 2
        for tile in range(tiles):

            @pl.when(at == tile * per)
            def _(tile=tile):
                for copy in right_copies(tile):
                    copy.wait()

        value = dot(right[i], turned[j], NT)
        live = (row_at < meta[base + i]) & (col_at < meta[base + tiles + j])
        value = jnp.where(live, value, 0.0).astype(jnp.bfloat16)

        @pl.when(at == 0)
        def _():
            for copy in left_copies():
                copy.wait()

        @pl.when(at >= 2)
        def _():
            for copy in outs(i, j, slot):
                copy.wait()

        upd[slot] = dot(flat[j], value, NT).astype(jnp.bfloat16)
        outs(i, j, slot)[0].start()
        top = (dot(upd[slot, :, :cut], upd[slot], TN) / size).astype(jnp.bfloat16)
        grm[slot, :cut] = top
        grm[slot, cut:, :cut] = top[:, cut:].T
        grm[slot, cut:, cut:] = (dot(upd[slot, :, cut:], upd[slot, :, cut:], TN) / size).astype(jnp.bfloat16)
        outs(i, j, slot)[1].start()
        return carry

    total = tiles * per
    lax.fori_loop(0, total, pair, 0)
    for at in range(max(0, total - 2), total):
        for copy in outs(at // per, at % per, at % 2):
            copy.wait()


def to_column(pieces):
    moved = lax.all_to_all(pieces, "row", 1, 0, tiled=False)
    cols = lax.axis_size("col")
    moved = moved.reshape((cols, -1) + pieces.shape[2:])
    return moved


def local(pan_left, pan_right, inverse, rank_list):
    tiles, slab, rank = pan_right.shape
    size = inverse.shape[1]
    rows, cols = lax.axis_size("row"), lax.axis_size("col")
    per = tiles * rows // cols
    my_row, my_col = lax.axis_index("row"), lax.axis_index("col")
    piece = slab // rows
    share = rank // rows
    half = tiles // 2
    turned = jnp.swapaxes(pan_right, 1, 2)
    place = ring_place(my_col, cols)
    cw_from = [ring_col(place - s + cols, cols) for s in range(cols)]
    ccw_from = [ring_col(place + s, cols) for s in range(cols)]
    ids = row_ids(my_row, rows)
    anywhere = pl.BlockSpec(memory_space=pltpu.HBM)
    vmem = pl.BlockSpec(memory_space=pltpu.VMEM)
    smem = pl.BlockSpec(memory_space=pltpu.SMEM)

    def solve(cut, inv):
        return pl.pallas_call(
            functools.partial(solve_kernel, cols),
            out_shape=jax.ShapeDtypeStruct((per * share, size), jnp.bfloat16),
            in_specs=[smem] + [anywhere] * 5,
            out_specs=vmem,
            scratch_shapes=[
                pltpu.VMEM((per * share, size), jnp.bfloat16),
                pltpu.VMEM((cols, 2, 2, slab // 4, size), jnp.bfloat16),
                pltpu.VMEM((per * share, size), jnp.bfloat16),
                pltpu.SemaphoreType.DMA((cols, per)),
                pltpu.SemaphoreType.DMA((cols, 2, 2)),
            ],
            compiler_params=pltpu.CompilerParams(vmem_limit_bytes=60 * MIB),
            cost_estimate=pl.CostEstimate(
                flops=2 * per * share * size * size, bytes_accessed=2 * size * (size + 2 * per * share), transcendentals=0
            ),
            name="solve",
        )(jnp.stack([my_row % 2] + cw_from + ccw_from).astype(jnp.int32), cut, *inv).reshape(per, share, size)

    cut = to_column(turned.reshape(tiles, rows, share, slab))
    ring = ring_of(cols)
    ahead = [(ring[i], ring[(i + 1) % cols]) for i in range(cols)]
    back = [(b, a) for a, b in ahead]
    part = slab // 2
    mine = lax.dynamic_slice_in_dim(inverse, (my_row % 2) * part, part, 0)
    inv_cw, inv_ccw = [mine[: part // 2]], [mine[part // 2 :]]
    for step in range(1, cols):
        inv_cw.append(lax.ppermute(inv_cw[-1], "col", ahead))
        inv_ccw.append(lax.ppermute(inv_ccw[-1], "col", back))
        held = (inv_cw[-1], inv_ccw[-1])
        if step == max(1, round((cols - 1) * 2 / 7)):
            held, cut = lax.optimization_barrier((held, cut))
            cut = lax.all_to_all(cut, "col", 0, 0, tiled=True)
        elif step == cols - 1:
            held, cut, turned = lax.optimization_barrier((held, cut, turned))
        else:
            held = lax.optimization_barrier(held)
        inv_cw[-1], inv_ccw[-1] = held
    inv = [jnp.stack(inv_cw), jnp.stack(inv_ccw)]
    inv = inv + swap_cores(inv, rows)
    cw, ccw = [turned[:half]], [turned[half:]]
    last = cols - 1
    marks = [max(1, round(last * m / 7)) for m in range(8)]
    left = pan_left
    for step in range(1, cols):
        cw.append(lax.ppermute(cw[-1], "col", ahead))
        ccw.append(lax.ppermute(ccw[-1], "col", back))
        if step == last:
            break
        held = (cw[-1], ccw[-1])
        if step == marks[1]:
            held, inv, left = lax.optimization_barrier((held, inv, left))
            ours = gather_y(solve(cut, inv), rows)
            left = to_column(left.reshape(tiles, rows, piece, rank))
        elif step == marks[2]:
            held, left = lax.optimization_barrier((held, left))
            left = lax.all_to_all(left, "col", 0, 0, tiled=True)
        elif step == marks[4]:
            held, left, ours = lax.optimization_barrier((held, left, ours))
            left = gather_y(left, rows)
            ours = ours + swap_cores(ours, rows)
        elif step == marks[6]:
            held, left, ours = lax.optimization_barrier((held, left, ours))
            left = left + swap_cores(left, rows)
        else:
            held = lax.optimization_barrier(held)
        cw[-1], ccw[-1] = held
    my_ranks = lax.dynamic_slice_in_dim(rank_list, my_row * tiles, tiles, 0)
    their_ranks = lax.dynamic_slice_in_dim(rank_list, my_col * per, per, 0)
    meta = jnp.concatenate([jnp.stack(ids + cw_from + ccw_from).astype(jnp.int32), my_ranks, their_ranks])
    operands = cw + ccw + ours + left
    update, gram = pl.pallas_call(
        functools.partial(main_kernel, cols, rows, tiles, per),
        out_shape=(
            jax.ShapeDtypeStruct((tiles, per, size, rank), jnp.bfloat16),
            jax.ShapeDtypeStruct((tiles, per, rank, rank), jnp.bfloat16),
        ),
        in_specs=[smem] + [anywhere] * len(operands),
        out_specs=(anywhere, anywhere),
        scratch_shapes=[
            pltpu.VMEM((tiles, rank, size), jnp.bfloat16),
            pltpu.VMEM((per, rank, size), jnp.bfloat16),
            pltpu.VMEM((per, cols, rows, piece, rank), jnp.bfloat16),
            pltpu.VMEM((2, size, rank), jnp.bfloat16),
            pltpu.VMEM((2, rank, rank), jnp.bfloat16),
            pltpu.SemaphoreType.DMA((tiles, cols)),
            pltpu.SemaphoreType.DMA((rows,)),
            pltpu.SemaphoreType.DMA((rows, per)),
            pltpu.SemaphoreType.DMA((2, 2)),
        ],
        compiler_params=pltpu.CompilerParams(vmem_limit_bytes=60 * MIB),
        cost_estimate=pl.CostEstimate(
            flops=tiles * per * (6 * rank * rank * size),
            bytes_accessed=2 * tiles * per * size * rank + 2 * size * rank * (tiles + 2 * per),
            transcendentals=0,
        ),
        name="main",
    )(meta, *operands)
    return update, gram


def solution(mesh):
    in_specs = (P("row", "col", None), P("row", "col", None), P("col", None), P())
    out_specs = (P("row", "col", None, None), P("row", "col", None, None))
    return jax.shard_map(local, mesh=mesh, in_specs=in_specs, out_specs=out_specs, check_vma=False)
```

time: 323 us -> 270 us (0.84)
  the two profiles are of different devices: /device:TPU:19 before, /device:TPU:0 now
where the time goes in v2:
time: 270 us
  waiting for transfers between devices  137 us (51%)
  starting transfers between devices  65.3 us (24%)
  Pallas kernels  44.1 us (16%)
  local copies, waits for them, and re-layouts  21.8 us (8%)
    ppermute x7, waiting for transfers between devices, local(): cw.append(lax.ppermute(cw[-1], 'col', ahead))  56.8 us
    pallas_call x1, Pallas kernels, local(): pl.pallas_call(functools.partial(main_kernel, cols, rows, tiles, per), ou...  35.7 us
    ppermute x7, waiting for transfers between devices, local(): inv_ccw.append(lax.ppermute(inv_ccw[-1], 'col', back))  30.7 us
    ppermute x7, waiting for transfers between devices, local(): ccw.append(lax.ppermute(ccw[-1], 'col', back))  23.1 us
    ppermute x7, waiting for transfers between devices, local(): inv_cw.append(lax.ppermute(inv_cw[-1], 'col', ahead))  17.9 us
    ppermute x7, starting transfers between devices, local(): cw.append(lax.ppermute(cw[-1], 'col', ahead))  16.7 us
    unnamed x51, local copies, waits for them, and re-layouts  15.4 us
    ppermute x7, starting transfers between devices, local(): inv_cw.append(lax.ppermute(inv_cw[-1], 'col', ahead))  15.1 us
  transfers between devices with their start and end apart: 40, of which 26 were waited for; matrix products, arithmetic and copies ran while one was open for 5% of the time, Pallas kernels for 3%

profile of v2, /device:TPU:0, one launch (start us, length us, event | category | flops | bytes accessed | tf_op | source)
XLA Modules:
  0.0 269.8 jit_solution(1732669125290990562)
XLA Ops:
  0.6 1.5 copy.11
  3.2 4.3 %all-to-all-start = ((bf16[1,4,4,128,256]{4,3,1,0,2:T(8,128)(2,1)}), bf16[1,4,4,128,256]{4,3,1,0,2:T(8,128)(2,1)}, u32[]{:S(2)}, u32[]{:S(2)}) async-start(bf16[1,4,4,128,256]{4,3,1,0,2:T(8,128)(2,1)} %copy.12), calls=%async_computation | async-start | bytes 2097152 | tf_op jit(solution)/shard_map/all_to_all | solution.py:184
  7.5 1.9 bitcast_dynamic-update-slice_fusion.7
  9.3 2.9 %collective-permute-start.1 = (bf16[64,2048]{1,0:T(8,128)(2,1)S(1)}, bf16[64,2048]{1,0:T(8,128)(2,1)S(1)}, u32[]{:S(2)}, u32[]{:S(2)}) collective-permute-start(bf16[64,2048]{1,0:T(8,128)(2,1)S(1)} %get-tuple-element.91), channel_id=1, source_target_pairs={{2,0},{4,2},{6,4},{7,6},{5,7},{3,5},{1,3},{0,1},{10,8},{12,10},{14... | collective-permute-start | bytes 786440 | tf_op jit(solution)/shard_map/ppermute | solution.py:237
  12.4 6.9 %collective-permute-done.1 = bf16[64,2048]{1,0:T(8,128)(2,1)S(1)} collective-permute-done((bf16[64,2048]{1,0:T(8,128)(2,1)S(1)}, bf16[64,2048]{1,0:T(8,128)(2,1)S(1)}, u32[]{:S(2)}, u32[]{:S(2)}) %collective-permute-start.1) | collective-permute-done | bytes 262176 | tf_op jit(solution)/shard_map/ppermute | solution.py:237
  19.3 1.4 collective-permute-done
  21.0 1.7 collective-permute-start.3
  23.4 4.9 %collective-permute-done.2 = bf16[64,2048]{1,0:T(8,128)(2,1)S(1)} collective-permute-done((bf16[64,2048]{1,0:T(8,128)(2,1)S(1)}, bf16[64,2048]{1,0:T(8,128)(2,1)S(1)}, u32[]{:S(2)}, u32[]{:S(2)}) %collective-permute-start.2) | collective-permute-done | bytes 262176 | tf_op jit(solution)/shard_map/ppermute | solution.py:236
  28.8 1.6 collective-permute-start.4
  31.7 4.6 %all-to-all-start.1 = ((bf16[8,2,128,256]{3,2,1,0:T(8,128)(2,1)}), bf16[8,2,128,256]{3,2,1,0:T(8,128)(2,1)S(1)}, u32[]{:S(2)}, u32[]{:S(2)}) async-start(bf16[8,2,128,256]{3,2,1,0:T(8,128)(2,1)} %bitcast.17), calls=%async_computation.1 | async-start | bytes 2097152 | tf_op jit(solution)/shard_map/all_to_all | solution.py:241
  36.4 2.0 collective-permute-start.5
  38.4 1.7 bitcast_dynamic-update-slice_fusion.5
  40.1 16.6 %collective-permute-done.5 = bf16[64,2048]{1,0:T(8,128)(2,1)S(1)} collective-permute-done((bf16[64,2048]{1,0:T(8,128)(2,1)}, bf16[64,2048]{1,0:T(8,128)(2,1)S(1)}, u32[]{:S(2)}, u32[]{:S(2)}) %collective-permute-start.5) | collective-permute-done | bytes 262176 | tf_op jit(solution)/shard_map/ppermute | solution.py:237
  56.7 10.0 %collective-permute-start.6 = (bf16[64,2048]{1,0:T(8,128)(2,1)}, bf16[64,2048]{1,0:T(8,128)(2,1)S(1)}, u32[]{:S(2)}, u32[]{:S(2)}) collective-permute-start(bf16[64,2048]{1,0:T(8,128)(2,1)} %collective-permute-done.4), channel_id=1, source_target_pairs={{0,2},{2,4},{4,6},{6,7},{7,5},{5,3},{3,1},{1,0},{8,10},{10,12},{12... | collective-permute-start | bytes 786440 | tf_op jit(solution)/shard_map/ppermute | solution.py:236
  66.7 1.7 bitcast_dynamic-update-slice_fusion.12
  69.1 1.8 collective-permute-done.6
  70.9 3.9 %collective-permute-done.7 = bf16[64,2048]{1,0:T(8,128)(2,1)S(1)} collective-permute-done((bf16[64,2048]{1,0:T(8,128)(2,1)S(1)}, bf16[64,2048]{1,0:T(8,128)(2,1)S(1)}, u32[]{:S(2)}, u32[]{:S(2)}) %collective-permute-start.7) | collective-permute-done | bytes 262176 | tf_op jit(solution)/shard_map/ppermute | solution.py:237
  75.5 2.0 collective-permute-start.9
  78.2 4.0 %collective-permute-done.8 = bf16[64,2048]{1,0:T(8,128)(2,1)S(1)} collective-permute-done((bf16[64,2048]{1,0:T(8,128)(2,1)S(1)}, bf16[64,2048]{1,0:T(8,128)(2,1)S(1)}, u32[]{:S(2)}, u32[]{:S(2)}) %collective-permute-start.8) | collective-permute-done | bytes 262176 | tf_op jit(solution)/shard_map/ppermute | solution.py:236
  82.3 1.4 collective-permute-start.10
  85.7 2.9 %collective-permute-done.10 = bf16[64,2048]{1,0:T(8,128)(2,1)S(1)} collective-permute-done((bf16[64,2048]{1,0:T(8,128)(2,1)S(1)}, bf16[64,2048]{1,0:T(8,128)(2,1)S(1)}, u32[]{:S(2)}, u32[]{:S(2)}) %collective-permute-start.10) | collective-permute-done | bytes 262176 | tf_op jit(solution)/shard_map/ppermute | solution.py:236
  88.6 1.4 collective-permute-done.11
  90.0 1.7 collective-permute-start.12
  93.5 2.9 %collective-permute-done.12 = bf16[64,2048]{1,0:T(8,128)(2,1)S(1)} collective-permute-done((bf16[64,2048]{1,0:T(8,128)(2,1)S(1)}, bf16[64,2048]{1,0:T(8,128)(2,1)S(1)}, u32[]{:S(2)}, u32[]{:S(2)}) %collective-permute-start.12) | collective-permute-done | bytes 262176 | tf_op jit(solution)/shard_map/ppermute | solution.py:236
  97.1 1.5 collective-permute-done.13
  98.6 1.8 bitcast_dynamic-update-slice_fusion.8.refs_0_
  102.5 2.0 collective-permute-start.14
  104.6 12.1 %collective-permute-done.15.refs_9_ = bf16[2,512,256]{2,1,0:T(8,128)(2,1)S(1)} collective-permute-done((bf16[2,512,256]{2,1,0:T(8,128)(2,1)S(1)}, bf16[2,512,256]{2,1,0:T(8,128)(2,1)S(1)}, u32[]{:S(2)}, u32[]{:S(2)}) %collective-permute-start.15) | collective-permute-done | bytes 524320 | tf_op jit(solution)/shard_map/ppermute | solution.py:255
  117.9 4.2 %all-to-all-start.2 = ((bf16[1,4,4,64,512]{4,3,1,0,2:T(8,128)(2,1)}), bf16[1,4,4,64,512]{4,3,1,0,2:T(8,128)(2,1)}, u32[]{:S(2)}, u32[]{:S(2)}) async-start(bf16[1,4,4,64,512]{4,3,1,0,2:T(8,128)(2,1)} %copy.13), calls=%async_computation.2 | async-start | bytes 2097152 | tf_op jit(solution)/shard_map/all_to_all | solution.py:184
  122.2 1.8 collective-permute-start.18
  124.2 12.2 %collective-permute-done.18.refs_2_ = bf16[2,512,256]{2,1,0:T(8,128)(2,1)S(1)} collective-permute-done((bf16[2,512,256]{2,1,0:T(8,128)(2,1)S(1)}, bf16[2,512,256]{2,1,0:T(8,128)(2,1)S(1)}, u32[]{:S(2)}, u32[]{:S(2)}) %collective-permute-start.18) | collective-permute-done | bytes 524320 | tf_op jit(solution)/shard_map/ppermute | solution.py:254
  136.5 1.5 collective-permute-done.19.refs_10_
  137.9 3.6 %all-to-all-start.3 = ((bf16[8,2,64,512]{3,2,1,0:T(8,128)(2,1)}), bf16[8,2,64,512]{3,2,1,0:T(8,128)(2,1)S(1)}, u32[]{:S(2)}, u32[]{:S(2)}) async-start(bf16[8,2,64,512]{3,2,1,0:T(8,128)(2,1)} %bitcast.37), calls=%async_computation.3 | async-start | bytes 2097152 | tf_op jit(solution)/shard_map/all_to_all | solution.py:265
  142.4 1.7 collective-permute-start.20
  144.4 8.4 %solve.1 = bf16[256,2048]{1,0:T(8,128)(2,1)} custom-call(s32[17]{0:T(128)} %stack.154.meta, bf16[8,2,128,256]{3,2,1,0:T(8,128)(2,1)} %copy-done, bf16[8,64,2048]{2,1,0:T(8,128)(2,1)} %bitcast_dynamic-update-slice_fusion.8.refs_0_, bf16[8,64,2048]{2,1,0:T(8,128)(2,1)} %bitcast_dynamic-update-slice_fusion.refs_1_, ...), custom_call_target="tpu_custom_call" | custom-call | flops 2147483648 | bytes 10485760 | tf_op jit(solution)/shard_map/solve/pallas_call | solution.py:209
  152.8 1.7 collective-permute-start.24
  154.5 14.9 %collective-permute-done.20.refs_3_ = bf16[2,512,256]{2,1,0:T(8,128)(2,1)S(1)} collective-permute-done((bf16[2,512,256]{2,1,0:T(8,128)(2,1)S(1)}, bf16[2,512,256]{2,1,0:T(8,128)(2,1)S(1)}, u32[]{:S(2)}, u32[]{:S(2)}) %collective-permute-start.20) | collective-permute-done | bytes 524320 | tf_op jit(solution)/shard_map/ppermute | solution.py:254
  169.5 2.3 collective-permute-done.21.refs_11_
  171.8 7.2 %collective-permute-start.22 = (bf16[2,512,256]{2,1,0:T(8,128)(2,1)S(1)}, bf16[2,512,256]{2,1,0:T(8,128)(2,1)}, u32[]{:S(2)}, u32[]{:S(2)}) collective-permute-start(bf16[2,512,256]{2,1,0:T(8,128)(2,1)S(1)} %collective-permute-done.20.refs_3_), channel_id=1, source_target_pairs={{0,2},{2,4},{4,6},{6,7},{7,5},{5,3},{3,1},{1,0},{8,10},{10,12},{12... | collective-permute-start | bytes 1572872 | tf_op jit(solution)/shard_map/ppermute | solution.py:254
  179.0 9.9 %collective-permute-done.22.refs_4_ = bf16[2,512,256]{2,1,0:T(8,128)(2,1)} collective-permute-done((bf16[2,512,256]{2,1,0:T(8,128)(2,1)S(1)}, bf16[2,512,256]{2,1,0:T(8,128)(2,1)}, u32[]{:S(2)}, u32[]{:S(2)}) %collective-permute-start.22) | collective-permute-done | bytes 524320 | tf_op jit(solution)/shard_map/ppermute | solution.py:254
  188.9 2.5 collective-permute-done.23.refs_12_
  191.4 1.4 collective-permute-start.25
  195.1 8.0 %collective-permute-done.25.refs_5_ = bf16[2,512,256]{2,1,0:T(8,128)(2,1)S(1)} collective-permute-done((bf16[2,512,256]{2,1,0:T(8,128)(2,1)}, bf16[2,512,256]{2,1,0:T(8,128)(2,1)S(1)}, u32[]{:S(2)}, u32[]{:S(2)}) %collective-permute-start.25) | collective-permute-done | bytes 524320 | tf_op jit(solution)/shard_map/ppermute | solution.py:254
  203.2 2.1 collective-permute-done.26.refs_13_
  207.3 9.0 %collective-permute-done.29.refs_21_ = bf16[8,2,64,512]{3,2,1,0:T(8,128)(2,1)S(1)} collective-permute-done((bf16[8,2,64,512]{3,2,1,0:T(8,128)(2,1)S(1)}, bf16[8,2,64,512]{3,2,1,0:T(8,128)(2,1)S(1)}, u32[]{:S(2)}, u32[]{:S(2)}) %collective-permute-start.29) | collective-permute-done | bytes 1048608 | tf_op jit(solution)/shard_map/ppermute | solution.py:40
  218.5 1.6 collective-permute-start.32
  221.4 11.4 %collective-permute-done.32.refs_7_ = bf16[2,512,256]{2,1,0:T(8,128)(2,1)} collective-permute-done((bf16[2,512,256]{2,1,0:T(8,128)(2,1)}, bf16[2,512,256]{2,1,0:T(8,128)(2,1)}, u32[]{:S(2)}, u32[]{:S(2)}) %collective-permute-start.32) | collective-permute-done | bytes 524320 | tf_op jit(solution)/shard_map/ppermute | solution.py:254
  234.1 35.7 %main.1 = (bf16[4,2,2048,512]{3,2,1,0:T(8,128)(2,1)}, bf16[4,2,512,512]{3,2,1,0:T(8,128)(2,1)}) custom-call(s32[26]{0:T(128)} %concatenate.3.meta, bf16[2,512,256]{2,1,0:T(8,128)(2,1)} %copy-done.5, bf16[2,512,256]{2,1,0:T(8,128)(2,1)} %copy-done.12, bf16[2,512,256]{2,1,0:T(8,128)(2,1)} %copy-done.13, bf16[2,512,256]{2,1,0:T(8,128)(2,1)} %copy-done.15, ...), custom_call_target="tpu_custom_call" | custom-call | flops 25769803776 | bytes 33554432 | tf_op jit(solution)/shard_map/main/pallas_call | solution.py:280
  (94 shorter events, 24.6 us)
Async XLA Ops:
  3.2 25.6 %all-to-all-start = ((bf16[1,4,4,128,256]{4,3,1,0,2:T(8,128)(2,1)}), bf16[1,4,4,128,256]{4,3,1,0,2:T(8,128)(2,1)}, u32[]{:S(2)}, u32[]{:S(2)}) async-start(bf16[1,4,4,128,256]{4,3,1,0,2:T(8,128)(2,1)} %copy.12), calls=%async_computation | async-start | bytes 2097152 | tf_op jit(solution)/shard_map/all_to_all | solution.py:184
  9.3 9.9 %collective-permute-start.1 = (bf16[64,2048]{1,0:T(8,128)(2,1)S(1)}, bf16[64,2048]{1,0:T(8,128)(2,1)S(1)}, u32[]{:S(2)}, u32[]{:S(2)}) collective-permute-start(bf16[64,2048]{1,0:T(8,128)(2,1)S(1)} %get-tuple-element.91), channel_id=1, source_target_pairs={{2,0},{4,2},{6,4},{7,6},{5,7},{3,5},{1,3},{0,1},{10,8},{12,10},{14... | collective-permute-start | bytes 786440 | tf_op jit(solution)/shard_map/ppermute | solution.py:237
  12.3 8.4 %collective-permute-start = (bf16[64,2048]{1,0:T(8,128)(2,1)S(1)}, bf16[64,2048]{1,0:T(8,128)(2,1)S(1)}, u32[]{:S(2)}, u32[]{:S(2)}) collective-permute-start(bf16[64,2048]{1,0:T(8,128)(2,1)S(1)} %get-tuple-element.97), channel_id=1, source_target_pairs={{0,2},{2,4},{4,6},{6,7},{7,5},{5,3},{3,1},{1,0},{8,10},{10,12},{12... | collective-permute-start | bytes 786440 | tf_op jit(solution)/shard_map/ppermute | solution.py:236
  20.7 7.7 %collective-permute-start.2 = (bf16[64,2048]{1,0:T(8,128)(2,1)S(1)}, bf16[64,2048]{1,0:T(8,128)(2,1)S(1)}, u32[]{:S(2)}, u32[]{:S(2)}) collective-permute-start(bf16[64,2048]{1,0:T(8,128)(2,1)S(1)} %collective-permute-done), channel_id=1, source_target_pairs={{0,2},{2,4},{4,6},{6,7},{7,5},{5,3},{3,1},{1,0},{8,10},{10,12},{12... | collective-permute-start | bytes 786440 | tf_op jit(solution)/shard_map/ppermute | solution.py:236
  21.0 7.8 %collective-permute-start.3 = (bf16[64,2048]{1,0:T(8,128)(2,1)S(1)}, bf16[64,2048]{1,0:T(8,128)(2,1)}, u32[]{:S(2)}, u32[]{:S(2)}) collective-permute-start(bf16[64,2048]{1,0:T(8,128)(2,1)S(1)} %collective-permute-done.1), channel_id=1, source_target_pairs={{2,0},{4,2},{6,4},{7,6},{5,7},{3,5},{1,3},{0,1},{10,8},{12,10},{14... | collective-permute-start | bytes 786440 | tf_op jit(solution)/shard_map/ppermute | solution.py:237
  28.8 11.3 %collective-permute-start.4 = (bf16[64,2048]{1,0:T(8,128)(2,1)S(1)}, bf16[64,2048]{1,0:T(8,128)(2,1)}, u32[]{:S(2)}, u32[]{:S(2)}) collective-permute-start(bf16[64,2048]{1,0:T(8,128)(2,1)S(1)} %collective-permute-done.2), channel_id=1, source_target_pairs={{0,2},{2,4},{4,6},{6,7},{7,5},{5,3},{3,1},{1,0},{8,10},{10,12},{12... | collective-permute-start | bytes 786440 | tf_op jit(solution)/shard_map/ppermute | solution.py:236
  31.7 66.8 %all-to-all-start.1 = ((bf16[8,2,128,256]{3,2,1,0:T(8,128)(2,1)}), bf16[8,2,128,256]{3,2,1,0:T(8,128)(2,1)S(1)}, u32[]{:S(2)}, u32[]{:S(2)}) async-start(bf16[8,2,128,256]{3,2,1,0:T(8,128)(2,1)} %bitcast.17), calls=%async_computation.1 | async-start | bytes 2097152 | tf_op jit(solution)/shard_map/all_to_all | solution.py:241
  36.4 20.3 %collective-permute-start.5 = (bf16[64,2048]{1,0:T(8,128)(2,1)}, bf16[64,2048]{1,0:T(8,128)(2,1)S(1)}, u32[]{:S(2)}, u32[]{:S(2)}) collective-permute-start(bf16[64,2048]{1,0:T(8,128)(2,1)} %collective-permute-done.3), channel_id=1, source_target_pairs={{2,0},{4,2},{6,4},{7,6},{5,7},{3,5},{1,3},{0,1},{10,8},{12,10},{14... | collective-permute-start | bytes 786440 | tf_op jit(solution)/shard_map/ppermute | solution.py:237
  56.7 14.2 %collective-permute-start.6 = (bf16[64,2048]{1,0:T(8,128)(2,1)}, bf16[64,2048]{1,0:T(8,128)(2,1)S(1)}, u32[]{:S(2)}, u32[]{:S(2)}) collective-permute-start(bf16[64,2048]{1,0:T(8,128)(2,1)} %collective-permute-done.4), channel_id=1, source_target_pairs={{0,2},{2,4},{4,6},{6,7},{7,5},{5,3},{3,1},{1,0},{8,10},{10,12},{12... | collective-permute-start | bytes 786440 | tf_op jit(solution)/shard_map/ppermute | solution.py:236
  68.4 6.4 %collective-permute-start.7 = (bf16[64,2048]{1,0:T(8,128)(2,1)S(1)}, bf16[64,2048]{1,0:T(8,128)(2,1)S(1)}, u32[]{:S(2)}, u32[]{:S(2)}) collective-permute-start(bf16[64,2048]{1,0:T(8,128)(2,1)S(1)} %collective-permute-done.5), channel_id=1, source_target_pairs={{2,0},{4,2},{6,4},{7,6},{5,7},{3,5},{1,3},{0,1},{10,8},{12,10},{14... | collective-permute-start | bytes 786440 | tf_op jit(solution)/shard_map/ppermute | solution.py:237
  74.8 7.5 %collective-permute-start.8 = (bf16[64,2048]{1,0:T(8,128)(2,1)S(1)}, bf16[64,2048]{1,0:T(8,128)(2,1)S(1)}, u32[]{:S(2)}, u32[]{:S(2)}) collective-permute-start(bf16[64,2048]{1,0:T(8,128)(2,1)S(1)} %collective-permute-done.6), channel_id=1, source_target_pairs={{0,2},{2,4},{4,6},{6,7},{7,5},{5,3},{3,1},{1,0},{8,10},{10,12},{12... | collective-permute-start | bytes 786440 | tf_op jit(solution)/shard_map/ppermute | solution.py:236
  75.5 6.8 %collective-permute-start.9 = (bf16[64,2048]{1,0:T(8,128)(2,1)S(1)}, bf16[64,2048]{1,0:T(8,128)(2,1)S(1)}, u32[]{:S(2)}, u32[]{:S(2)}) collective-permute-start(bf16[64,2048]{1,0:T(8,128)(2,1)S(1)} %collective-permute-done.7), channel_id=1, source_target_pairs={{2,0},{4,2},{6,4},{7,6},{5,7},{3,5},{1,3},{0,1},{10,8},{12,10},{14... | collective-permute-start | bytes 786440 | tf_op jit(solution)/shard_map/ppermute | solution.py:237
  82.3 6.4 %collective-permute-start.10 = (bf16[64,2048]{1,0:T(8,128)(2,1)S(1)}, bf16[64,2048]{1,0:T(8,128)(2,1)S(1)}, u32[]{:S(2)}, u32[]{:S(2)}) collective-permute-start(bf16[64,2048]{1,0:T(8,128)(2,1)S(1)} %collective-permute-done.8), channel_id=1, source_target_pairs={{0,2},{2,4},{4,6},{6,7},{7,5},{5,3},{3,1},{1,0},{8,10},{10,12},{12... | collective-permute-start | bytes 786440 | tf_op jit(solution)/shard_map/ppermute | solution.py:236
  83.6 6.4 %collective-permute-start.11 = (bf16[64,2048]{1,0:T(8,128)(2,1)S(1)}, bf16[64,2048]{1,0:T(8,128)(2,1)S(1)}, u32[]{:S(2)}, u32[]{:S(2)}) collective-permute-start(bf16[64,2048]{1,0:T(8,128)(2,1)S(1)} %collective-permute-done.9), channel_id=1, source_target_pairs={{2,0},{4,2},{6,4},{7,6},{5,7},{3,5},{1,3},{0,1},{10,8},{12,10},{14... | collective-permute-start | bytes 786440 | tf_op jit(solution)/shard_map/ppermute | solution.py:237
  85.7 31.0 %copy-start.2 = (bf16[4,256,512]{2,1,0:T(8,128)(2,1)S(1)}, bf16[4,256,512]{2,1,0:T(8,128)(2,1)}, u32[]{:S(2)}) copy-start(bf16[4,256,512]{2,1,0:T(8,128)(2,1)} %param.4) | copy-start | bytes 3145732
  90.0 6.4 %collective-permute-start.12 = (bf16[64,2048]{1,0:T(8,128)(2,1)S(1)}, bf16[64,2048]{1,0:T(8,128)(2,1)S(1)}, u32[]{:S(2)}, u32[]{:S(2)}) collective-permute-start(bf16[64,2048]{1,0:T(8,128)(2,1)S(1)} %collective-permute-done.10), channel_id=1, source_target_pairs={{0,2},{2,4},{4,6},{6,7},{7,5},{5,3},{3,1},{1,0},{8,10},{10,12},{12... | collective-permute-start | bytes 786440 | tf_op jit(solution)/shard_map/ppermute | solution.py:236
  91.7 6.8 %collective-permute-start.13 = (bf16[64,2048]{1,0:T(8,128)(2,1)S(1)}, bf16[64,2048]{1,0:T(8,128)(2,1)S(1)}, u32[]{:S(2)}, u32[]{:S(2)}) collective-permute-start(bf16[64,2048]{1,0:T(8,128)(2,1)S(1)} %collective-permute-done.11), channel_id=1, source_target_pairs={{2,0},{4,2},{6,4},{7,6},{5,7},{3,5},{1,3},{0,1},{10,8},{12,10},{14... | collective-permute-start | bytes 786440 | tf_op jit(solution)/shard_map/ppermute | solution.py:237
  98.6 19.3 %copy-start = (bf16[8,2,128,256]{3,2,1,0:T(8,128)(2,1)}, bf16[8,2,128,256]{3,2,1,0:T(8,128)(2,1)S(1)}, u32[]{:S(2)}) copy-start(bf16[8,2,128,256]{3,2,1,0:T(8,128)(2,1)S(1)} %all-to-all-done.1.cut) | copy-start | bytes 3145732
  100.4 16.3 %collective-permute-start.16 = (bf16[8,64,2048]{2,1,0:T(8,128)(2,1)}, bf16[8,64,2048]{2,1,0:T(8,128)(2,1)}, u32[]{:S(2)}, u32[]{:S(2)}) collective-permute-start(bf16[8,64,2048]{2,1,0:T(8,128)(2,1)} %bitcast_dynamic-update-slice_fusion.8.refs_0_), channel_id=1, source_target_pairs={{0,8},{8,0},{16,24},{24,16},{1,9},{9,1},{17,25},{25,17},{2,10},{10... | collective-permute-start | bytes 6291464 | tf_op jit(solution)/shard_map/ppermute | solution.py:45
  101.1 15.5 %collective-permute-start.17 = (bf16[8,64,2048]{2,1,0:T(8,128)(2,1)}, bf16[8,64,2048]{2,1,0:T(8,128)(2,1)}, u32[]{:S(2)}, u32[]{:S(2)}) collective-permute-start(bf16[8,64,2048]{2,1,0:T(8,128)(2,1)} %bitcast_dynamic-update-slice_fusion.refs_1_), channel_id=1, source_target_pairs={{0,8},{8,0},{16,24},{24,16},{1,9},{9,1},{17,25},{25,17},{2,10},{10... | collective-permute-start | bytes 6291464 | tf_op jit(solution)/shard_map/ppermute | solution.py:45
  102.5 14.1 %collective-permute-start.15 = (bf16[2,512,256]{2,1,0:T(8,128)(2,1)S(1)}, bf16[2,512,256]{2,1,0:T(8,128)(2,1)S(1)}, u32[]{:S(2)}, u32[]{:S(2)}) collective-permute-start(bf16[2,512,256]{2,1,0:T(8,128)(2,1)S(1)} %get-tuple-element.94.refs_8_), channel_id=1, source_target_pairs={{2,0},{4,2},{6,4},{7,6},{5,7},{3,5},{1,3},{0,1},{10,8},{12,10},{14... | collective-permute-start | bytes 1572872 | tf_op jit(solution)/shard_map/ppermute | solution.py:255
  102.5 14.1 %collective-permute-start.14 = (bf16[2,512,256]{2,1,0:T(8,128)(2,1)S(1)}, bf16[2,512,256]{2,1,0:T(8,128)(2,1)S(1)}, u32[]{:S(2)}, u32[]{:S(2)}) collective-permute-start(bf16[2,512,256]{2,1,0:T(8,128)(2,1)S(1)} %get-tuple-element.95.refs_0_), channel_id=1, source_target_pairs={{0,2},{2,4},{4,6},{6,7},{7,5},{5,3},{3,1},{1,0},{8,10},{10,12},{12... | collective-permute-start | bytes 1572872 | tf_op jit(solution)/shard_map/ppermute | solution.py:254
  117.9 20.0 %all-to-all-start.2 = ((bf16[1,4,4,64,512]{4,3,1,0,2:T(8,128)(2,1)}), bf16[1,4,4,64,512]{4,3,1,0,2:T(8,128)(2,1)}, u32[]{:S(2)}, u32[]{:S(2)}) async-start(bf16[1,4,4,64,512]{4,3,1,0,2:T(8,128)(2,1)} %copy.13), calls=%async_computation.2 | async-start | bytes 2097152 | tf_op jit(solution)/shard_map/all_to_all | solution.py:184
  122.2 14.3 %collective-permute-start.18 = (bf16[2,512,256]{2,1,0:T(8,128)(2,1)S(1)}, bf16[2,512,256]{2,1,0:T(8,128)(2,1)S(1)}, u32[]{:S(2)}, u32[]{:S(2)}) collective-permute-start(bf16[2,512,256]{2,1,0:T(8,128)(2,1)S(1)} %collective-permute-done.14.refs_1_), channel_id=1, source_target_pairs={{0,2},{2,4},{4,6},{6,7},{7,5},{5,3},{3,1},{1,0},{8,10},{10,12},{12... | collective-permute-start | bytes 1572872 | tf_op jit(solution)/shard_map/ppermute | solution.py:254
  124.0 14.0 %collective-permute-start.19 = (bf16[2,512,256]{2,1,0:T(8,128)(2,1)S(1)}, bf16[2,512,256]{2,1,0:T(8,128)(2,1)S(1)}, u32[]{:S(2)}, u32[]{:S(2)}) collective-permute-start(bf16[2,512,256]{2,1,0:T(8,128)(2,1)S(1)} %collective-permute-done.15.refs_9_), channel_id=1, source_target_pairs={{2,0},{4,2},{6,4},{7,6},{5,7},{3,5},{1,3},{0,1},{10,8},{12,10},{14... | collective-permute-start | bytes 1572872 | tf_op jit(solution)/shard_map/ppermute | solution.py:255
  136.5 16.3 %copy-start.13 = (bf16[2,512,256]{2,1,0:T(8,128)(2,1)}, bf16[2,512,256]{2,1,0:T(8,128)(2,1)S(1)}, u32[]{:S(2)}) copy-start(bf16[2,512,256]{2,1,0:T(8,128)(2,1)S(1)} %collective-permute-done.18.refs_2_) | copy-start | bytes 1572868
  137.9 53.5 %all-to-all-start.3 = ((bf16[8,2,64,512]{3,2,1,0:T(8,128)(2,1)}), bf16[8,2,64,512]{3,2,1,0:T(8,128)(2,1)S(1)}, u32[]{:S(2)}, u32[]{:S(2)}) async-start(bf16[8,2,64,512]{3,2,1,0:T(8,128)(2,1)} %bitcast.37), calls=%async_computation.3 | async-start | bytes 2097152 | tf_op jit(solution)/shard_map/all_to_all | solution.py:265
  142.4 78.2 %copy-start.18 = (s32[16]{0:T(128)S(1)}, s32[16]{0:T(128)}, u32[]{:S(2)}) copy-start(s32[16]{0:T(128)} %param.7) | copy-start | bytes 196
  142.4 27.1 %collective-permute-start.20 = (bf16[2,512,256]{2,1,0:T(8,128)(2,1)S(1)}, bf16[2,512,256]{2,1,0:T(8,128)(2,1)S(1)}, u32[]{:S(2)}, u32[]{:S(2)}) collective-permute-start(bf16[2,512,256]{2,1,0:T(8,128)(2,1)S(1)} %collective-permute-done.18.refs_2_), channel_id=1, source_target_pairs={{0,2},{2,4},{4,6},{6,7},{7,5},{5,3},{3,1},{1,0},{8,10},{10,12},{12... | collective-permute-start | bytes 1572872 | tf_op jit(solution)/shard_map/ppermute | solution.py:254
  144.1 27.7 %collective-permute-start.21 = (bf16[2,512,256]{2,1,0:T(8,128)(2,1)S(1)}, bf16[2,512,256]{2,1,0:T(8,128)(2,1)}, u32[]{:S(2)}, u32[]{:S(2)}) collective-permute-start(bf16[2,512,256]{2,1,0:T(8,128)(2,1)S(1)} %collective-permute-done.19.refs_10_), channel_id=1, source_target_pairs={{2,0},{4,2},{6,4},{7,6},{5,7},{3,5},{1,3},{0,1},{10,8},{12,10},{14... | collective-permute-start | bytes 1572872 | tf_op jit(solution)/shard_map/ppermute | solution.py:255
  152.8 26.2 %collective-permute-start.24 = (bf16[2,128,2048]{2,1,0:T(8,128)(2,1)}, bf16[2,128,2048]{2,1,0:T(8,128)(2,1)S(1)}, u32[]{:S(2)}, u32[]{:S(2)}) collective-permute-start(bf16[2,128,2048]{2,1,0:T(8,128)(2,1)} %bitcast.64), channel_id=1, source_target_pairs={{0,16},{8,24},{16,0},{24,8},{1,17},{9,25},{17,1},{25,9},{2,18},{10... | collective-permute-start | bytes 3145736 | tf_op jit(solution)/shard_map/ppermute | solution.py:40
  169.5 19.4 %copy-start.15 = (bf16[2,512,256]{2,1,0:T(8,128)(2,1)}, bf16[2,512,256]{2,1,0:T(8,128)(2,1)S(1)}, u32[]{:S(2)}) copy-start(bf16[2,512,256]{2,1,0:T(8,128)(2,1)S(1)} %collective-permute-done.20.refs_3_) | copy-start | bytes 1572868
  171.8 17.1 %collective-permute-start.22 = (bf16[2,512,256]{2,1,0:T(8,128)(2,1)S(1)}, bf16[2,512,256]{2,1,0:T(8,128)(2,1)}, u32[]{:S(2)}, u32[]{:S(2)}) collective-permute-start(bf16[2,512,256]{2,1,0:T(8,128)(2,1)S(1)} %collective-permute-done.20.refs_3_), channel_id=1, source_target_pairs={{0,2},{2,4},{4,6},{6,7},{7,5},{5,3},{3,1},{1,0},{8,10},{10,12},{12... | collective-permute-start | bytes 1572872 | tf_op jit(solution)/shard_map/ppermute | solution.py:254
  179.0 12.4 %collective-permute-start.23 = (bf16[2,512,256]{2,1,0:T(8,128)(2,1)}, bf16[2,512,256]{2,1,0:T(8,128)(2,1)}, u32[]{:S(2)}, u32[]{:S(2)}) collective-permute-start(bf16[2,512,256]{2,1,0:T(8,128)(2,1)} %collective-permute-done.21.refs_11_), channel_id=1, source_target_pairs={{2,0},{4,2},{6,4},{7,6},{5,7},{3,5},{1,3},{0,1},{10,8},{12,10},{14... | collective-permute-start | bytes 1572872 | tf_op jit(solution)/shard_map/ppermute | solution.py:255
  179.0 55.0 %copy-start.7 = (bf16[2,128,2048]{2,1,0:T(8,128)(2,1)}, bf16[2,128,2048]{2,1,0:T(8,128)(2,1)S(1)}, u32[]{:S(2)}) copy-start(bf16[2,128,2048]{2,1,0:T(8,128)(2,1)S(1)} %collective-permute-done.24.refs_17_) | copy-start | bytes 3145732
  191.4 42.6 %copy-start.3 = (bf16[8,2,64,512]{3,2,1,0:T(8,128)(2,1)}, bf16[8,2,64,512]{3,2,1,0:T(8,128)(2,1)S(1)}, u32[]{:S(2)}) copy-start(bf16[8,2,64,512]{3,2,1,0:T(8,128)(2,1)S(1)} %all-to-all-done.3.refs_20_) | copy-start | bytes 3145732
  191.4 11.7 %collective-permute-start.25 = (bf16[2,512,256]{2,1,0:T(8,128)(2,1)}, bf16[2,512,256]{2,1,0:T(8,128)(2,1)S(1)}, u32[]{:S(2)}, u32[]{:S(2)}) collective-permute-start(bf16[2,512,256]{2,1,0:T(8,128)(2,1)} %collective-permute-done.22.refs_4_), channel_id=1, source_target_pairs={{0,2},{2,4},{4,6},{6,7},{7,5},{5,3},{3,1},{1,0},{8,10},{10,12},{12... | collective-permute-start | bytes 1572872 | tf_op jit(solution)/shard_map/ppermute | solution.py:254
  192.8 12.4 %collective-permute-start.26 = (bf16[2,512,256]{2,1,0:T(8,128)(2,1)}, bf16[2,512,256]{2,1,0:T(8,128)(2,1)S(1)}, u32[]{:S(2)}, u32[]{:S(2)}) collective-permute-start(bf16[2,512,256]{2,1,0:T(8,128)(2,1)} %collective-permute-done.23.refs_12_), channel_id=1, source_target_pairs={{2,0},{4,2},{6,4},{7,6},{5,7},{3,5},{1,3},{0,1},{10,8},{12,10},{14... | collective-permute-start | bytes 1572872 | tf_op jit(solution)/shard_map/ppermute | solution.py:255
  193.5 22.8 %collective-permute-start.29 = (bf16[8,2,64,512]{3,2,1,0:T(8,128)(2,1)S(1)}, bf16[8,2,64,512]{3,2,1,0:T(8,128)(2,1)S(1)}, u32[]{:S(2)}, u32[]{:S(2)}) collective-permute-start(bf16[8,2,64,512]{3,2,1,0:T(8,128)(2,1)S(1)} %all-to-all-done.3.refs_20_), channel_id=1, source_target_pairs={{0,16},{8,24},{16,0},{24,8},{1,17},{9,25},{17,1},{25,9},{2,18},{10... | collective-permute-start | bytes 3145736 | tf_op jit(solution)/shard_map/ppermute | solution.py:40
  194.6 21.7 %collective-permute-start.30 = (bf16[2,128,2048]{2,1,0:T(8,128)(2,1)}, bf16[2,128,2048]{2,1,0:T(8,128)(2,1)S(1)}, u32[]{:S(2)}, u32[]{:S(2)}) collective-permute-start(bf16[2,128,2048]{2,1,0:T(8,128)(2,1)} %bitcast.65), channel_id=1, source_target_pairs={{0,8},{8,0},{16,24},{24,16},{1,9},{9,1},{17,25},{25,17},{2,10},{10... | collective-permute-start | bytes 3145736 | tf_op jit(solution)/shard_map/ppermute | solution.py:45
  194.6 21.7 %collective-permute-start.31 = (bf16[2,128,2048]{2,1,0:T(8,128)(2,1)S(1)}, bf16[2,128,2048]{2,1,0:T(8,128)(2,1)S(1)}, u32[]{:S(2)}, u32[]{:S(2)}) collective-permute-start(bf16[2,128,2048]{2,1,0:T(8,128)(2,1)S(1)} %collective-permute-done.24.refs_17_), channel_id=1, source_target_pairs={{0,8},{8,0},{16,24},{24,16},{1,9},{9,1},{17,25},{25,17},{2,10},{10... | collective-permute-start | bytes 3145736 | tf_op jit(solution)/shard_map/ppermute | solution.py:45
  205.3 11.4 %collective-permute-start.27 = (bf16[2,512,256]{2,1,0:T(8,128)(2,1)S(1)}, bf16[2,512,256]{2,1,0:T(8,128)(2,1)}, u32[]{:S(2)}, u32[]{:S(2)}) collective-permute-start(bf16[2,512,256]{2,1,0:T(8,128)(2,1)S(1)} %collective-permute-done.25.refs_5_), channel_id=1, source_target_pairs={{0,2},{2,4},{4,6},{6,7},{7,5},{5,3},{3,1},{1,0},{8,10},{10,12},{12... | collective-permute-start | bytes 1572872 | tf_op jit(solution)/shard_map/ppermute | solution.py:254
  206.2 11.8 %collective-permute-start.28 = (bf16[2,512,256]{2,1,0:T(8,128)(2,1)S(1)}, bf16[2,512,256]{2,1,0:T(8,128)(2,1)}, u32[]{:S(2)}, u32[]{:S(2)}) collective-permute-start(bf16[2,512,256]{2,1,0:T(8,128)(2,1)S(1)} %collective-permute-done.26.refs_13_), channel_id=1, source_target_pairs={{2,0},{4,2},{6,4},{7,6},{5,7},{3,5},{1,3},{0,1},{10,8},{12,10},{14... | collective-permute-start | bytes 1572872 | tf_op jit(solution)/shard_map/ppermute | solution.py:255
  216.3 17.8 %copy-start.8 = (bf16[8,2,64,512]{3,2,1,0:T(8,128)(2,1)}, bf16[8,2,64,512]{3,2,1,0:T(8,128)(2,1)S(1)}, u32[]{:S(2)}) copy-start(bf16[8,2,64,512]{3,2,1,0:T(8,128)(2,1)S(1)} %collective-permute-done.29.refs_21_) | copy-start | bytes 3145732
  218.0 16.1 %collective-permute-start.34 = (bf16[8,2,64,512]{3,2,1,0:T(8,128)(2,1)S(1)}, bf16[8,2,64,512]{3,2,1,0:T(8,128)(2,1)}, u32[]{:S(2)}, u32[]{:S(2)}) collective-permute-start(bf16[8,2,64,512]{3,2,1,0:T(8,128)(2,1)S(1)} %all-to-all-done.3.refs_20_), channel_id=1, source_target_pairs={{0,8},{8,0},{16,24},{24,16},{1,9},{9,1},{17,25},{25,17},{2,10},{10... | collective-permute-start | bytes 3145736 | tf_op jit(solution)/shard_map/ppermute | solution.py:45
  218.0 16.1 %collective-permute-start.35 = (bf16[8,2,64,512]{3,2,1,0:T(8,128)(2,1)S(1)}, bf16[8,2,64,512]{3,2,1,0:T(8,128)(2,1)}, u32[]{:S(2)}, u32[]{:S(2)}) collective-permute-start(bf16[8,2,64,512]{3,2,1,0:T(8,128)(2,1)S(1)} %collective-permute-done.29.refs_21_), channel_id=1, source_target_pairs={{0,8},{8,0},{16,24},{24,16},{1,9},{9,1},{17,25},{25,17},{2,10},{10... | collective-permute-start | bytes 3145736 | tf_op jit(solution)/shard_map/ppermute | solution.py:45
  218.5 14.2 %collective-permute-start.32 = (bf16[2,512,256]{2,1,0:T(8,128)(2,1)}, bf16[2,512,256]{2,1,0:T(8,128)(2,1)}, u32[]{:S(2)}, u32[]{:S(2)}) collective-permute-start(bf16[2,512,256]{2,1,0:T(8,128)(2,1)} %collective-permute-done.27.refs_6_), channel_id=1, source_target_pairs={{0,2},{2,4},{4,6},{6,7},{7,5},{5,3},{3,1},{1,0},{8,10},{10,12},{12... | collective-permute-start | bytes 1572872 | tf_op jit(solution)/shard_map/ppermute | solution.py:254
  220.1 13.9 %collective-permute-start.33 = (bf16[2,512,256]{2,1,0:T(8,128)(2,1)}, bf16[2,512,256]{2,1,0:T(8,128)(2,1)}, u32[]{:S(2)}, u32[]{:S(2)}) collective-permute-start(bf16[2,512,256]{2,1,0:T(8,128)(2,1)} %collective-permute-done.28.refs_14_), channel_id=1, source_target_pairs={{2,0},{4,2},{6,4},{7,6},{5,7},{3,5},{1,3},{0,1},{10,8},{12,10},{14... | collective-permute-start | bytes 1572872 | tf_op jit(solution)/shard_map/ppermute | solution.py:255
  (11 other events, 79.1 us)

commit v3 on v2

--- a/solution.py
+++ b/solution.py
@@ -59,8 +59,9 @@
 def solve_kernel(cols, meta, cut, *refs):
     it = iter(refs)
     inv = [next(it) for _ in range(4)]
-    out, right, whole, solved, rsem, isem = it
     per, share, width = cut.shape[1:]
+    out = [next(it) for _ in range(per)]
+    right, whole, solved, rsem, isem = it
     core = meta[0]
     pulls = []
     for s in range(cols):
@@ -82,34 +83,39 @@
         solved[:, b * BLOCK : end] = dot(right[:, :end], flat[b * BLOCK : end, :end], NT).astype(jnp.bfloat16)
     for b in range(size // BLOCK):
         start = b * BLOCK
-        out[:, start : start + BLOCK] = dot(
-            solved[:, start:], flat[start:, start : start + BLOCK], NN
-        ).astype(jnp.bfloat16)
+        value = dot(solved[:, start:], flat[start:, start : start + BLOCK], NN).astype(jnp.bfloat16)
+        for j in range(per):
+            out[j][:, start : start + BLOCK] = value[j * share : (j + 1) * share]
 
 
 def main_kernel(cols, rows, tiles, per, meta, *refs):
     it = iter(refs)
     cw = [next(it) for _ in range(cols)]
     ccw = [next(it) for _ in range(cols)]
-    ours = [next(it) for _ in range(rows)]
-    left = [next(it) for _ in range(rows)]
+    ours = [[next(it) for _ in range(rows)] for _ in range(per)]
+    left = [[next(it) for _ in range(rows)] for _ in range(2)]
     update, gram = next(it), next(it)
     right, turned, whole, upd, grm, rsem, tsem, lsem, osem = it
     half = tiles // 2
     size, width, rank = right.shape[2], right.shape[2] // cols, right.shape[1]
-    share = ours[0].shape[1]
+    share, some = ours[0][0].shape[0], left[0][0].shape[0]
     base = rows + 2 * cols
 
     def turned_copies():
         spots = [pl.multiple_of(meta[k] * share, share) for k in range(rows)]
         return [
-            pltpu.make_async_copy(ours[k], turned.at[:, pl.ds(spots[k], share), :], tsem.at[k]) for k in range(rows)
+            pltpu.make_async_copy(ours[j][k], turned.at[j, pl.ds(spots[k], share), :], tsem.at[j, k])
+            for j in range(per)
+            for k in range(rows)
         ]
 
     def left_copies():
         return [
-            pltpu.make_async_copy(left[k].at[:, j], whole.at[j, :, meta[k]], lsem.at[k, j])
+            pltpu.make_async_copy(
+                left[h][k].at[:, j], whole.at[j, h * some : (h + 1) * some, meta[k]], lsem.at[h, k, j]
+            )
             for j in range(per)
+            for h in range(2)
             for k in range(rows)
         ]
 
@@ -150,10 +156,6 @@
                 for copy in right_copies(tile):
                     copy.wait()
 
-        value = dot(right[i], turned[j], NT)
-        live = (row_at < meta[base + i]) & (col_at < meta[base + tiles + j])
-        value = jnp.where(live, value, 0.0).astype(jnp.bfloat16)
-
         @pl.when(at == 0)
         def _():
             for copy in left_copies():
@@ -164,12 +166,32 @@
             for copy in outs(i, j, slot):
                 copy.wait()
 
-        upd[slot] = dot(flat[j], value, NT).astype(jnp.bfloat16)
-        outs(i, j, slot)[0].start()
-        top = (dot(upd[slot, :, :cut], upd[slot], TN) / size).astype(jnp.bfloat16)
-        grm[slot, :cut] = top
-        grm[slot, cut:, :cut] = top[:, cut:].T
-        grm[slot, cut:, cut:] = (dot(upd[slot, :, cut:], upd[slot, :, cut:], TN) / size).astype(jnp.bfloat16)
+        def work(tall, wide):
+            value = dot(right[i, :tall], turned[j, :wide], NT)
+            live = (row_at[:tall, :wide] < meta[base + i]) & (col_at[:tall, :wide] < meta[base + tiles + j])
+            value = jnp.where(live, value, 0.0).astype(jnp.bfloat16)
+            upd[slot, :, :tall] = dot(flat[j, :, :wide], value, NT).astype(jnp.bfloat16)
+            if tall < rank:
+                upd[slot, :, tall:] = jnp.zeros((size, rank - tall), jnp.bfloat16)
+            outs(i, j, slot)[0].start()
+            top = (dot(upd[slot, :, :cut], upd[slot, :, :tall], TN) / size).astype(jnp.bfloat16)
+            grm[slot, :cut, :tall] = top
+            if tall < rank:
+                grm[slot, :cut, cut:] = jnp.zeros((cut, rank - cut), jnp.bfloat16)
+                grm[slot, cut:] = jnp.zeros((rank - cut, rank), jnp.bfloat16)
+            else:
+                grm[slot, cut:, :cut] = top[:, cut:].T
+                grm[slot, cut:, cut:] = (dot(upd[slot, :, cut:], upd[slot, :, cut:], TN) / size).astype(jnp.bfloat16)
+
+        for tall in (cut, rank):
+            for wide in (cut, rank):
+                low = meta[base + i] <= cut if tall == cut else meta[base + i] > cut
+                thin = meta[base + tiles + j] <= cut if wide == cut else meta[base + tiles + j] > cut
+
+                @pl.when(jnp.logical_and(low, thin))
+                def _(tall=tall, wide=wide):
+                    work(tall, wide)
+
         outs(i, j, slot)[1].start()
         return carry
 
@@ -208,9 +230,9 @@
     def solve(cut, inv):
         return pl.pallas_call(
             functools.partial(solve_kernel, cols),
-            out_shape=jax.ShapeDtypeStruct((per * share, size), jnp.bfloat16),
+            out_shape=[jax.ShapeDtypeStruct((share, size), jnp.bfloat16)] * per,
             in_specs=[smem] + [anywhere] * 5,
-            out_specs=vmem,
+            out_specs=[vmem] * per,
             scratch_shapes=[
                 pltpu.VMEM((per * share, size), jnp.bfloat16),
                 pltpu.VMEM((cols, 2, 2, slab // 4, size), jnp.bfloat16),
@@ -223,7 +245,7 @@
                 flops=2 * per * share * size * size, bytes_accessed=2 * size * (size + 2 * per * share), transcendentals=0
             ),
             name="solve",
-        )(jnp.stack([my_row % 2] + cw_from + ccw_from).astype(jnp.int32), cut, *inv).reshape(per, share, size)
+        )(jnp.stack([my_row % 2] + cw_from + ccw_from).astype(jnp.int32), cut, *inv)
 
     cut = to_column(turned.reshape(tiles, rows, share, slab))
     ring = ring_of(cols)
@@ -231,16 +253,20 @@
     back = [(b, a) for a, b in ahead]
     part = slab // 2
     mine = lax.dynamic_slice_in_dim(inverse, (my_row % 2) * part, part, 0)
+    left = pan_left
     inv_cw, inv_ccw = [mine[: part // 2]], [mine[part // 2 :]]
     for step in range(1, cols):
         inv_cw.append(lax.ppermute(inv_cw[-1], "col", ahead))
         inv_ccw.append(lax.ppermute(inv_ccw[-1], "col", back))
         held = (inv_cw[-1], inv_ccw[-1])
         if step == max(1, round((cols - 1) * 2 / 7)):
-            held, cut = lax.optimization_barrier((held, cut))
+            held, cut, left = lax.optimization_barrier((held, cut, left))
+            left = to_column(left.reshape(tiles, rows, piece, rank))
+        elif step == max(1, round((cols - 1) * 4 / 7)):
+            held, cut, left = lax.optimization_barrier((held, cut, left))
             cut = lax.all_to_all(cut, "col", 0, 0, tiled=True)
         elif step == cols - 1:
-            held, cut, turned = lax.optimization_barrier((held, cut, turned))
+            held, turned = lax.optimization_barrier((held, turned))
         else:
             held = lax.optimization_barrier(held)
         inv_cw[-1], inv_ccw[-1] = held
@@ -249,7 +275,6 @@
     cw, ccw = [turned[:half]], [turned[half:]]
     last = cols - 1
     marks = [max(1, round(last * m / 7)) for m in range(8)]
-    left = pan_left
     for step in range(1, cols):
         cw.append(lax.ppermute(cw[-1], "col", ahead))
         ccw.append(lax.ppermute(ccw[-1], "col", back))
@@ -257,26 +282,34 @@
             break
         held = (cw[-1], ccw[-1])
         if step == marks[1]:
-            held, inv, left = lax.optimization_barrier((held, inv, left))
-            ours = gather_y(solve(cut, inv), rows)
-            left = to_column(left.reshape(tiles, rows, piece, rank))
+            held, inv, left, cut = lax.optimization_barrier((held, inv, left, cut))
+            solved = solve(cut, inv)
+            left = lax.all_to_all(left, "col", 0, 0, tiled=True)
         elif step == marks[2]:
-            held, left = lax.optimization_barrier((held, left))
-            left = lax.all_to_all(left, "col", 0, 0, tiled=True)
+            held, solved = lax.optimization_barrier((held, solved))
+            first = [gather_y(part, rows) for part in solved[: per // 2]]
+        elif step == marks[3]:
+            held, left, first = lax.optimization_barrier((held, left, first))
+            second = [gather_y(part, rows) for part in solved[per // 2 :]]
         elif step == marks[4]:
-            held, left, ours = lax.optimization_barrier((held, left, ours))
-            left = gather_y(left, rows)
-            ours = ours + swap_cores(ours, rows)
+            held, second = lax.optimization_barrier((held, second))
+            left = [left[: cols // 2], left[cols // 2 :]]
+            left[0] = gather_y(left[0], rows)
+            ours = [part + swap_cores(part, rows) for part in first]
+        elif step == marks[5]:
+            held, left[0], ours = lax.optimization_barrier((held, left[0], ours))
+            left[1] = gather_y(left[1], rows)
+            ours = ours + [part + swap_cores(part, rows) for part in second]
         elif step == marks[6]:
             held, left, ours = lax.optimization_barrier((held, left, ours))
-            left = left + swap_cores(left, rows)
+            left = [part + swap_cores(part, rows) for part in left]
         else:
             held = lax.optimization_barrier(held)
         cw[-1], ccw[-1] = held
     my_ranks = lax.dynamic_slice_in_dim(rank_list, my_row * tiles, tiles, 0)
     their_ranks = lax.dynamic_slice_in_dim(rank_list, my_col * per, per, 0)
     meta = jnp.concatenate([jnp.stack(ids + cw_from + ccw_from).astype(jnp.int32), my_ranks, their_ranks])
-    operands = cw + ccw + ours + left
+    operands = cw + ccw + [a for group in ours + left for a in group]
     update, gram = pl.pallas_call(
         functools.partial(main_kernel, cols, rows, tiles, per),
         out_shape=(
@@ -292,8 +325,8 @@
             pltpu.VMEM((2, size, rank), jnp.bfloat16),
             pltpu.VMEM((2, rank, rank), jnp.bfloat16),
             pltpu.SemaphoreType.DMA((tiles, cols)),
-            pltpu.SemaphoreType.DMA((rows,)),
-            pltpu.SemaphoreType.DMA((rows, per)),
+            pltpu.SemaphoreType.DMA((per, rows)),
+            pltpu.SemaphoreType.DMA((2, rows, per)),
             pltpu.SemaphoreType.DMA((2, 2)),
         ],
         compiler_params=pltpu.CompilerParams(vmem_limit_bytes=60 * MIB),

time: 270 us -> 264 us (0.978)
  waiting for transfers between devices: 137 us -> 145 us
  local copies, waits for them, and re-layouts: 21.8 us -> 16.7 us
  Pallas kernels: 44.1 us -> 40.6 us
  starting transfers between devices: 65.3 us -> 61.8 us
    ppermute x7, waiting for transfers between devices: 30.7 us -> 14.7 us  [local(): inv_ccw.append(lax.ppermute(inv_ccw[-1], 'col', back))]
    ppermute x7, waiting for transfers between devices: 23.1 us -> 35.7 us  [local(): ccw.append(lax.ppermute(ccw[-1], 'col', back))]
    ppermute x2 -> x4, waiting for transfers between devices: 9 us -> 18.2 us  [gather_y(): lax.ppermute(piece, 'row', [(i, (i + 2 * step) % rows) for i in range(row...]
    ppermute x7, waiting for transfers between devices: 56.8 us -> 48.9 us  [local(): cw.append(lax.ppermute(cw[-1], 'col', ahead))]
    ppermute x7, starting transfers between devices: 15.1 us -> 8.26 us  [local(): inv_cw.append(lax.ppermute(inv_cw[-1], 'col', ahead))]
    all_to_all x1, starting transfers between devices: 3.56 us -> 9.34 us  [local(): left = lax.all_to_all(left, 'col', 0, 0, tiled=True)]
    ppermute x7, waiting for transfers between devices: 17.9 us -> 21.8 us  [local(): inv_cw.append(lax.ppermute(inv_cw[-1], 'col', ahead))]
    unnamed x51 -> x63, local copies, waits for them, and re-layouts: 15.4 us -> 11.5 us
  transfers between devices with their start and end apart: 40 -> 46, of which waited for: 26 -> 29; matrix products, arithmetic and copies ran while one was open for 5% -> 5% of each run, Pallas kernels for 3% -> 3%
where the time goes in v3:
time: 264 us; the launch traced here: 265 us
  waiting for transfers between devices  145 us (55%)
  starting transfers between devices  61.8 us (23%)
  Pallas kernels  40.6 us (15%)
  local copies, waits for them, and re-layouts  16.7 us (6%)
    ppermute x7, waiting for transfers between devices, local(): cw.append(lax.ppermute(cw[-1], 'col', ahead))  48.9 us
    ppermute x7, waiting for transfers between devices, local(): ccw.append(lax.ppermute(ccw[-1], 'col', back))  35.7 us
    pallas_call x1, Pallas kernels, local(): pl.pallas_call(functools.partial(main_kernel, cols, rows, tiles, per), ou...  32.2 us
    ppermute x7, waiting for transfers between devices, local(): inv_cw.append(lax.ppermute(inv_cw[-1], 'col', ahead))  21.8 us
    ppermute x4, waiting for transfers between devices, gather_y(): lax.ppermute(piece, 'row', [(i, (i + 2 * step) % rows) for i in range(row...  18.2 us
    ppermute x7, waiting for transfers between devices, local(): inv_ccw.append(lax.ppermute(inv_ccw[-1], 'col', back))  14.7 us
    ppermute x7, starting transfers between devices, local(): cw.append(lax.ppermute(cw[-1], 'col', ahead))  13.7 us
    unnamed x63, local copies, waits for them, and re-layouts  11.5 us
  transfers between devices with their start and end apart: 46, of which 29 were waited for; matrix products, arithmetic and copies ran while one was open for 5% of the time, Pallas kernels for 3%

profile of v3, /device:TPU:0, one launch (start us, length us, event | category | flops | bytes accessed | tf_op | source)
XLA Modules:
  0.0 265.0 jit_solution(9259306444793810863)
XLA Ops:
  0.6 1.5 copy.11
  3.2 4.2 %all-to-all-start = ((bf16[1,4,4,128,256]{4,3,1,0,2:T(8,128)(2,1)}), bf16[1,4,4,128,256]{4,3,1,0,2:T(8,128)(2,1)}, u32[]{:S(2)}, u32[]{:S(2)}) async-start(bf16[1,4,4,128,256]{4,3,1,0,2:T(8,128)(2,1)} %copy.12), calls=%async_computation | async-start | bytes 2097152 | tf_op jit(solution)/shard_map/all_to_all | solution.py:206
  8.4 2.9 %collective-permute-start.1 = (bf16[64,2048]{1,0:T(8,128)(2,1)S(1)}, bf16[64,2048]{1,0:T(8,128)(2,1)S(1)}, u32[]{:S(2)}, u32[]{:S(2)}) collective-permute-start(bf16[64,2048]{1,0:T(8,128)(2,1)S(1)} %get-tuple-element.131), channel_id=1, source_target_pairs={{2,0},{4,2},{6,4},{7,6},{5,7},{3,5},{1,3},{0,1},{10,8},{12,10},{14... | collective-permute-start | bytes 786440 | tf_op jit(solution)/shard_map/ppermute | solution.py:260
  11.5 6.9 %collective-permute-done.1 = bf16[64,2048]{1,0:T(8,128)(2,1)S(1)} collective-permute-done((bf16[64,2048]{1,0:T(8,128)(2,1)S(1)}, bf16[64,2048]{1,0:T(8,128)(2,1)S(1)}, u32[]{:S(2)}, u32[]{:S(2)}) %collective-permute-start.1) | collective-permute-done | bytes 262176 | tf_op jit(solution)/shard_map/ppermute | solution.py:260
  18.3 1.4 collective-permute-done
  20.1 1.7 collective-permute-start.3
  22.6 4.8 %collective-permute-done.2 = bf16[64,2048]{1,0:T(8,128)(2,1)S(1)} collective-permute-done((bf16[64,2048]{1,0:T(8,128)(2,1)S(1)}, bf16[64,2048]{1,0:T(8,128)(2,1)S(1)}, u32[]{:S(2)}, u32[]{:S(2)}) %collective-permute-start.2) | collective-permute-done | bytes 262176 | tf_op jit(solution)/shard_map/ppermute | solution.py:259
  27.7 1.6 collective-permute-start.4
  31.5 4.3 %all-to-all-start.1 = ((bf16[1,4,4,64,512]{4,3,1,0,2:T(8,128)(2,1)}), bf16[1,4,4,64,512]{4,3,1,0,2:T(8,128)(2,1)}, u32[]{:S(2)}, u32[]{:S(2)}) async-start(bf16[1,4,4,64,512]{4,3,1,0,2:T(8,128)(2,1)} %copy.13), calls=%async_computation.1 | async-start | bytes 2097152 | tf_op jit(solution)/shard_map/all_to_all | solution.py:206
  36.5 1.6 collective-permute-start.6
  40.0 5.2 %collective-permute-done.6 = bf16[64,2048]{1,0:T(8,128)(2,1)S(1)} collective-permute-done((bf16[64,2048]{1,0:T(8,128)(2,1)S(1)}, bf16[64,2048]{1,0:T(8,128)(2,1)S(1)}, u32[]{:S(2)}, u32[]{:S(2)}) %collective-permute-start.6) | collective-permute-done | bytes 262176 | tf_op jit(solution)/shard_map/ppermute | solution.py:259
  45.2 1.3 collective-permute-done.7
  46.5 3.8 %all-to-all-done.1 = bf16[1,4,4,64,512]{4,3,1,0,2:T(8,128)(2,1)} async-done(((bf16[1,4,4,64,512]{4,3,1,0,2:T(8,128)(2,1)}), bf16[1,4,4,64,512]{4,3,1,0,2:T(8,128)(2,1)}, u32[]{:S(2)}, u32[]{:S(2)}) %all-to-all-start.1) | async-done | bytes 1048608 | tf_op jit(solution)/shard_map/all_to_all | solution.py:206
  50.3 1.6 collective-permute-start.8
  53.8 4.4 %collective-permute-done.8 = bf16[64,2048]{1,0:T(8,128)(2,1)S(1)} collective-permute-done((bf16[64,2048]{1,0:T(8,128)(2,1)S(1)}, bf16[64,2048]{1,0:T(8,128)(2,1)S(1)}, u32[]{:S(2)}, u32[]{:S(2)}) %collective-permute-start.8) | collective-permute-done | bytes 262176 | tf_op jit(solution)/shard_map/ppermute | solution.py:259
  58.2 2.0 collective-permute-done.9
  60.2 1.6 collective-permute-start.10
  63.6 3.2 %collective-permute-done.10 = bf16[64,2048]{1,0:T(8,128)(2,1)S(1)} collective-permute-done((bf16[64,2048]{1,0:T(8,128)(2,1)S(1)}, bf16[64,2048]{1,0:T(8,128)(2,1)S(1)}, u32[]{:S(2)}, u32[]{:S(2)}) %collective-permute-start.10) | collective-permute-done | bytes 262176 | tf_op jit(solution)/shard_map/ppermute | solution.py:259
  66.8 2.0 collective-permute-done.11
  68.8 1.5 collective-permute-start.12
  72.3 2.9 %collective-permute-done.12 = bf16[64,2048]{1,0:T(8,128)(2,1)S(1)} collective-permute-done((bf16[64,2048]{1,0:T(8,128)(2,1)S(1)}, bf16[64,2048]{1,0:T(8,128)(2,1)S(1)}, u32[]{:S(2)}, u32[]{:S(2)}) %collective-permute-start.12) | collective-permute-done | bytes 262176 | tf_op jit(solution)/shard_map/ppermute | solution.py:259
  75.2 2.2 collective-permute-done.13
  79.4 3.6 %all-to-all-start.2 = ((bf16[8,2,128,256]{3,2,1,0:T(8,128)(2,1)}), bf16[8,2,128,256]{3,2,1,0:T(8,128)(2,1)S(1)}, u32[]{:S(2)}, u32[]{:S(2)}) async-start(bf16[8,2,128,256]{3,2,1,0:T(8,128)(2,1)} %bitcast.17), calls=%async_computation.2 | async-start | bytes 2097152 | tf_op jit(solution)/shard_map/all_to_all | solution.py:267
  83.0 2.0 collective-permute-start.15
  85.1 28.7 %collective-permute-done.15.refs_9_ = bf16[2,512,256]{2,1,0:T(8,128)(2,1)S(1)} collective-permute-done((bf16[2,512,256]{2,1,0:T(8,128)(2,1)S(1)}, bf16[2,512,256]{2,1,0:T(8,128)(2,1)S(1)}, u32[]{:S(2)}, u32[]{:S(2)}) %collective-permute-start.15) | collective-permute-done | bytes 524320 | tf_op jit(solution)/shard_map/ppermute | solution.py:280
  114.8 9.3 %all-to-all-start.3 = ((bf16[8,2,64,512]{3,2,1,0:T(8,128)(2,1)}), bf16[8,2,64,512]{3,2,1,0:T(8,128)(2,1)S(1)}, u32[]{:S(2)}, u32[]{:S(2)}) async-start(bf16[8,2,64,512]{3,2,1,0:T(8,128)(2,1)} %bitcast.21), calls=%async_computation.3 | async-start | bytes 2097152 | tf_op jit(solution)/shard_map/all_to_all | solution.py:287
  124.1 2.0 collective-permute-start.18
  126.9 8.3 %solve.1 = (bf16[128,2048]{1,0:T(8,128)(2,1)}, bf16[128,2048]{1,0:T(8,128)(2,1)}) custom-call(s32[17]{0:T(128)} %stack.154.meta, bf16[8,2,128,256]{3,2,1,0:T(8,128)(2,1)} %copy-done, bf16[8,64,2048]{2,1,0:T(8,128)(2,1)} %bitcast_dynamic-update-slice_fusion.8.refs_0_, bf16[8,64,2048]{2,1,0:T(8,128)(2,1)} %bitcast_dynamic-update-slice_fusion.refs_1_, ...), custom_call_target="tpu_custom_call" | custom-call | flops 2147483648 | bytes 10485760 | tf_op jit(solution)/shard_map/solve/pallas_call | solution.py:231
  135.2 17.9 %collective-permute-done.18.refs_2_ = bf16[2,512,256]{2,1,0:T(8,128)(2,1)} collective-permute-done((bf16[2,512,256]{2,1,0:T(8,128)(2,1)}, bf16[2,512,256]{2,1,0:T(8,128)(2,1)}, u32[]{:S(2)}, u32[]{:S(2)}) %collective-permute-start.18) | collective-permute-done | bytes 524320 | tf_op jit(solution)/shard_map/ppermute | solution.py:279
  153.2 1.7 collective-permute-done.19.refs_10_
  154.9 7.1 %collective-permute-start.20 = (bf16[2,512,256]{2,1,0:T(8,128)(2,1)}, bf16[2,512,256]{2,1,0:T(8,128)(2,1)}, u32[]{:S(2)}, u32[]{:S(2)}) collective-permute-start(bf16[2,512,256]{2,1,0:T(8,128)(2,1)} %collective-permute-done.18.refs_2_), channel_id=1, source_target_pairs={{0,2},{2,4},{4,6},{6,7},{7,5},{5,3},{3,1},{1,0},{8,10},{10,12},{12... | collective-permute-start | bytes 1572872 | tf_op jit(solution)/shard_map/ppermute | solution.py:279
  162.9 1.1 collective-permute-start.25
  164.1 8.5 %collective-permute-done.20.refs_3_ = bf16[2,512,256]{2,1,0:T(8,128)(2,1)} collective-permute-done((bf16[2,512,256]{2,1,0:T(8,128)(2,1)}, bf16[2,512,256]{2,1,0:T(8,128)(2,1)}, u32[]{:S(2)}, u32[]{:S(2)}) %collective-permute-start.20) | collective-permute-done | bytes 524320 | tf_op jit(solution)/shard_map/ppermute | solution.py:279
  172.6 2.3 collective-permute-done.21.refs_11_
  174.9 2.2 collective-permute-done.22.refs_17_
  177.1 2.0 collective-permute-start.23
  180.5 7.9 %collective-permute-done.25.refs_21_ = bf16[128,2048]{1,0:T(8,128)(2,1)} collective-permute-done((bf16[128,2048]{1,0:T(8,128)(2,1)}, bf16[128,2048]{1,0:T(8,128)(2,1)}, u32[]{:S(2)}, u32[]{:S(2)}) %collective-permute-start.25) | collective-permute-done | bytes 524320 | tf_op jit(solution)/shard_map/ppermute | solution.py:40
  189.3 1.4 collective-permute-start.26
  191.3 5.8 %collective-permute-done.28.refs_25_ = bf16[4,2,64,512]{3,2,1,0:T(8,128)(2,1)S(1)} collective-permute-done((bf16[4,2,64,512]{3,2,1,0:T(8,128)(2,1)S(1)}, bf16[4,2,64,512]{3,2,1,0:T(8,128)(2,1)S(1)}, u32[]{:S(2)}, u32[]{:S(2)}) %collective-permute-start.28) | collective-permute-done | bytes 524320 | tf_op jit(solution)/shard_map/ppermute | solution.py:40
  198.7 4.2 %collective-permute-done.26.refs_5_ = bf16[2,512,256]{2,1,0:T(8,128)(2,1)S(1)} collective-permute-done((bf16[2,512,256]{2,1,0:T(8,128)(2,1)S(1)}, bf16[2,512,256]{2,1,0:T(8,128)(2,1)S(1)}, u32[]{:S(2)}, u32[]{:S(2)}) %collective-permute-start.26) | collective-permute-done | bytes 524320 | tf_op jit(solution)/shard_map/ppermute | solution.py:279
  202.9 1.7 collective-permute-done.27.refs_13_
  205.3 1.3 collective-permute-start.32
  206.6 2.2 collective-permute-done.33.refs_29_
  208.8 9.0 %collective-permute-done.31.refs_6_ = bf16[2,512,256]{2,1,0:T(8,128)(2,1)S(1)} collective-permute-done((bf16[2,512,256]{2,1,0:T(8,128)(2,1)S(1)}, bf16[2,512,256]{2,1,0:T(8,128)(2,1)S(1)}, u32[]{:S(2)}, u32[]{:S(2)}) %collective-permute-start.31) | collective-permute-done | bytes 524320 | tf_op jit(solution)/shard_map/ppermute | solution.py:279
  218.6 1.7 collective-permute-start.37
  220.9 9.3 %collective-permute-done.36.refs_7_ = bf16[2,512,256]{2,1,0:T(8,128)(2,1)S(1)} collective-permute-done((bf16[2,512,256]{2,1,0:T(8,128)(2,1)S(1)}, bf16[2,512,256]{2,1,0:T(8,128)(2,1)S(1)}, u32[]{:S(2)}, u32[]{:S(2)}) %collective-permute-start.36) | collective-permute-done | bytes 524320 | tf_op jit(solution)/shard_map/ppermute | solution.py:279
  231.2 1.4 collective-permute-done.41.refs_31_
  232.6 32.2 %main.1 = (bf16[4,2,2048,512]{3,2,1,0:T(8,128)(2,1)}, bf16[4,2,512,512]{3,2,1,0:T(8,128)(2,1)}) custom-call(s32[26]{0:T(128)} %concatenate.3.meta, bf16[2,512,256]{2,1,0:T(8,128)(2,1)} %copy-done.3, bf16[2,512,256]{2,1,0:T(8,128)(2,1)} %copy-done.8, bf16[2,512,256]{2,1,0:T(8,128)(2,1)} %collective-permute-done.18.refs_2_, ...), custom_call_target="tpu_custom_call" | custom-call | flops 25769803776 | bytes 33554432 | tf_op jit(solution)/shard_map/main/pallas_call | solution.py:313
  (119 shorter events, 26.3 us)
Async XLA Ops:
  3.2 24.5 %all-to-all-start = ((bf16[1,4,4,128,256]{4,3,1,0,2:T(8,128)(2,1)}), bf16[1,4,4,128,256]{4,3,1,0,2:T(8,128)(2,1)}, u32[]{:S(2)}, u32[]{:S(2)}) async-start(bf16[1,4,4,128,256]{4,3,1,0,2:T(8,128)(2,1)} %copy.12), calls=%async_computation | async-start | bytes 2097152 | tf_op jit(solution)/shard_map/all_to_all | solution.py:206
  8.4 9.9 %collective-permute-start.1 = (bf16[64,2048]{1,0:T(8,128)(2,1)S(1)}, bf16[64,2048]{1,0:T(8,128)(2,1)S(1)}, u32[]{:S(2)}, u32[]{:S(2)}) collective-permute-start(bf16[64,2048]{1,0:T(8,128)(2,1)S(1)} %get-tuple-element.131), channel_id=1, source_target_pairs={{2,0},{4,2},{6,4},{7,6},{5,7},{3,5},{1,3},{0,1},{10,8},{12,10},{14... | collective-permute-start | bytes 786440 | tf_op jit(solution)/shard_map/ppermute | solution.py:260
  11.4 8.4 %collective-permute-start = (bf16[64,2048]{1,0:T(8,128)(2,1)S(1)}, bf16[64,2048]{1,0:T(8,128)(2,1)S(1)}, u32[]{:S(2)}, u32[]{:S(2)}) collective-permute-start(bf16[64,2048]{1,0:T(8,128)(2,1)S(1)} %get-tuple-element.139), channel_id=1, source_target_pairs={{0,2},{2,4},{4,6},{6,7},{7,5},{5,3},{3,1},{1,0},{8,10},{10,12},{12... | collective-permute-start | bytes 786440 | tf_op jit(solution)/shard_map/ppermute | solution.py:259
  19.7 7.6 %collective-permute-start.2 = (bf16[64,2048]{1,0:T(8,128)(2,1)S(1)}, bf16[64,2048]{1,0:T(8,128)(2,1)S(1)}, u32[]{:S(2)}, u32[]{:S(2)}) collective-permute-start(bf16[64,2048]{1,0:T(8,128)(2,1)S(1)} %collective-permute-done), channel_id=1, source_target_pairs={{0,2},{2,4},{4,6},{6,7},{7,5},{5,3},{3,1},{1,0},{8,10},{10,12},{12... | collective-permute-start | bytes 786440 | tf_op jit(solution)/shard_map/ppermute | solution.py:259
  20.1 7.6 %collective-permute-start.3 = (bf16[64,2048]{1,0:T(8,128)(2,1)S(1)}, bf16[64,2048]{1,0:T(8,128)(2,1)S(1)}, u32[]{:S(2)}, u32[]{:S(2)}) collective-permute-start(bf16[64,2048]{1,0:T(8,128)(2,1)S(1)} %collective-permute-done.1), channel_id=1, source_target_pairs={{2,0},{4,2},{6,4},{7,6},{5,7},{3,5},{1,3},{0,1},{10,8},{12,10},{14... | collective-permute-start | bytes 786440 | tf_op jit(solution)/shard_map/ppermute | solution.py:260
  27.7 8.8 %collective-permute-start.4 = (bf16[64,2048]{1,0:T(8,128)(2,1)S(1)}, bf16[64,2048]{1,0:T(8,128)(2,1)S(1)}, u32[]{:S(2)}, u32[]{:S(2)}) collective-permute-start(bf16[64,2048]{1,0:T(8,128)(2,1)S(1)} %collective-permute-done.2), channel_id=1, source_target_pairs={{0,2},{2,4},{4,6},{6,7},{7,5},{5,3},{3,1},{1,0},{8,10},{10,12},{12... | collective-permute-start | bytes 786440 | tf_op jit(solution)/shard_map/ppermute | solution.py:259
  30.0 6.5 %collective-permute-start.5 = (bf16[64,2048]{1,0:T(8,128)(2,1)S(1)}, bf16[64,2048]{1,0:T(8,128)(2,1)S(1)}, u32[]{:S(2)}, u32[]{:S(2)}) collective-permute-start(bf16[64,2048]{1,0:T(8,128)(2,1)S(1)} %collective-permute-done.3), channel_id=1, source_target_pairs={{2,0},{4,2},{6,4},{7,6},{5,7},{3,5},{1,3},{0,1},{10,8},{12,10},{14... | collective-permute-start | bytes 786440 | tf_op jit(solution)/shard_map/ppermute | solution.py:260
  31.5 18.8 %all-to-all-start.1 = ((bf16[1,4,4,64,512]{4,3,1,0,2:T(8,128)(2,1)}), bf16[1,4,4,64,512]{4,3,1,0,2:T(8,128)(2,1)}, u32[]{:S(2)}, u32[]{:S(2)}) async-start(bf16[1,4,4,64,512]{4,3,1,0,2:T(8,128)(2,1)} %copy.13), calls=%async_computation.1 | async-start | bytes 2097152 | tf_op jit(solution)/shard_map/all_to_all | solution.py:206
  36.5 8.7 %collective-permute-start.6 = (bf16[64,2048]{1,0:T(8,128)(2,1)S(1)}, bf16[64,2048]{1,0:T(8,128)(2,1)S(1)}, u32[]{:S(2)}, u32[]{:S(2)}) collective-permute-start(bf16[64,2048]{1,0:T(8,128)(2,1)S(1)} %collective-permute-done.4), channel_id=1, source_target_pairs={{0,2},{2,4},{4,6},{6,7},{7,5},{5,3},{3,1},{1,0},{8,10},{10,12},{12... | collective-permute-start | bytes 786440 | tf_op jit(solution)/shard_map/ppermute | solution.py:259
  38.1 8.4 %collective-permute-start.7 = (bf16[64,2048]{1,0:T(8,128)(2,1)S(1)}, bf16[64,2048]{1,0:T(8,128)(2,1)S(1)}, u32[]{:S(2)}, u32[]{:S(2)}) collective-permute-start(bf16[64,2048]{1,0:T(8,128)(2,1)S(1)} %collective-permute-done.5), channel_id=1, source_target_pairs={{2,0},{4,2},{6,4},{7,6},{5,7},{3,5},{1,3},{0,1},{10,8},{12,10},{14... | collective-permute-start | bytes 786440 | tf_op jit(solution)/shard_map/ppermute | solution.py:260
  50.3 7.8 %collective-permute-start.8 = (bf16[64,2048]{1,0:T(8,128)(2,1)S(1)}, bf16[64,2048]{1,0:T(8,128)(2,1)S(1)}, u32[]{:S(2)}, u32[]{:S(2)}) collective-permute-start(bf16[64,2048]{1,0:T(8,128)(2,1)S(1)} %collective-permute-done.6), channel_id=1, source_target_pairs={{0,2},{2,4},{4,6},{6,7},{7,5},{5,3},{3,1},{1,0},{8,10},{10,12},{12... | collective-permute-start | bytes 786440 | tf_op jit(solution)/shard_map/ppermute | solution.py:259
  52.6 7.6 %collective-permute-start.9 = (bf16[64,2048]{1,0:T(8,128)(2,1)S(1)}, bf16[64,2048]{1,0:T(8,128)(2,1)S(1)}, u32[]{:S(2)}, u32[]{:S(2)}) collective-permute-start(bf16[64,2048]{1,0:T(8,128)(2,1)S(1)} %collective-permute-done.7), channel_id=1, source_target_pairs={{2,0},{4,2},{6,4},{7,6},{5,7},{3,5},{1,3},{0,1},{10,8},{12,10},{14... | collective-permute-start | bytes 786440 | tf_op jit(solution)/shard_map/ppermute | solution.py:260
  60.2 6.6 %collective-permute-start.10 = (bf16[64,2048]{1,0:T(8,128)(2,1)S(1)}, bf16[64,2048]{1,0:T(8,128)(2,1)S(1)}, u32[]{:S(2)}, u32[]{:S(2)}) collective-permute-start(bf16[64,2048]{1,0:T(8,128)(2,1)S(1)} %collective-permute-done.8), channel_id=1, source_target_pairs={{0,2},{2,4},{4,6},{6,7},{7,5},{5,3},{3,1},{1,0},{8,10},{10,12},{12... | collective-permute-start | bytes 786440 | tf_op jit(solution)/shard_map/ppermute | solution.py:259
  62.5 6.4 %collective-permute-start.11 = (bf16[64,2048]{1,0:T(8,128)(2,1)S(1)}, bf16[64,2048]{1,0:T(8,128)(2,1)S(1)}, u32[]{:S(2)}, u32[]{:S(2)}) collective-permute-start(bf16[64,2048]{1,0:T(8,128)(2,1)S(1)} %collective-permute-done.9), channel_id=1, source_target_pairs={{2,0},{4,2},{6,4},{7,6},{5,7},{3,5},{1,3},{0,1},{10,8},{12,10},{14... | collective-permute-start | bytes 786440 | tf_op jit(solution)/shard_map/ppermute | solution.py:260
  68.8 6.4 %collective-permute-start.12 = (bf16[64,2048]{1,0:T(8,128)(2,1)S(1)}, bf16[64,2048]{1,0:T(8,128)(2,1)S(1)}, u32[]{:S(2)}, u32[]{:S(2)}) collective-permute-start(bf16[64,2048]{1,0:T(8,128)(2,1)S(1)} %collective-permute-done.10), channel_id=1, source_target_pairs={{0,2},{2,4},{4,6},{6,7},{7,5},{5,3},{3,1},{1,0},{8,10},{10,12},{12... | collective-permute-start | bytes 786440 | tf_op jit(solution)/shard_map/ppermute | solution.py:259
  71.1 6.4 %collective-permute-start.13 = (bf16[64,2048]{1,0:T(8,128)(2,1)S(1)}, bf16[64,2048]{1,0:T(8,128)(2,1)S(1)}, u32[]{:S(2)}, u32[]{:S(2)}) collective-permute-start(bf16[64,2048]{1,0:T(8,128)(2,1)S(1)} %collective-permute-done.11), channel_id=1, source_target_pairs={{2,0},{4,2},{6,4},{7,6},{5,7},{3,5},{1,3},{0,1},{10,8},{12,10},{14... | collective-permute-start | bytes 786440 | tf_op jit(solution)/shard_map/ppermute | solution.py:260
  78.1 35.7 %collective-permute-start.16 = (bf16[8,64,2048]{2,1,0:T(8,128)(2,1)}, bf16[8,64,2048]{2,1,0:T(8,128)(2,1)}, u32[]{:S(2)}, u32[]{:S(2)}) collective-permute-start(bf16[8,64,2048]{2,1,0:T(8,128)(2,1)} %bitcast_dynamic-update-slice_fusion.8.refs_0_), channel_id=1, source_target_pairs={{0,8},{8,0},{16,24},{24,16},{1,9},{9,1},{17,25},{25,17},{2,10},{10... | collective-permute-start | bytes 6291464 | tf_op jit(solution)/shard_map/ppermute | solution.py:45
  78.9 34.9 %collective-permute-start.17 = (bf16[8,64,2048]{2,1,0:T(8,128)(2,1)}, bf16[8,64,2048]{2,1,0:T(8,128)(2,1)}, u32[]{:S(2)}, u32[]{:S(2)}) collective-permute-start(bf16[8,64,2048]{2,1,0:T(8,128)(2,1)} %bitcast_dynamic-update-slice_fusion.refs_1_), channel_id=1, source_target_pairs={{0,8},{8,0},{16,24},{24,16},{1,9},{9,1},{17,25},{25,17},{2,10},{10... | collective-permute-start | bytes 6291464 | tf_op jit(solution)/shard_map/ppermute | solution.py:45
  79.4 34.4 %all-to-all-start.2 = ((bf16[8,2,128,256]{3,2,1,0:T(8,128)(2,1)}), bf16[8,2,128,256]{3,2,1,0:T(8,128)(2,1)S(1)}, u32[]{:S(2)}, u32[]{:S(2)}) async-start(bf16[8,2,128,256]{3,2,1,0:T(8,128)(2,1)} %bitcast.17), calls=%async_computation.2 | async-start | bytes 2097152 | tf_op jit(solution)/shard_map/all_to_all | solution.py:267
  83.0 30.7 %collective-permute-start.15 = (bf16[2,512,256]{2,1,0:T(8,128)(2,1)S(1)}, bf16[2,512,256]{2,1,0:T(8,128)(2,1)S(1)}, u32[]{:S(2)}, u32[]{:S(2)}) collective-permute-start(bf16[2,512,256]{2,1,0:T(8,128)(2,1)S(1)} %get-tuple-element.136.refs_8_), channel_id=1, source_target_pairs={{2,0},{4,2},{6,4},{7,6},{5,7},{3,5},{1,3},{0,1},{10,8},{12,10},{14... | collective-permute-start | bytes 1572872 | tf_op jit(solution)/shard_map/ppermute | solution.py:280
  85.0 28.8 %collective-permute-start.14 = (bf16[2,512,256]{2,1,0:T(8,128)(2,1)S(1)}, bf16[2,512,256]{2,1,0:T(8,128)(2,1)S(1)}, u32[]{:S(2)}, u32[]{:S(2)}) collective-permute-start(bf16[2,512,256]{2,1,0:T(8,128)(2,1)S(1)} %get-tuple-element.137.refs_0_), channel_id=1, source_target_pairs={{0,2},{2,4},{4,6},{6,7},{7,5},{5,3},{3,1},{1,0},{8,10},{10,12},{12... | collective-permute-start | bytes 1572872 | tf_op jit(solution)/shard_map/ppermute | solution.py:279
  114.8 62.3 %all-to-all-start.3 = ((bf16[8,2,64,512]{3,2,1,0:T(8,128)(2,1)}), bf16[8,2,64,512]{3,2,1,0:T(8,128)(2,1)S(1)}, u32[]{:S(2)}, u32[]{:S(2)}) async-start(bf16[8,2,64,512]{3,2,1,0:T(8,128)(2,1)} %bitcast.21), calls=%async_computation.3 | async-start | bytes 2097152 | tf_op jit(solution)/shard_map/all_to_all | solution.py:287
  124.1 29.1 %collective-permute-start.18 = (bf16[2,512,256]{2,1,0:T(8,128)(2,1)}, bf16[2,512,256]{2,1,0:T(8,128)(2,1)}, u32[]{:S(2)}, u32[]{:S(2)}) collective-permute-start(bf16[2,512,256]{2,1,0:T(8,128)(2,1)} %copy-done.8), channel_id=1, source_target_pairs={{0,2},{2,4},{4,6},{6,7},{7,5},{5,3},{3,1},{1,0},{8,10},{10,12},{12... | collective-permute-start | bytes 1572872 | tf_op jit(solution)/shard_map/ppermute | solution.py:279
  126.2 28.8 %collective-permute-start.19 = (bf16[2,512,256]{2,1,0:T(8,128)(2,1)}, bf16[2,512,256]{2,1,0:T(8,128)(2,1)}, u32[]{:S(2)}, u32[]{:S(2)}) collective-permute-start(bf16[2,512,256]{2,1,0:T(8,128)(2,1)} %copy-done.7), channel_id=1, source_target_pairs={{2,0},{4,2},{6,4},{7,6},{5,7},{3,5},{1,3},{0,1},{10,8},{12,10},{14... | collective-permute-start | bytes 1572872 | tf_op jit(solution)/shard_map/ppermute | solution.py:280
  135.2 95.1 %copy-start.24 = (s32[16]{0:T(128)S(1)}, s32[16]{0:T(128)}, u32[]{:S(2)}) copy-start(s32[16]{0:T(128)} %param.7) | copy-start | bytes 196
  154.9 17.7 %collective-permute-start.20 = (bf16[2,512,256]{2,1,0:T(8,128)(2,1)}, bf16[2,512,256]{2,1,0:T(8,128)(2,1)}, u32[]{:S(2)}, u32[]{:S(2)}) collective-permute-start(bf16[2,512,256]{2,1,0:T(8,128)(2,1)} %collective-permute-done.18.refs_2_), channel_id=1, source_target_pairs={{0,2},{2,4},{4,6},{6,7},{7,5},{5,3},{3,1},{1,0},{8,10},{10,12},{12... | collective-permute-start | bytes 1572872 | tf_op jit(solution)/shard_map/ppermute | solution.py:279
  162.0 12.8 %collective-permute-start.21 = (bf16[2,512,256]{2,1,0:T(8,128)(2,1)}, bf16[2,512,256]{2,1,0:T(8,128)(2,1)}, u32[]{:S(2)}, u32[]{:S(2)}) collective-permute-start(bf16[2,512,256]{2,1,0:T(8,128)(2,1)} %collective-permute-done.19.refs_10_), channel_id=1, source_target_pairs={{2,0},{4,2},{6,4},{7,6},{5,7},{3,5},{1,3},{0,1},{10,8},{12,10},{14... | collective-permute-start | bytes 1572872 | tf_op jit(solution)/shard_map/ppermute | solution.py:280
  162.0 15.1 %collective-permute-start.22 = (bf16[128,2048]{1,0:T(8,128)(2,1)}, bf16[128,2048]{1,0:T(8,128)(2,1)S(1)}, u32[]{:S(2)}, u32[]{:S(2)}) collective-permute-start(bf16[128,2048]{1,0:T(8,128)(2,1)} %get-tuple-element.118.refs_16_), channel_id=1, source_target_pairs={{0,16},{8,24},{16,0},{24,8},{1,17},{9,25},{17,1},{25,9},{2,18},{10... | collective-permute-start | bytes 1572872 | tf_op jit(solution)/shard_map/ppermute | solution.py:40
  162.9 25.5 %collective-permute-start.25 = (bf16[128,2048]{1,0:T(8,128)(2,1)}, bf16[128,2048]{1,0:T(8,128)(2,1)}, u32[]{:S(2)}, u32[]{:S(2)}) collective-permute-start(bf16[128,2048]{1,0:T(8,128)(2,1)} %get-tuple-element.122.refs_20_), channel_id=1, source_target_pairs={{0,16},{8,24},{16,0},{24,8},{1,17},{9,25},{17,1},{25,9},{2,18},{10... | collective-permute-start | bytes 1572872 | tf_op jit(solution)/shard_map/ppermute | solution.py:40
  177.1 11.3 %collective-permute-start.23 = (bf16[2,512,256]{2,1,0:T(8,128)(2,1)}, bf16[2,512,256]{2,1,0:T(8,128)(2,1)S(1)}, u32[]{:S(2)}, u32[]{:S(2)}) collective-permute-start(bf16[2,512,256]{2,1,0:T(8,128)(2,1)} %collective-permute-done.20.refs_3_), channel_id=1, source_target_pairs={{0,2},{2,4},{4,6},{6,7},{7,5},{5,3},{3,1},{1,0},{8,10},{10,12},{12... | collective-permute-start | bytes 1572872 | tf_op jit(solution)/shard_map/ppermute | solution.py:279
  179.1 10.1 %collective-permute-start.24 = (bf16[2,512,256]{2,1,0:T(8,128)(2,1)}, bf16[2,512,256]{2,1,0:T(8,128)(2,1)S(1)}, u32[]{:S(2)}, u32[]{:S(2)}) collective-permute-start(bf16[2,512,256]{2,1,0:T(8,128)(2,1)} %collective-permute-done.21.refs_11_), channel_id=1, source_target_pairs={{2,0},{4,2},{6,4},{7,6},{5,7},{3,5},{1,3},{0,1},{10,8},{12,10},{14... | collective-permute-start | bytes 1572872 | tf_op jit(solution)/shard_map/ppermute | solution.py:280
  179.5 53.0 %copy-start.4 = (bf16[4,2,64,512]{3,2,1,0:T(8,128)(2,1)}, bf16[4,2,64,512]{3,2,1,0:T(8,128)(2,1)S(1)}, u32[]{:S(2)}) copy-start(bf16[4,2,64,512]{3,2,1,0:T(8,128)(2,1)S(1)} %get-tuple-element.128.refs_28_) | copy-start | bytes 1572868
  179.5 17.6 %collective-permute-start.28 = (bf16[4,2,64,512]{3,2,1,0:T(8,128)(2,1)S(1)}, bf16[4,2,64,512]{3,2,1,0:T(8,128)(2,1)S(1)}, u32[]{:S(2)}, u32[]{:S(2)}) collective-permute-start(bf16[4,2,64,512]{3,2,1,0:T(8,128)(2,1)S(1)} %get-tuple-element.126.refs_24_), channel_id=1, source_target_pairs={{0,16},{8,24},{16,0},{24,8},{1,17},{9,25},{17,1},{25,9},{2,18},{10... | collective-permute-start | bytes 1572872 | tf_op jit(solution)/shard_map/ppermute | solution.py:40
  180.5 17.6 %collective-permute-start.29 = (bf16[128,2048]{1,0:T(8,128)(2,1)S(1)}, bf16[128,2048]{1,0:T(8,128)(2,1)S(1)}, u32[]{:S(2)}, u32[]{:S(2)}) collective-permute-start(bf16[128,2048]{1,0:T(8,128)(2,1)S(1)} %copy-done.9), channel_id=1, source_target_pairs={{0,8},{8,0},{16,24},{24,16},{1,9},{9,1},{17,25},{25,17},{2,10},{10... | collective-permute-start | bytes 1572872 | tf_op jit(solution)/shard_map/ppermute | solution.py:45
  188.5 9.7 %collective-permute-start.30 = (bf16[128,2048]{1,0:T(8,128)(2,1)S(1)}, bf16[128,2048]{1,0:T(8,128)(2,1)S(1)}, u32[]{:S(2)}, u32[]{:S(2)}) collective-permute-start(bf16[128,2048]{1,0:T(8,128)(2,1)S(1)} %copy-done.12), channel_id=1, source_target_pairs={{0,8},{8,0},{16,24},{24,16},{1,9},{9,1},{17,25},{25,17},{2,10},{10... | collective-permute-start | bytes 1572872 | tf_op jit(solution)/shard_map/ppermute | solution.py:45
  189.3 13.6 %collective-permute-start.26 = (bf16[2,512,256]{2,1,0:T(8,128)(2,1)S(1)}, bf16[2,512,256]{2,1,0:T(8,128)(2,1)S(1)}, u32[]{:S(2)}, u32[]{:S(2)}) collective-permute-start(bf16[2,512,256]{2,1,0:T(8,128)(2,1)S(1)} %collective-permute-done.23.refs_4_), channel_id=1, source_target_pairs={{0,2},{2,4},{4,6},{6,7},{7,5},{5,3},{3,1},{1,0},{8,10},{10,12},{12... | collective-permute-start | bytes 1572872 | tf_op jit(solution)/shard_map/ppermute | solution.py:279
  190.7 13.9 %collective-permute-start.27 = (bf16[2,512,256]{2,1,0:T(8,128)(2,1)S(1)}, bf16[2,512,256]{2,1,0:T(8,128)(2,1)S(1)}, u32[]{:S(2)}, u32[]{:S(2)}) collective-permute-start(bf16[2,512,256]{2,1,0:T(8,128)(2,1)S(1)} %collective-permute-done.24.refs_12_), channel_id=1, source_target_pairs={{2,0},{4,2},{6,4},{7,6},{5,7},{3,5},{1,3},{0,1},{10,8},{12,10},{14... | collective-permute-start | bytes 1572872 | tf_op jit(solution)/shard_map/ppermute | solution.py:280
  197.2 11.6 %collective-permute-start.33 = (bf16[4,2,64,512]{3,2,1,0:T(8,128)(2,1)S(1)}, bf16[4,2,64,512]{3,2,1,0:T(8,128)(2,1)}, u32[]{:S(2)}, u32[]{:S(2)}) collective-permute-start(bf16[4,2,64,512]{3,2,1,0:T(8,128)(2,1)S(1)} %get-tuple-element.128.refs_28_), channel_id=1, source_target_pairs={{0,16},{8,24},{16,0},{24,8},{1,17},{9,25},{17,1},{25,9},{2,18},{10... | collective-permute-start | bytes 1572872 | tf_op jit(solution)/shard_map/ppermute | solution.py:40
  198.1 10.7 %collective-permute-start.34 = (bf16[128,2048]{1,0:T(8,128)(2,1)S(1)}, bf16[128,2048]{1,0:T(8,128)(2,1)S(1)}, u32[]{:S(2)}, u32[]{:S(2)}) collective-permute-start(bf16[128,2048]{1,0:T(8,128)(2,1)S(1)} %copy-done.10), channel_id=1, source_target_pairs={{0,8},{8,0},{16,24},{24,16},{1,9},{9,1},{17,25},{25,17},{2,10},{10... | collective-permute-start | bytes 1572872 | tf_op jit(solution)/shard_map/ppermute | solution.py:45
  198.2 10.6 %collective-permute-start.35 = (bf16[128,2048]{1,0:T(8,128)(2,1)}, bf16[128,2048]{1,0:T(8,128)(2,1)S(1)}, u32[]{:S(2)}, u32[]{:S(2)}) collective-permute-start(bf16[128,2048]{1,0:T(8,128)(2,1)} %collective-permute-done.25.refs_21_), channel_id=1, source_target_pairs={{0,8},{8,0},{16,24},{24,16},{1,9},{9,1},{17,25},{25,17},{2,10},{10... | collective-permute-start | bytes 1572872 | tf_op jit(solution)/shard_map/ppermute | solution.py:45
  204.6 13.2 %collective-permute-start.31 = (bf16[2,512,256]{2,1,0:T(8,128)(2,1)S(1)}, bf16[2,512,256]{2,1,0:T(8,128)(2,1)S(1)}, u32[]{:S(2)}, u32[]{:S(2)}) collective-permute-start(bf16[2,512,256]{2,1,0:T(8,128)(2,1)S(1)} %collective-permute-done.26.refs_5_), channel_id=1, source_target_pairs={{0,2},{2,4},{4,6},{6,7},{7,5},{5,3},{3,1},{1,0},{8,10},{10,12},{12... | collective-permute-start | bytes 1572872 | tf_op jit(solution)/shard_map/ppermute | solution.py:279
  205.3 13.0 %collective-permute-start.32 = (bf16[2,512,256]{2,1,0:T(8,128)(2,1)S(1)}, bf16[2,512,256]{2,1,0:T(8,128)(2,1)}, u32[]{:S(2)}, u32[]{:S(2)}) collective-permute-start(bf16[2,512,256]{2,1,0:T(8,128)(2,1)S(1)} %collective-permute-done.27.refs_13_), channel_id=1, source_target_pairs={{2,0},{4,2},{6,4},{7,6},{5,7},{3,5},{1,3},{0,1},{10,8},{12,10},{14... | collective-permute-start | bytes 1572872 | tf_op jit(solution)/shard_map/ppermute | solution.py:280
  218.3 11.9 %collective-permute-start.36 = (bf16[2,512,256]{2,1,0:T(8,128)(2,1)S(1)}, bf16[2,512,256]{2,1,0:T(8,128)(2,1)S(1)}, u32[]{:S(2)}, u32[]{:S(2)}) collective-permute-start(bf16[2,512,256]{2,1,0:T(8,128)(2,1)S(1)} %collective-permute-done.31.refs_6_), channel_id=1, source_target_pairs={{0,2},{2,4},{4,6},{6,7},{7,5},{5,3},{3,1},{1,0},{8,10},{10,12},{12... | collective-permute-start | bytes 1572872 | tf_op jit(solution)/shard_map/ppermute | solution.py:279
  218.6 12.6 %collective-permute-start.37 = (bf16[2,512,256]{2,1,0:T(8,128)(2,1)}, bf16[2,512,256]{2,1,0:T(8,128)(2,1)}, u32[]{:S(2)}, u32[]{:S(2)}) collective-permute-start(bf16[2,512,256]{2,1,0:T(8,128)(2,1)} %collective-permute-done.32.refs_14_), channel_id=1, source_target_pairs={{2,0},{4,2},{6,4},{7,6},{5,7},{3,5},{1,3},{0,1},{10,8},{12,10},{14... | collective-permute-start | bytes 1572872 | tf_op jit(solution)/shard_map/ppermute | solution.py:280
  220.3 10.9 %collective-permute-start.38 = (bf16[4,2,64,512]{3,2,1,0:T(8,128)(2,1)S(1)}, bf16[4,2,64,512]{3,2,1,0:T(8,128)(2,1)}, u32[]{:S(2)}, u32[]{:S(2)}) collective-permute-start(bf16[4,2,64,512]{3,2,1,0:T(8,128)(2,1)S(1)} %get-tuple-element.126.refs_24_), channel_id=1, source_target_pairs={{0,8},{8,0},{16,24},{24,16},{1,9},{9,1},{17,25},{25,17},{2,10},{10... | collective-permute-start | bytes 1572872 | tf_op jit(solution)/shard_map/ppermute | solution.py:45
  220.3 10.9 %collective-permute-start.39 = (bf16[4,2,64,512]{3,2,1,0:T(8,128)(2,1)S(1)}, bf16[4,2,64,512]{3,2,1,0:T(8,128)(2,1)}, u32[]{:S(2)}, u32[]{:S(2)}) collective-permute-start(bf16[4,2,64,512]{3,2,1,0:T(8,128)(2,1)S(1)} %collective-permute-done.28.refs_25_), channel_id=1, source_target_pairs={{0,8},{8,0},{16,24},{24,16},{1,9},{9,1},{17,25},{25,17},{2,10},{10... | collective-permute-start | bytes 1572872 | tf_op jit(solution)/shard_map/ppermute | solution.py:45
  220.8 10.4 %collective-permute-start.40 = (bf16[4,2,64,512]{3,2,1,0:T(8,128)(2,1)S(1)}, bf16[4,2,64,512]{3,2,1,0:T(8,128)(2,1)}, u32[]{:S(2)}, u32[]{:S(2)}) collective-permute-start(bf16[4,2,64,512]{3,2,1,0:T(8,128)(2,1)S(1)} %get-tuple-element.128.refs_28_), channel_id=1, source_target_pairs={{0,8},{8,0},{16,24},{24,16},{1,9},{9,1},{17,25},{25,17},{2,10},{10... | collective-permute-start | bytes 1572872 | tf_op jit(solution)/shard_map/ppermute | solution.py:45
  230.2 2.3 collective-permute-start.41
  (23 other events, 550.3 us)

commit v4 on v3

--- a/solution.py
+++ b/solution.py
@@ -29,6 +29,10 @@
 def ring_col(place, count):
     place = place % count
     return jnp.where(place < count // 2, 2 * place, count - 1 - 2 * (place - count // 2))
+
+
+def split_steps(cols, half):
+    return (cols - 2) // half
 
 
 def tie(array, *after):
@@ -90,8 +94,16 @@
 
 def main_kernel(cols, rows, tiles, per, meta, *refs):
     it = iter(refs)
-    cw = [next(it) for _ in range(cols)]
-    ccw = [next(it) for _ in range(cols)]
+    split = split_steps(cols, tiles // 2)
+
+    def message(step):
+        if 1 <= step <= split:
+            return [next(it) for _ in range(tiles // 2)]
+        whole = next(it)
+        return [whole.at[k] for k in range(tiles // 2)]
+
+    cw = [message(s) for s in range(cols)]
+    ccw = [message(s) for s in range(cols)]
     ours = [[next(it) for _ in range(rows)] for _ in range(per)]
     left = [[next(it) for _ in range(rows)] for _ in range(2)]
     update, gram = next(it), next(it)
@@ -124,7 +136,7 @@
         spots = [pl.multiple_of(meta[start + s] * width, width) for s in range(cols)]
         return [
             pltpu.make_async_copy(
-                msgs[s].at[tile % half], right.at[tile, :, pl.ds(spots[s], width)], rsem.at[tile, s]
+                msgs[s][tile % half], right.at[tile, :, pl.ds(spots[s], width)], rsem.at[tile, s]
             )
             for s in range(cols)
         ]
@@ -255,61 +267,69 @@
     mine = lax.dynamic_slice_in_dim(inverse, (my_row % 2) * part, part, 0)
     left = pan_left
     inv_cw, inv_ccw = [mine[: part // 2]], [mine[part // 2 :]]
+    last = cols - 1
+    marks = [max(1, round(last * m / 7)) for m in range(8)]
+    split = split_steps(cols, half)
+    cw, ccw = [turned[:half]], [turned[half:]]
+    now = [[turned[part * half + k] for k in range(half)] for part in range(2)]
     for step in range(1, cols):
-        inv_cw.append(lax.ppermute(inv_cw[-1], "col", ahead))
-        inv_ccw.append(lax.ppermute(inv_ccw[-1], "col", back))
-        held = (inv_cw[-1], inv_ccw[-1])
-        if step == max(1, round((cols - 1) * 2 / 7)):
+        held = [lax.ppermute(inv_cw[-1], "col", ahead), lax.ppermute(inv_ccw[-1], "col", back)]
+        tile = (step - 1) % half
+        going = step <= split * half
+        if going:
+            held += [lax.ppermute(now[0][tile], "col", ahead), lax.ppermute(now[1][tile], "col", back)]
+        if step == marks[2]:
             held, cut, left = lax.optimization_barrier((held, cut, left))
             left = to_column(left.reshape(tiles, rows, piece, rank))
-        elif step == max(1, round((cols - 1) * 4 / 7)):
+        elif step == marks[4]:
             held, cut, left = lax.optimization_barrier((held, cut, left))
             cut = lax.all_to_all(cut, "col", 0, 0, tiled=True)
-        elif step == cols - 1:
-            held, turned = lax.optimization_barrier((held, turned))
+        elif step == last:
+            held, cut, left = lax.optimization_barrier((held, cut, left))
         else:
             held = lax.optimization_barrier(held)
-        inv_cw[-1], inv_ccw[-1] = held
+        inv_cw.append(held[0])
+        inv_ccw.append(held[1])
+        if going:
+            now[0][tile], now[1][tile] = held[2:]
+            if tile == half - 1:
+                cw.append(tuple(now[0]))
+                ccw.append(tuple(now[1]))
     inv = [jnp.stack(inv_cw), jnp.stack(inv_ccw)]
     inv = inv + swap_cores(inv, rows)
-    cw, ccw = [turned[:half]], [turned[half:]]
-    last = cols - 1
-    marks = [max(1, round(last * m / 7)) for m in range(8)]
-    for step in range(1, cols):
-        cw.append(lax.ppermute(cw[-1], "col", ahead))
-        ccw.append(lax.ppermute(ccw[-1], "col", back))
-        if step == last:
-            break
+    solved = solve(cut, inv)
+    first = [gather_y(part, rows) for part in solved[: per // 2]]
+    left = lax.all_to_all(left, "col", 0, 0, tiled=True)
+    held = (jnp.stack(now[0]), jnp.stack(now[1]))
+    marks = [max(1, round((last - split) * m / 4)) for m in range(5)]
+    for step in range(1, last - split + 1):
+        cw.append(lax.ppermute(held[0], "col", ahead))
+        ccw.append(lax.ppermute(held[1], "col", back))
         held = (cw[-1], ccw[-1])
         if step == marks[1]:
-            held, inv, left, cut = lax.optimization_barrier((held, inv, left, cut))
-            solved = solve(cut, inv)
-            left = lax.all_to_all(left, "col", 0, 0, tiled=True)
-        elif step == marks[2]:
-            held, solved = lax.optimization_barrier((held, solved))
-            first = [gather_y(part, rows) for part in solved[: per // 2]]
-        elif step == marks[3]:
             held, left, first = lax.optimization_barrier((held, left, first))
             second = [gather_y(part, rows) for part in solved[per // 2 :]]
-        elif step == marks[4]:
-            held, second = lax.optimization_barrier((held, second))
+            ours = [part + swap_cores(part, rows) for part in first]
+        elif step == marks[2]:
+            held, second, ours = lax.optimization_barrier((held, second, ours))
             left = [left[: cols // 2], left[cols // 2 :]]
             left[0] = gather_y(left[0], rows)
-            ours = [part + swap_cores(part, rows) for part in first]
-        elif step == marks[5]:
+            ours = ours + [part + swap_cores(part, rows) for part in second]
+        elif step == marks[3]:
             held, left[0], ours = lax.optimization_barrier((held, left[0], ours))
             left[1] = gather_y(left[1], rows)
-            ours = ours + [part + swap_cores(part, rows) for part in second]
-        elif step == marks[6]:
-            held, left, ours = lax.optimization_barrier((held, left, ours))
-            left = [part + swap_cores(part, rows) for part in left]
+            left[0] = left[0] + swap_cores(left[0], rows)
+        elif step == last - split:
+            held, left = lax.optimization_barrier((held, left))
+            left[1] = left[1] + swap_cores(left[1], rows)
         else:
             held = lax.optimization_barrier(held)
         cw[-1], ccw[-1] = held
     my_ranks = lax.dynamic_slice_in_dim(rank_list, my_row * tiles, tiles, 0)
     their_ranks = lax.dynamic_slice_in_dim(rank_list, my_col * per, per, 0)
     meta = jnp.concatenate([jnp.stack(ids + cw_from + ccw_from).astype(jnp.int32), my_ranks, their_ranks])
-    operands = cw + ccw + [a for group in ours + left for a in group]
+    operands = [a for part in cw + ccw for a in (part if isinstance(part, tuple) else (part,))]
+    operands += [a for group in ours + left for a in group]
     update, gram = pl.pallas_call(
         functools.partial(main_kernel, cols, rows, tiles, per),
         out_shape=(

time: 264 us -> 244 us (0.924)
  waiting for transfers between devices: 145 us -> 105 us
  starting transfers between devices: 61.8 us -> 76.4 us
  Pallas kernels: 40.6 us -> 43.5 us
    ppermute x4, waiting for transfers between devices: 18.2 us -> 0.01 us  [gather_y(): lax.ppermute(piece, 'row', [(i, (i + 2 * step) % rows) for i in range(row...]
    ppermute x28 -> x34, waiting for transfers between devices: 121 us -> 104 us  [the longest x4 39.1 us: local(): cw.append(lax.ppermute(held[0], 'col', ahead))]
    ppermute x28 -> x34, starting transfers between devices: 34.8 us -> 50.3 us  [the longest x7 15.7 us: local(): lax.ppermute(inv_cw[-1], 'col', ahead)]
    all_to_all x1, starting transfers between devices: 9.34 us -> 4.99 us  [local(): left = lax.all_to_all(left, 'col', 0, 0, tiled=True)]
    all_to_all x2, waiting for transfers between devices: 3.83 us -> 0.01 us  [to_column(): moved = lax.all_to_all(pieces, 'row', 1, 0, tiled=False)]
    pallas_call x1, Pallas kernels: 32.2 us -> 35.1 us  [local(): pl.pallas_call(functools.partial(main_kernel, cols, rows, tiles, per), ou...]
  transfers between devices with their start and end apart: 46 -> 52, of which waited for: 29 -> 21; matrix products, arithmetic and copies ran while one was open for 5% -> 7% of each run, Pallas kernels for 3% -> 3%
where the time goes in v4:
time: 244 us; the launch traced here: 247 us
  waiting for transfers between devices  105 us (43%)
  starting transfers between devices  76.4 us (31%)
  Pallas kernels  43.5 us (18%)
  local copies, waits for them, and re-layouts  18.8 us (8%)
    ppermute x4, waiting for transfers between devices, local(): cw.append(lax.ppermute(held[0], 'col', ahead))  39.1 us
    pallas_call x1, Pallas kernels, local(): pl.pallas_call(functools.partial(main_kernel, cols, rows, tiles, per), ou...  35.1 us
    ppermute x7, waiting for transfers between devices, local(): lax.ppermute(inv_ccw[-1], 'col', back)  29.1 us
    ppermute x7, waiting for transfers between devices, local(): lax.ppermute(inv_cw[-1], 'col', ahead)  23.9 us
    ppermute x7, starting transfers between devices, local(): lax.ppermute(inv_cw[-1], 'col', ahead)  15.7 us
    ppermute x6, starting transfers between devices, local(): lax.ppermute(now[1][tile], 'col', back)  12 us
    ppermute x4, starting transfers between devices, local(): cw.append(lax.ppermute(held[0], 'col', ahead))  11.8 us
    unnamed x63, local copies, waits for them, and re-layouts  11.6 us
  transfers between devices with their start and end apart: 52, of which 21 were waited for; matrix products, arithmetic and copies ran while one was open for 7% of the time, Pallas kernels for 3%

profile of v4, /device:TPU:0, one launch (start us, length us, event | category | flops | bytes accessed | tf_op | source)
XLA Modules:
  0.0 246.8 jit_solution(8698483324960360746)
XLA Ops:
  0.6 1.5 copy.11
  2.1 1.1 copy.12
  3.2 4.4 %all-to-all-start = ((bf16[1,4,4,128,256]{4,3,1,0,2:T(8,128)(2,1)}), bf16[1,4,4,128,256]{4,3,1,0,2:T(8,128)(2,1)}, u32[]{:S(2)}, u32[]{:S(2)}) async-start(bf16[1,4,4,128,256]{4,3,1,0,2:T(8,128)(2,1)} %copy.12), calls=%async_computation | async-start | bytes 2097152 | tf_op jit(solution)/shard_map/all_to_all | solution.py:218
  8.6 2.9 %collective-permute-start.3 = (bf16[512,256]{1,0:T(8,128)(2,1)}, bf16[512,256]{1,0:T(8,128)(2,1)}, u32[]{:S(2)}, u32[]{:S(2)}) collective-permute-start(bf16[512,256]{1,0:T(8,128)(2,1)} %get-tuple-element.146), channel_id=1, source_target_pairs={{2,0},{4,2},{6,4},{7,6},{5,7},{3,5},{1,3},{0,1},{10,8},{12,10},{14... | collective-permute-start | bytes 786440 | tf_op jit(solution)/shard_map/ppermute | solution.py:280
  12.5 1.9 collective-permute-start.1
  14.6 1.9 collective-permute-start.7
  16.5 2.6 %collective-permute-done.3.refs_12_ = bf16[512,256]{1,0:T(8,128)(2,1)} collective-permute-done((bf16[512,256]{1,0:T(8,128)(2,1)}, bf16[512,256]{1,0:T(8,128)(2,1)}, u32[]{:S(2)}, u32[]{:S(2)}) %collective-permute-start.3) | collective-permute-done | bytes 262176 | tf_op jit(solution)/shard_map/ppermute | solution.py:280
  19.1 2.0 collective-permute-start.6
  21.0 3.6 %collective-permute-done.1 = bf16[64,2048]{1,0:T(8,128)(2,1)S(1)} collective-permute-done((bf16[64,2048]{1,0:T(8,128)(2,1)S(1)}, bf16[64,2048]{1,0:T(8,128)(2,1)S(1)}, u32[]{:S(2)}, u32[]{:S(2)}) %collective-permute-start.1) | collective-permute-done | bytes 262176 | tf_op jit(solution)/shard_map/ppermute | solution.py:276
  24.6 1.9 collective-permute-done
  26.5 2.1 collective-permute-start.4
  30.3 1.9 collective-permute-start.11
  32.2 10.4 %collective-permute-done.4 = bf16[64,2048]{1,0:T(8,128)(2,1)S(1)} collective-permute-done((bf16[64,2048]{1,0:T(8,128)(2,1)S(1)}, bf16[64,2048]{1,0:T(8,128)(2,1)S(1)}, u32[]{:S(2)}, u32[]{:S(2)}) %collective-permute-start.4) | collective-permute-done | bytes 262176 | tf_op jit(solution)/shard_map/ppermute | solution.py:276
  43.7 1.7 collective-permute-start.14
  46.8 4.3 %all-to-all-start.1 = ((bf16[1,4,4,64,512]{4,3,1,0,2:T(8,128)(2,1)}), bf16[1,4,4,64,512]{4,3,1,0,2:T(8,128)(2,1)}, u32[]{:S(2)}, u32[]{:S(2)}) async-start(bf16[1,4,4,64,512]{4,3,1,0,2:T(8,128)(2,1)} %copy.13), calls=%async_computation.1 | async-start | bytes 2097152 | tf_op jit(solution)/shard_map/all_to_all | solution.py:218
  51.8 1.7 collective-permute-start.15
  54.2 1.5 collective-permute-start.12
  57.6 1.6 collective-permute-start.19
  59.2 1.9 collective-permute-done.15.refs_15_
  61.1 6.6 %collective-permute-done.12 = bf16[64,2048]{1,0:T(8,128)(2,1)S(1)} collective-permute-done((bf16[64,2048]{1,0:T(8,128)(2,1)S(1)}, bf16[64,2048]{1,0:T(8,128)(2,1)S(1)}, u32[]{:S(2)}, u32[]{:S(2)}) %collective-permute-start.12) | collective-permute-done | bytes 262176 | tf_op jit(solution)/shard_map/ppermute | solution.py:276
  69.2 5.6 %all-to-all-start.2 = ((bf16[8,2,128,256]{3,2,1,0:T(8,128)(2,1)}), bf16[8,2,128,256]{3,2,1,0:T(8,128)(2,1)S(1)}, u32[]{:S(2)}, u32[]{:S(2)}) async-start(bf16[8,2,128,256]{3,2,1,0:T(8,128)(2,1)} %bitcast.21), calls=%async_computation.2 | async-start | bytes 2097152 | tf_op jit(solution)/shard_map/all_to_all | solution.py:286
  74.8 2.0 collective-permute-start.22
  77.6 2.0 collective-permute-start.23
  79.6 20.6 %collective-permute-done.17 = bf16[64,2048]{1,0:T(8,128)(2,1)S(1)} collective-permute-done((bf16[64,2048]{1,0:T(8,128)(2,1)S(1)}, bf16[64,2048]{1,0:T(8,128)(2,1)S(1)}, u32[]{:S(2)}, u32[]{:S(2)}) %collective-permute-start.17) | collective-permute-done | bytes 262176 | tf_op jit(solution)/shard_map/ppermute | solution.py:276
  100.2 8.0 %collective-permute-start.20 = (bf16[64,2048]{1,0:T(8,128)(2,1)S(1)}, bf16[64,2048]{1,0:T(8,128)(2,1)S(1)}, u32[]{:S(2)}, u32[]{:S(2)}) collective-permute-start(bf16[64,2048]{1,0:T(8,128)(2,1)S(1)} %collective-permute-done.16), channel_id=1, source_target_pairs={{0,2},{2,4},{4,6},{6,7},{7,5},{5,3},{3,1},{1,0},{8,10},{10,12},{12... | collective-permute-start | bytes 786440 | tf_op jit(solution)/shard_map/ppermute | solution.py:276
  109.6 2.4 collective-permute-done.20
  112.1 2.5 %collective-permute-done.21 = bf16[64,2048]{1,0:T(8,128)(2,1)S(1)} collective-permute-done((bf16[64,2048]{1,0:T(8,128)(2,1)S(1)}, bf16[64,2048]{1,0:T(8,128)(2,1)S(1)}, u32[]{:S(2)}, u32[]{:S(2)}) %collective-permute-start.21) | collective-permute-done | bytes 262176 | tf_op jit(solution)/shard_map/ppermute | solution.py:276
  114.6 3.0 %collective-permute-start.26 = (bf16[64,2048]{1,0:T(8,128)(2,1)S(1)}, bf16[64,2048]{1,0:T(8,128)(2,1)S(1)}, u32[]{:S(2)}, u32[]{:S(2)}) collective-permute-start(bf16[64,2048]{1,0:T(8,128)(2,1)S(1)} %collective-permute-done.20), channel_id=1, source_target_pairs={{0,2},{2,4},{4,6},{6,7},{7,5},{5,3},{3,1},{1,0},{8,10},{10,12},{12... | collective-permute-start | bytes 786440 | tf_op jit(solution)/shard_map/ppermute | solution.py:276
  119.0 2.5 %collective-permute-done.26 = bf16[64,2048]{1,0:T(8,128)(2,1)S(1)} collective-permute-done((bf16[64,2048]{1,0:T(8,128)(2,1)S(1)}, bf16[64,2048]{1,0:T(8,128)(2,1)S(1)}, u32[]{:S(2)}, u32[]{:S(2)}) %collective-permute-start.26) | collective-permute-done | bytes 262176 | tf_op jit(solution)/shard_map/ppermute | solution.py:276
  121.5 2.4 collective-permute-done.27
  125.9 5.0 %all-to-all-start.3 = ((bf16[8,2,64,512]{3,2,1,0:T(8,128)(2,1)}), bf16[8,2,64,512]{3,2,1,0:T(8,128)(2,1)S(1)}, u32[]{:S(2)}, u32[]{:S(2)}) async-start(bf16[8,2,64,512]{3,2,1,0:T(8,128)(2,1)} %bitcast.25), calls=%async_computation.3 | async-start | bytes 2097152 | tf_op jit(solution)/shard_map/all_to_all | solution.py:302
  132.6 2.1 collective-permute-start.24
  134.7 1.1 pad_maximum_fusion.1
  135.8 8.4 %solve.1 = (bf16[128,2048]{1,0:T(8,128)(2,1)}, bf16[128,2048]{1,0:T(8,128)(2,1)}) custom-call(s32[17]{0:T(128)} %stack.160.meta, bf16[8,2,128,256]{3,2,1,0:T(8,128)(2,1)} %copy-done, bf16[8,64,2048]{2,1,0:T(8,128)(2,1)} %bitcast_dynamic-update-slice_fusion.8.refs_0_, bf16[8,64,2048]{2,1,0:T(8,128)(2,1)} %bitcast_dynamic-update-slice_fusion.refs_1_, ...), custom_call_target="tpu_custom_call" | custom-call | flops 2147483648 | bytes 10485760 | tf_op jit(solution)/shard_map/solve/pallas_call | solution.py:243
  144.3 1.3 collective-permute-start.30
  146.4 13.4 %collective-permute-done.24.refs_7_ = bf16[2,512,256]{2,1,0:T(8,128)(2,1)} collective-permute-done((bf16[2,512,256]{2,1,0:T(8,128)(2,1)S(1)}, bf16[2,512,256]{2,1,0:T(8,128)(2,1)}, u32[]{:S(2)}, u32[]{:S(2)}) %collective-permute-start.24) | collective-permute-done | bytes 524320 | tf_op jit(solution)/shard_map/ppermute | solution.py:306
  159.8 1.9 collective-permute-done.25.refs_18_
  161.7 7.2 %collective-permute-start.31 = (bf16[2,512,256]{2,1,0:T(8,128)(2,1)}, bf16[2,512,256]{2,1,0:T(8,128)(2,1)S(1)}, u32[]{:S(2)}, u32[]{:S(2)}) collective-permute-start(bf16[2,512,256]{2,1,0:T(8,128)(2,1)} %collective-permute-done.24.refs_7_), channel_id=1, source_target_pairs={{0,2},{2,4},{4,6},{6,7},{7,5},{5,3},{3,1},{1,0},{8,10},{10,12},{12... | collective-permute-start | bytes 1572872 | tf_op jit(solution)/shard_map/ppermute | solution.py:306
  169.5 1.3 collective-permute-start.38
  170.8 8.6 %collective-permute-done.31.refs_8_ = bf16[2,512,256]{2,1,0:T(8,128)(2,1)S(1)} collective-permute-done((bf16[2,512,256]{2,1,0:T(8,128)(2,1)}, bf16[2,512,256]{2,1,0:T(8,128)(2,1)S(1)}, u32[]{:S(2)}, u32[]{:S(2)}) %collective-permute-start.31) | collective-permute-done | bytes 524320 | tf_op jit(solution)/shard_map/ppermute | solution.py:306
  179.4 2.1 collective-permute-done.32.refs_19_
  181.5 1.8 collective-permute-start.36
  184.1 1.3 collective-permute-start.45
  185.4 8.1 %collective-permute-done.36.refs_9_ = bf16[2,512,256]{2,1,0:T(8,128)(2,1)S(1)} collective-permute-done((bf16[2,512,256]{2,1,0:T(8,128)(2,1)S(1)}, bf16[2,512,256]{2,1,0:T(8,128)(2,1)S(1)}, u32[]{:S(2)}, u32[]{:S(2)}) %collective-permute-start.36) | collective-permute-done | bytes 524320 | tf_op jit(solution)/shard_map/ppermute | solution.py:306
  193.5 2.2 collective-permute-done.37.refs_20_
  196.5 1.4 collective-permute-start.42
  198.3 9.0 %collective-permute-done.41.refs_10_ = bf16[2,512,256]{2,1,0:T(8,128)(2,1)S(1)} collective-permute-done((bf16[2,512,256]{2,1,0:T(8,128)(2,1)S(1)}, bf16[2,512,256]{2,1,0:T(8,128)(2,1)S(1)}, u32[]{:S(2)}, u32[]{:S(2)}) %collective-permute-start.41) | collective-permute-done | bytes 524320 | tf_op jit(solution)/shard_map/ppermute | solution.py:306
  211.5 35.1 %main.1 = (bf16[4,2,2048,512]{3,2,1,0:T(8,128)(2,1)}, bf16[4,2,512,512]{3,2,1,0:T(8,128)(2,1)}) custom-call(s32[26]{0:T(128)} %concatenate.3.meta, bf16[2,512,256]{2,1,0:T(8,128)(2,1)} %get-tuple-element.141.refs_0_, bf16[512,256]{1,0:T(8,128)(2,1)} %collective-permute-done.2.refs_1_, bf16[512,256]{1,0:T(8,128)(2,1)} %collective-permute-done.6.refs_2_, ...), custom_call_target="tpu_custom_call" | custom-call | flops 25769803776 | bytes 33554432 | tf_op jit(solution)/shard_map/main/pallas_call | solution.py:333
  (134 shorter events, 26.1 us)
Async XLA Ops:
  3.2 39.4 %all-to-all-start = ((bf16[1,4,4,128,256]{4,3,1,0,2:T(8,128)(2,1)}), bf16[1,4,4,128,256]{4,3,1,0,2:T(8,128)(2,1)}, u32[]{:S(2)}, u32[]{:S(2)}) async-start(bf16[1,4,4,128,256]{4,3,1,0,2:T(8,128)(2,1)} %copy.12), calls=%async_computation | async-start | bytes 2097152 | tf_op jit(solution)/shard_map/all_to_all | solution.py:218
  8.6 10.5 %collective-permute-start.3 = (bf16[512,256]{1,0:T(8,128)(2,1)}, bf16[512,256]{1,0:T(8,128)(2,1)}, u32[]{:S(2)}, u32[]{:S(2)}) collective-permute-start(bf16[512,256]{1,0:T(8,128)(2,1)} %get-tuple-element.146), channel_id=1, source_target_pairs={{2,0},{4,2},{6,4},{7,6},{5,7},{3,5},{1,3},{0,1},{10,8},{12,10},{14... | collective-permute-start | bytes 786440 | tf_op jit(solution)/shard_map/ppermute | solution.py:280
  11.5 9.5 %collective-permute-start.2 = (bf16[512,256]{1,0:T(8,128)(2,1)}, bf16[512,256]{1,0:T(8,128)(2,1)}, u32[]{:S(2)}, u32[]{:S(2)}) collective-permute-start(bf16[512,256]{1,0:T(8,128)(2,1)} %get-tuple-element.147), channel_id=1, source_target_pairs={{0,2},{2,4},{4,6},{6,7},{7,5},{5,3},{3,1},{1,0},{8,10},{10,12},{12... | collective-permute-start | bytes 786440 | tf_op jit(solution)/shard_map/ppermute | solution.py:280
  12.5 12.1 %collective-permute-start.1 = (bf16[64,2048]{1,0:T(8,128)(2,1)S(1)}, bf16[64,2048]{1,0:T(8,128)(2,1)S(1)}, u32[]{:S(2)}, u32[]{:S(2)}) collective-permute-start(bf16[64,2048]{1,0:T(8,128)(2,1)S(1)} %get-tuple-element.137), channel_id=1, source_target_pairs={{2,0},{4,2},{6,4},{7,6},{5,7},{3,5},{1,3},{0,1},{10,8},{12,10},{14... | collective-permute-start | bytes 786440 | tf_op jit(solution)/shard_map/ppermute | solution.py:276
  14.5 12.0 %collective-permute-start = (bf16[64,2048]{1,0:T(8,128)(2,1)S(1)}, bf16[64,2048]{1,0:T(8,128)(2,1)S(1)}, u32[]{:S(2)}, u32[]{:S(2)}) collective-permute-start(bf16[64,2048]{1,0:T(8,128)(2,1)S(1)} %get-tuple-element.149), channel_id=1, source_target_pairs={{0,2},{2,4},{4,6},{6,7},{7,5},{5,3},{3,1},{1,0},{8,10},{10,12},{12... | collective-permute-start | bytes 786440 | tf_op jit(solution)/shard_map/ppermute | solution.py:276
  14.6 15.8 %collective-permute-start.7 = (bf16[512,256]{1,0:T(8,128)(2,1)}, bf16[512,256]{1,0:T(8,128)(2,1)}, u32[]{:S(2)}, u32[]{:S(2)}) collective-permute-start(bf16[512,256]{1,0:T(8,128)(2,1)} %get-tuple-element.144), channel_id=1, source_target_pairs={{2,0},{4,2},{6,4},{7,6},{5,7},{3,5},{1,3},{0,1},{10,8},{12,10},{14... | collective-permute-start | bytes 786440 | tf_op jit(solution)/shard_map/ppermute | solution.py:280
  19.1 13.1 %collective-permute-start.6 = (bf16[512,256]{1,0:T(8,128)(2,1)}, bf16[512,256]{1,0:T(8,128)(2,1)}, u32[]{:S(2)}, u32[]{:S(2)}) collective-permute-start(bf16[512,256]{1,0:T(8,128)(2,1)} %get-tuple-element.145), channel_id=1, source_target_pairs={{0,2},{2,4},{4,6},{6,7},{7,5},{5,3},{3,1},{1,0},{8,10},{10,12},{12... | collective-permute-start | bytes 786440 | tf_op jit(solution)/shard_map/ppermute | solution.py:280
  26.5 25.3 %collective-permute-start.10 = (bf16[512,256]{1,0:T(8,128)(2,1)}, bf16[512,256]{1,0:T(8,128)(2,1)}, u32[]{:S(2)}, u32[]{:S(2)}) collective-permute-start(bf16[512,256]{1,0:T(8,128)(2,1)} %collective-permute-done.2.refs_1_), channel_id=1, source_target_pairs={{0,2},{2,4},{4,6},{6,7},{7,5},{5,3},{3,1},{1,0},{8,10},{10,12},{12... | collective-permute-start | bytes 786440 | tf_op jit(solution)/shard_map/ppermute | solution.py:280
  26.5 16.0 %collective-permute-start.4 = (bf16[64,2048]{1,0:T(8,128)(2,1)S(1)}, bf16[64,2048]{1,0:T(8,128)(2,1)S(1)}, u32[]{:S(2)}, u32[]{:S(2)}) collective-permute-start(bf16[64,2048]{1,0:T(8,128)(2,1)S(1)} %collective-permute-done), channel_id=1, source_target_pairs={{0,2},{2,4},{4,6},{6,7},{7,5},{5,3},{3,1},{1,0},{8,10},{10,12},{12... | collective-permute-start | bytes 786440 | tf_op jit(solution)/shard_map/ppermute | solution.py:276
  28.6 14.0 %collective-permute-start.5 = (bf16[64,2048]{1,0:T(8,128)(2,1)S(1)}, bf16[64,2048]{1,0:T(8,128)(2,1)S(1)}, u32[]{:S(2)}, u32[]{:S(2)}) collective-permute-start(bf16[64,2048]{1,0:T(8,128)(2,1)S(1)} %collective-permute-done.1), channel_id=1, source_target_pairs={{2,0},{4,2},{6,4},{7,6},{5,7},{3,5},{1,3},{0,1},{10,8},{12,10},{14... | collective-permute-start | bytes 786440 | tf_op jit(solution)/shard_map/ppermute | solution.py:276
  30.3 23.1 %collective-permute-start.11 = (bf16[512,256]{1,0:T(8,128)(2,1)}, bf16[512,256]{1,0:T(8,128)(2,1)S(1)}, u32[]{:S(2)}, u32[]{:S(2)}) collective-permute-start(bf16[512,256]{1,0:T(8,128)(2,1)} %collective-permute-done.3.refs_12_), channel_id=1, source_target_pairs={{2,0},{4,2},{6,4},{7,6},{5,7},{3,5},{1,3},{0,1},{10,8},{12,10},{14... | collective-permute-start | bytes 786440 | tf_op jit(solution)/shard_map/ppermute | solution.py:280
  42.6 10.9 %collective-permute-start.8 = (bf16[64,2048]{1,0:T(8,128)(2,1)S(1)}, bf16[64,2048]{1,0:T(8,128)(2,1)S(1)}, u32[]{:S(2)}, u32[]{:S(2)}) collective-permute-start(bf16[64,2048]{1,0:T(8,128)(2,1)S(1)} %collective-permute-done.4), channel_id=1, source_target_pairs={{0,2},{2,4},{4,6},{6,7},{7,5},{5,3},{3,1},{1,0},{8,10},{10,12},{12... | collective-permute-start | bytes 786440 | tf_op jit(solution)/shard_map/ppermute | solution.py:276
  43.7 14.0 %collective-permute-start.14 = (bf16[512,256]{1,0:T(8,128)(2,1)}, bf16[512,256]{1,0:T(8,128)(2,1)}, u32[]{:S(2)}, u32[]{:S(2)}) collective-permute-start(bf16[512,256]{1,0:T(8,128)(2,1)} %collective-permute-done.6.refs_2_), channel_id=1, source_target_pairs={{0,2},{2,4},{4,6},{6,7},{7,5},{5,3},{3,1},{1,0},{8,10},{10,12},{12... | collective-permute-start | bytes 786440 | tf_op jit(solution)/shard_map/ppermute | solution.py:280
  45.4 8.0 %collective-permute-start.9 = (bf16[64,2048]{1,0:T(8,128)(2,1)S(1)}, bf16[64,2048]{1,0:T(8,128)(2,1)S(1)}, u32[]{:S(2)}, u32[]{:S(2)}) collective-permute-start(bf16[64,2048]{1,0:T(8,128)(2,1)S(1)} %collective-permute-done.5), channel_id=1, source_target_pairs={{2,0},{4,2},{6,4},{7,6},{5,7},{3,5},{1,3},{0,1},{10,8},{12,10},{14... | collective-permute-start | bytes 786440 | tf_op jit(solution)/shard_map/ppermute | solution.py:276
  46.8 20.9 %all-to-all-start.1 = ((bf16[1,4,4,64,512]{4,3,1,0,2:T(8,128)(2,1)}), bf16[1,4,4,64,512]{4,3,1,0,2:T(8,128)(2,1)}, u32[]{:S(2)}, u32[]{:S(2)}) async-start(bf16[1,4,4,64,512]{4,3,1,0,2:T(8,128)(2,1)} %copy.13), calls=%async_computation.1 | async-start | bytes 2097152 | tf_op jit(solution)/shard_map/all_to_all | solution.py:218
  51.8 9.3 %collective-permute-start.15 = (bf16[512,256]{1,0:T(8,128)(2,1)}, bf16[512,256]{1,0:T(8,128)(2,1)S(1)}, u32[]{:S(2)}, u32[]{:S(2)}) collective-permute-start(bf16[512,256]{1,0:T(8,128)(2,1)} %collective-permute-done.7.refs_13_), channel_id=1, source_target_pairs={{2,0},{4,2},{6,4},{7,6},{5,7},{3,5},{1,3},{0,1},{10,8},{12,10},{14... | collective-permute-start | bytes 786440 | tf_op jit(solution)/shard_map/ppermute | solution.py:280
  53.5 24.1 %collective-permute-start.18 = (bf16[512,256]{1,0:T(8,128)(2,1)}, bf16[512,256]{1,0:T(8,128)(2,1)S(1)}, u32[]{:S(2)}, u32[]{:S(2)}) collective-permute-start(bf16[512,256]{1,0:T(8,128)(2,1)} %collective-permute-done.10.refs_3_), channel_id=1, source_target_pairs={{0,2},{2,4},{4,6},{6,7},{7,5},{5,3},{3,1},{1,0},{8,10},{10,12},{12... | collective-permute-start | bytes 786440 | tf_op jit(solution)/shard_map/ppermute | solution.py:280
  54.2 13.6 %collective-permute-start.12 = (bf16[64,2048]{1,0:T(8,128)(2,1)S(1)}, bf16[64,2048]{1,0:T(8,128)(2,1)S(1)}, u32[]{:S(2)}, u32[]{:S(2)}) collective-permute-start(bf16[64,2048]{1,0:T(8,128)(2,1)S(1)} %collective-permute-done.8), channel_id=1, source_target_pairs={{0,2},{2,4},{4,6},{6,7},{7,5},{5,3},{3,1},{1,0},{8,10},{10,12},{12... | collective-permute-start | bytes 786440 | tf_op jit(solution)/shard_map/ppermute | solution.py:276
  55.6 12.1 %collective-permute-start.13 = (bf16[64,2048]{1,0:T(8,128)(2,1)S(1)}, bf16[64,2048]{1,0:T(8,128)(2,1)S(1)}, u32[]{:S(2)}, u32[]{:S(2)}) collective-permute-start(bf16[64,2048]{1,0:T(8,128)(2,1)S(1)} %collective-permute-done.9), channel_id=1, source_target_pairs={{2,0},{4,2},{6,4},{7,6},{5,7},{3,5},{1,3},{0,1},{10,8},{12,10},{14... | collective-permute-start | bytes 786440 | tf_op jit(solution)/shard_map/ppermute | solution.py:276
  57.6 21.9 %collective-permute-start.19 = (bf16[512,256]{1,0:T(8,128)(2,1)}, bf16[512,256]{1,0:T(8,128)(2,1)}, u32[]{:S(2)}, u32[]{:S(2)}) collective-permute-start(bf16[512,256]{1,0:T(8,128)(2,1)} %copy-done.22), channel_id=1, source_target_pairs={{2,0},{4,2},{6,4},{7,6},{5,7},{3,5},{1,3},{0,1},{10,8},{12,10},{14... | collective-permute-start | bytes 786440 | tf_op jit(solution)/shard_map/ppermute | solution.py:280
  67.7 11.8 %collective-permute-start.16 = (bf16[64,2048]{1,0:T(8,128)(2,1)S(1)}, bf16[64,2048]{1,0:T(8,128)(2,1)S(1)}, u32[]{:S(2)}, u32[]{:S(2)}) collective-permute-start(bf16[64,2048]{1,0:T(8,128)(2,1)S(1)} %collective-permute-done.12), channel_id=1, source_target_pairs={{0,2},{2,4},{4,6},{6,7},{7,5},{5,3},{3,1},{1,0},{8,10},{10,12},{12... | collective-permute-start | bytes 786440 | tf_op jit(solution)/shard_map/ppermute | solution.py:276
  69.2 54.7 %all-to-all-start.2 = ((bf16[8,2,128,256]{3,2,1,0:T(8,128)(2,1)}), bf16[8,2,128,256]{3,2,1,0:T(8,128)(2,1)S(1)}, u32[]{:S(2)}, u32[]{:S(2)}) async-start(bf16[8,2,128,256]{3,2,1,0:T(8,128)(2,1)} %bitcast.21), calls=%async_computation.2 | async-start | bytes 2097152 | tf_op jit(solution)/shard_map/all_to_all | solution.py:286
  74.8 34.8 %collective-permute-start.22 = (bf16[512,256]{1,0:T(8,128)(2,1)}, bf16[512,256]{1,0:T(8,128)(2,1)S(1)}, u32[]{:S(2)}, u32[]{:S(2)}) collective-permute-start(bf16[512,256]{1,0:T(8,128)(2,1)} %collective-permute-done.14.refs_4_), channel_id=1, source_target_pairs={{0,2},{2,4},{4,6},{6,7},{7,5},{5,3},{3,1},{1,0},{8,10},{10,12},{12... | collective-permute-start | bytes 786440 | tf_op jit(solution)/shard_map/ppermute | solution.py:280
  76.8 23.4 %collective-permute-start.17 = (bf16[64,2048]{1,0:T(8,128)(2,1)S(1)}, bf16[64,2048]{1,0:T(8,128)(2,1)S(1)}, u32[]{:S(2)}, u32[]{:S(2)}) collective-permute-start(bf16[64,2048]{1,0:T(8,128)(2,1)S(1)} %collective-permute-done.13), channel_id=1, source_target_pairs={{2,0},{4,2},{6,4},{7,6},{5,7},{3,5},{1,3},{0,1},{10,8},{12,10},{14... | collective-permute-start | bytes 786440 | tf_op jit(solution)/shard_map/ppermute | solution.py:276
  77.6 32.1 %collective-permute-start.23 = (bf16[512,256]{1,0:T(8,128)(2,1)}, bf16[512,256]{1,0:T(8,128)(2,1)S(1)}, u32[]{:S(2)}, u32[]{:S(2)}) collective-permute-start(bf16[512,256]{1,0:T(8,128)(2,1)} %copy-done.23), channel_id=1, source_target_pairs={{2,0},{4,2},{6,4},{7,6},{5,7},{3,5},{1,3},{0,1},{10,8},{12,10},{14... | collective-permute-start | bytes 786440 | tf_op jit(solution)/shard_map/ppermute | solution.py:280
  100.2 11.9 %collective-permute-start.20 = (bf16[64,2048]{1,0:T(8,128)(2,1)S(1)}, bf16[64,2048]{1,0:T(8,128)(2,1)S(1)}, u32[]{:S(2)}, u32[]{:S(2)}) collective-permute-start(bf16[64,2048]{1,0:T(8,128)(2,1)S(1)} %collective-permute-done.16), channel_id=1, source_target_pairs={{0,2},{2,4},{4,6},{6,7},{7,5},{5,3},{3,1},{1,0},{8,10},{10,12},{12... | collective-permute-start | bytes 786440 | tf_op jit(solution)/shard_map/ppermute | solution.py:276
  114.6 6.9 %collective-permute-start.26 = (bf16[64,2048]{1,0:T(8,128)(2,1)S(1)}, bf16[64,2048]{1,0:T(8,128)(2,1)S(1)}, u32[]{:S(2)}, u32[]{:S(2)}) collective-permute-start(bf16[64,2048]{1,0:T(8,128)(2,1)S(1)} %collective-permute-done.20), channel_id=1, source_target_pairs={{0,2},{2,4},{4,6},{6,7},{7,5},{5,3},{3,1},{1,0},{8,10},{10,12},{12... | collective-permute-start | bytes 786440 | tf_op jit(solution)/shard_map/ppermute | solution.py:276
  124.7 11.1 %collective-permute-start.28 = (bf16[8,64,2048]{2,1,0:T(8,128)(2,1)}, bf16[8,64,2048]{2,1,0:T(8,128)(2,1)}, u32[]{:S(2)}, u32[]{:S(2)}) collective-permute-start(bf16[8,64,2048]{2,1,0:T(8,128)(2,1)} %bitcast_dynamic-update-slice_fusion.8.refs_0_), channel_id=1, source_target_pairs={{0,8},{8,0},{16,24},{24,16},{1,9},{9,1},{17,25},{25,17},{2,10},{10... | collective-permute-start | bytes 6291464 | tf_op jit(solution)/shard_map/ppermute | solution.py:49
  125.4 10.4 %collective-permute-start.29 = (bf16[8,64,2048]{2,1,0:T(8,128)(2,1)}, bf16[8,64,2048]{2,1,0:T(8,128)(2,1)}, u32[]{:S(2)}, u32[]{:S(2)}) collective-permute-start(bf16[8,64,2048]{2,1,0:T(8,128)(2,1)} %bitcast_dynamic-update-slice_fusion.refs_1_), channel_id=1, source_target_pairs={{0,8},{8,0},{16,24},{24,16},{1,9},{9,1},{17,25},{25,17},{2,10},{10... | collective-permute-start | bytes 6291464 | tf_op jit(solution)/shard_map/ppermute | solution.py:49
  125.9 35.8 %all-to-all-start.3 = ((bf16[8,2,64,512]{3,2,1,0:T(8,128)(2,1)}), bf16[8,2,64,512]{3,2,1,0:T(8,128)(2,1)S(1)}, u32[]{:S(2)}, u32[]{:S(2)}) async-start(bf16[8,2,64,512]{3,2,1,0:T(8,128)(2,1)} %bitcast.25), calls=%async_computation.3 | async-start | bytes 2097152 | tf_op jit(solution)/shard_map/all_to_all | solution.py:302
  132.6 27.2 %collective-permute-start.24 = (bf16[2,512,256]{2,1,0:T(8,128)(2,1)S(1)}, bf16[2,512,256]{2,1,0:T(8,128)(2,1)}, u32[]{:S(2)}, u32[]{:S(2)}) collective-permute-start(bf16[2,512,256]{2,1,0:T(8,128)(2,1)S(1)} %pad_maximum_fusion), channel_id=1, source_target_pairs={{0,2},{2,4},{4,6},{6,7},{7,5},{5,3},{3,1},{1,0},{8,10},{10,12},{12... | collective-permute-start | bytes 1572872 | tf_op jit(solution)/shard_map/ppermute | solution.py:306
  135.7 25.9 %collective-permute-start.25 = (bf16[2,512,256]{2,1,0:T(8,128)(2,1)S(1)}, bf16[2,512,256]{2,1,0:T(8,128)(2,1)}, u32[]{:S(2)}, u32[]{:S(2)}) collective-permute-start(bf16[2,512,256]{2,1,0:T(8,128)(2,1)S(1)} %pad_maximum_fusion.1), channel_id=1, source_target_pairs={{2,0},{4,2},{6,4},{7,6},{5,7},{3,5},{1,3},{0,1},{10,8},{12,10},{14... | collective-permute-start | bytes 1572872 | tf_op jit(solution)/shard_map/ppermute | solution.py:307
  144.3 17.4 %collective-permute-start.30 = (bf16[128,2048]{1,0:T(8,128)(2,1)}, bf16[128,2048]{1,0:T(8,128)(2,1)}, u32[]{:S(2)}, u32[]{:S(2)}) collective-permute-start(bf16[128,2048]{1,0:T(8,128)(2,1)} %get-tuple-element.122.refs_22_), channel_id=1, source_target_pairs={{0,16},{8,24},{16,0},{24,8},{1,17},{9,25},{17,1},{25,9},{2,18},{10... | collective-permute-start | bytes 1572872 | tf_op jit(solution)/shard_map/ppermute | solution.py:44
  145.6 23.9 %collective-permute-start.33 = (bf16[128,2048]{1,0:T(8,128)(2,1)}, bf16[128,2048]{1,0:T(8,128)(2,1)}, u32[]{:S(2)}, u32[]{:S(2)}) collective-permute-start(bf16[128,2048]{1,0:T(8,128)(2,1)} %get-tuple-element.126.refs_26_), channel_id=1, source_target_pairs={{0,16},{8,24},{16,0},{24,8},{1,17},{9,25},{17,1},{25,9},{2,18},{10... | collective-permute-start | bytes 1572872 | tf_op jit(solution)/shard_map/ppermute | solution.py:44
  161.7 17.7 %collective-permute-start.31 = (bf16[2,512,256]{2,1,0:T(8,128)(2,1)}, bf16[2,512,256]{2,1,0:T(8,128)(2,1)S(1)}, u32[]{:S(2)}, u32[]{:S(2)}) collective-permute-start(bf16[2,512,256]{2,1,0:T(8,128)(2,1)} %collective-permute-done.24.refs_7_), channel_id=1, source_target_pairs={{0,2},{2,4},{4,6},{6,7},{7,5},{5,3},{3,1},{1,0},{8,10},{10,12},{12... | collective-permute-start | bytes 1572872 | tf_op jit(solution)/shard_map/ppermute | solution.py:306
  168.8 12.6 %collective-permute-start.32 = (bf16[2,512,256]{2,1,0:T(8,128)(2,1)}, bf16[2,512,256]{2,1,0:T(8,128)(2,1)S(1)}, u32[]{:S(2)}, u32[]{:S(2)}) collective-permute-start(bf16[2,512,256]{2,1,0:T(8,128)(2,1)} %collective-permute-done.25.refs_18_), channel_id=1, source_target_pairs={{2,0},{4,2},{6,4},{7,6},{5,7},{3,5},{1,3},{0,1},{10,8},{12,10},{14... | collective-permute-start | bytes 1572872 | tf_op jit(solution)/shard_map/ppermute | solution.py:307
  168.9 12.6 %collective-permute-start.34 = (bf16[128,2048]{1,0:T(8,128)(2,1)}, bf16[128,2048]{1,0:T(8,128)(2,1)S(1)}, u32[]{:S(2)}, u32[]{:S(2)}) collective-permute-start(bf16[128,2048]{1,0:T(8,128)(2,1)} %get-tuple-element.122.refs_22_), channel_id=1, source_target_pairs={{0,8},{8,0},{16,24},{24,16},{1,9},{9,1},{17,25},{25,17},{2,10},{10... | collective-permute-start | bytes 1572872 | tf_op jit(solution)/shard_map/ppermute | solution.py:49
  168.9 12.7 %collective-permute-start.35 = (bf16[128,2048]{1,0:T(8,128)(2,1)}, bf16[128,2048]{1,0:T(8,128)(2,1)S(1)}, u32[]{:S(2)}, u32[]{:S(2)}) collective-permute-start(bf16[128,2048]{1,0:T(8,128)(2,1)} %collective-permute-done.30.refs_23_), channel_id=1, source_target_pairs={{0,8},{8,0},{16,24},{24,16},{1,9},{9,1},{17,25},{25,17},{2,10},{10... | collective-permute-start | bytes 1572872 | tf_op jit(solution)/shard_map/ppermute | solution.py:49
  169.5 14.6 %collective-permute-start.38 = (bf16[4,2,64,512]{3,2,1,0:T(8,128)(2,1)S(1)}, bf16[4,2,64,512]{3,2,1,0:T(8,128)(2,1)S(1)}, u32[]{:S(2)}, u32[]{:S(2)}) collective-permute-start(bf16[4,2,64,512]{3,2,1,0:T(8,128)(2,1)S(1)} %get-tuple-element.130.refs_30_), channel_id=1, source_target_pairs={{0,16},{8,24},{16,0},{24,8},{1,17},{9,25},{17,1},{25,9},{2,18},{10... | collective-permute-start | bytes 1572872 | tf_op jit(solution)/shard_map/ppermute | solution.py:44
  181.5 12.0 %collective-permute-start.36 = (bf16[2,512,256]{2,1,0:T(8,128)(2,1)S(1)}, bf16[2,512,256]{2,1,0:T(8,128)(2,1)S(1)}, u32[]{:S(2)}, u32[]{:S(2)}) collective-permute-start(bf16[2,512,256]{2,1,0:T(8,128)(2,1)S(1)} %collective-permute-done.31.refs_8_), channel_id=1, source_target_pairs={{0,2},{2,4},{4,6},{6,7},{7,5},{5,3},{3,1},{1,0},{8,10},{10,12},{12... | collective-permute-start | bytes 1572872 | tf_op jit(solution)/shard_map/ppermute | solution.py:306
  183.3 12.4 %collective-permute-start.37 = (bf16[2,512,256]{2,1,0:T(8,128)(2,1)S(1)}, bf16[2,512,256]{2,1,0:T(8,128)(2,1)S(1)}, u32[]{:S(2)}, u32[]{:S(2)}) collective-permute-start(bf16[2,512,256]{2,1,0:T(8,128)(2,1)S(1)} %collective-permute-done.32.refs_19_), channel_id=1, source_target_pairs={{2,0},{4,2},{6,4},{7,6},{5,7},{3,5},{1,3},{0,1},{10,8},{12,10},{14... | collective-permute-start | bytes 1572872 | tf_op jit(solution)/shard_map/ppermute | solution.py:307
  183.6 12.1 %collective-permute-start.39 = (bf16[128,2048]{1,0:T(8,128)(2,1)S(1)}, bf16[128,2048]{1,0:T(8,128)(2,1)S(1)}, u32[]{:S(2)}, u32[]{:S(2)}) collective-permute-start(bf16[128,2048]{1,0:T(8,128)(2,1)S(1)} %copy-done.8), channel_id=1, source_target_pairs={{0,8},{8,0},{16,24},{24,16},{1,9},{9,1},{17,25},{25,17},{2,10},{10... | collective-permute-start | bytes 1572872 | tf_op jit(solution)/shard_map/ppermute | solution.py:49
  183.6 12.1 %collective-permute-start.40 = (bf16[128,2048]{1,0:T(8,128)(2,1)}, bf16[128,2048]{1,0:T(8,128)(2,1)S(1)}, u32[]{:S(2)}, u32[]{:S(2)}) collective-permute-start(bf16[128,2048]{1,0:T(8,128)(2,1)} %collective-permute-done.33.refs_27_), channel_id=1, source_target_pairs={{0,8},{8,0},{16,24},{24,16},{1,9},{9,1},{17,25},{25,17},{2,10},{10... | collective-permute-start | bytes 1572872 | tf_op jit(solution)/shard_map/ppermute | solution.py:49
  184.1 14.2 %collective-permute-start.45 = (bf16[4,2,64,512]{3,2,1,0:T(8,128)(2,1)S(1)}, bf16[4,2,64,512]{3,2,1,0:T(8,128)(2,1)}, u32[]{:S(2)}, u32[]{:S(2)}) collective-permute-start(bf16[4,2,64,512]{3,2,1,0:T(8,128)(2,1)S(1)} %get-tuple-element.134.refs_34_), channel_id=1, source_target_pairs={{0,16},{8,24},{16,0},{24,8},{1,17},{9,25},{17,1},{25,9},{2,18},{10... | collective-permute-start | bytes 1572872 | tf_op jit(solution)/shard_map/ppermute | solution.py:44
  195.7 11.6 %collective-permute-start.41 = (bf16[2,512,256]{2,1,0:T(8,128)(2,1)S(1)}, bf16[2,512,256]{2,1,0:T(8,128)(2,1)S(1)}, u32[]{:S(2)}, u32[]{:S(2)}) collective-permute-start(bf16[2,512,256]{2,1,0:T(8,128)(2,1)S(1)} %collective-permute-done.36.refs_9_), channel_id=1, source_target_pairs={{0,2},{2,4},{4,6},{6,7},{7,5},{5,3},{3,1},{1,0},{8,10},{10,12},{12... | collective-permute-start | bytes 1572872 | tf_op jit(solution)/shard_map/ppermute | solution.py:306
  196.5 11.6 %collective-permute-start.42 = (bf16[2,512,256]{2,1,0:T(8,128)(2,1)S(1)}, bf16[2,512,256]{2,1,0:T(8,128)(2,1)S(1)}, u32[]{:S(2)}, u32[]{:S(2)}) collective-permute-start(bf16[2,512,256]{2,1,0:T(8,128)(2,1)S(1)} %collective-permute-done.37.refs_20_), channel_id=1, source_target_pairs={{2,0},{4,2},{6,4},{7,6},{5,7},{3,5},{1,3},{0,1},{10,8},{12,10},{14... | collective-permute-start | bytes 1572872 | tf_op jit(solution)/shard_map/ppermute | solution.py:307
  197.8 10.3 %collective-permute-start.43 = (bf16[4,2,64,512]{3,2,1,0:T(8,128)(2,1)S(1)}, bf16[4,2,64,512]{3,2,1,0:T(8,128)(2,1)S(1)}, u32[]{:S(2)}, u32[]{:S(2)}) collective-permute-start(bf16[4,2,64,512]{3,2,1,0:T(8,128)(2,1)S(1)} %get-tuple-element.130.refs_30_), channel_id=1, source_target_pairs={{0,8},{8,0},{16,24},{24,16},{1,9},{9,1},{17,25},{25,17},{2,10},{10... | collective-permute-start | bytes 1572872 | tf_op jit(solution)/shard_map/ppermute | solution.py:49
  197.8 10.3 %collective-permute-start.44 = (bf16[4,2,64,512]{3,2,1,0:T(8,128)(2,1)S(1)}, bf16[4,2,64,512]{3,2,1,0:T(8,128)(2,1)S(1)}, u32[]{:S(2)}, u32[]{:S(2)}) collective-permute-start(bf16[4,2,64,512]{3,2,1,0:T(8,128)(2,1)S(1)} %collective-permute-done.38.refs_31_), channel_id=1, source_target_pairs={{0,8},{8,0},{16,24},{24,16},{1,9},{9,1},{17,25},{25,17},{2,10},{10... | collective-permute-start | bytes 1572872 | tf_op jit(solution)/shard_map/ppermute | solution.py:49
  (29 other events, 525.0 us)
